TPU v7x, 32 devices: a whole 2x2x4 slice. The times are simulated.
32 devices in a mesh: frame: 16 (over z, y, x), pix: 2 (over core).
Axes of the slice: x: 2, y: 2, z: 4, core: 2. Of those that a mesh axis runs over, the one named last changes fastest.
Arguments:
- frames: bfloat16 [1024, 32768], P('frame', 'pix'), as said below
- cycle_map: int32 [32768], P('pix'), may hold values from -1 to 15, as said below
Outputs:
- correlation: bfloat16 [16, 1024, 1024], P('frame', 'pix')
Inputs may be any that keep to these rules, and one draw needn't show every extreme that they name: `frames`: every entry is positive. `cycle_map`: pixels come in aligned blocks of 128; every pixel of a block is either -1 or one common cycle, and the first pixel of a block that holds a cycle belongs to it. Within each sector (aligned blocks of 16384 pixels, one a pix group) every cycle holds at least one and at most 8 blocks, and every cycle holds exactly 1024 pixels in some sector.
All inputs are finite; a program needn't handle non-finite values.
Results may differ from a plain program's by a relative error of at most 0.012.
Values may be sent and summed in bfloat16 or wider, within the bound.
No kernel may reach another device: no remote copies, remote signals or barrier semaphores. Data moves between devices by JAX's collectives and lax.ppermute only.
A program may use at most 64 MiB of HBM per device.

v0:
```python
import functools

import jax
import jax.numpy as jnp
from jax import lax
from jax.experimental import pallas as pl
from jax.experimental.pallas import tpu as pltpu
from jax.sharding import PartitionSpec as P

BLOCK = 128
HALF_WIN = 2
PAD = 8
TILE = 256
CHUNK = 128
ONES = 16
VMEM_BYTES = 32 * 1024 * 1024
LIST, COUNT, PIXELS = 0, 1, 2
SWAP = [(0, 1), (1, 0)]
WHOLE = pl.BlockSpec(memory_space=pltpu.VMEM)
ANYWHERE = pl.BlockSpec(memory_space=pl.ANY)


def call(kernel, name, out_shape, flops=0, bytes_accessed=0, limit=VMEM_BYTES, **kw):
    return pl.pallas_call(
        kernel,
        out_shape=out_shape,
        compiler_params=pltpu.CompilerParams(vmem_limit_bytes=limit),
        cost_estimate=pl.CostEstimate(
            flops=flops, bytes_accessed=bytes_accessed, transcendentals=0
        ),
        name=name,
        **kw,
    )


def keep(cm_ref, block, wanted):
    valid = (cm_ref[pl.ds(block, 1), :] >= 0) & wanted
    return valid.astype(jnp.float32).astype(jnp.bfloat16)


def take(frames_ref, block):
    return frames_ref[:, pl.ds(pl.multiple_of(block * BLOCK, BLOCK), BLOCK)]


def find_blocks(cm, cap_blocks, meta_ref):
    blocks = cm.shape[0]
    width = meta_ref.shape[1]
    first = cm[:, 0:1]
    member = first == lax.broadcasted_iota(jnp.int32, (blocks, BLOCK), 1)
    member_f = member.astype(jnp.float32)
    row = lax.broadcasted_iota(jnp.int32, (blocks, blocks), 0)
    col = lax.broadcasted_iota(jnp.int32, (blocks, blocks), 1)
    earlier = (col < row).astype(jnp.float32).astype(jnp.bfloat16)
    before = jnp.dot(earlier, member_f.astype(jnp.bfloat16), preferred_element_type=jnp.float32)
    rank = jnp.sum(before * member_f, axis=1, keepdims=True).astype(jnp.int32)
    slot = jnp.where(first >= 0, first * cap_blocks + rank, -1)
    hit = slot == lax.broadcasted_iota(jnp.int32, (blocks, width), 1)
    index = lax.broadcasted_iota(jnp.int32, (blocks, width), 0).astype(jnp.float32)
    pixels = jnp.sum((cm >= 0).astype(jnp.float32), axis=1, keepdims=True)
    meta_ref[...] = jnp.zeros_like(meta_ref)
    meta_ref[LIST : LIST + 1, :] = jnp.sum(
        jnp.where(hit, index, 0.0), axis=0, keepdims=True
    ).astype(jnp.int32)
    meta_ref[COUNT : COUNT + 1, 0:BLOCK] = jnp.sum(member_f, axis=0, keepdims=True).astype(
        jnp.int32
    )
    meta_ref[PIXELS : PIXELS + 1, 0:BLOCK] = jnp.sum(
        member_f * pixels, axis=0, keepdims=True
    ).astype(jnp.int32)


def move_kernel(cap_blocks, cm_hbm, frames_hbm, out_ref, meta_ref, *scratch):
    frames_ref, cm_ref, meta_s, sems = scratch
    n, move = out_ref.shape[:2]
    half = cap_blocks - move
    get_cm = pltpu.make_async_copy(cm_hbm, cm_ref, sems.at[0])
    get_cm.start()
    get_frames = pltpu.make_async_copy(frames_hbm, frames_ref, sems.at[1])
    get_frames.start()
    get_cm.wait()
    find_blocks(cm_ref[...], cap_blocks, meta_ref)
    to_scalars = pltpu.make_async_copy(meta_ref, meta_s, sems.at[2])
    to_scalars.start()
    to_scalars.wait()
    get_frames.wait()
    for q in range(n):
        count = meta_s[COUNT, q]
        for i in range(move):
            block = meta_s[LIST, q * cap_blocks + half + i]
            out_ref[q, i] = take(frames_ref, block) * keep(cm_ref, block, half + i < count)


def pack_move(cm, frames, cap_blocks, move):
    n = cm.shape[0] // cap_blocks
    meta = jax.ShapeDtypeStruct((8, cm.shape[0]), jnp.int32)
    return call(
        functools.partial(move_kernel, cap_blocks),
        "pack_move",
        [jax.ShapeDtypeStruct((n, move, frames.shape[0], BLOCK), frames.dtype), meta],
        in_specs=[ANYWHERE] * 2,
        out_specs=[WHOLE] * 2,
        scratch_shapes=[
            pltpu.VMEM(frames.shape, frames.dtype),
            pltpu.VMEM(cm.shape, cm.dtype),
            pltpu.SMEM(meta.shape, meta.dtype),
            pltpu.SemaphoreType.DMA((3,)),
        ],
    )(
        pltpu.with_memory_space_constraint(cm, pltpu.HBM),
        pltpu.with_memory_space_constraint(frames, pltpu.HBM),
    )


def own_kernel(cap_blocks, meta_s, cm_ref, frames_ref, out_hbm, tail_ref, lead_ref, sem):
    n, lead = lead_ref.shape[:2]

    def put(out_ref, first):
        for q in range(n):
            count = meta_s[COUNT, q]
            for i in range(out_ref.shape[1]):
                block = meta_s[LIST, q * cap_blocks + first + i]
                kept = take(frames_ref, block) * keep(cm_ref, block, first + i < count)
                out_ref[q, i] = kept

    put(lead_ref, 0)
    write = pltpu.make_async_copy(lead_ref, out_hbm.at[:, 0:lead], sem)
    write.start()
    put(tail_ref, lead)
    write.wait()


def pack_own(meta, cm, frames, cap_blocks, half, move):
    rows = frames.shape[0]
    n = cm.shape[0] // cap_blocks
    return call(
        functools.partial(own_kernel, cap_blocks),
        "pack_own",
        [
            pltpu.HBM((n, half, rows, BLOCK), frames.dtype),
            jax.ShapeDtypeStruct((n, move, rows, BLOCK), frames.dtype),
        ],
        in_specs=[pl.BlockSpec(memory_space=pltpu.SMEM)] + [WHOLE] * 2,
        out_specs=[ANYWHERE, WHOLE],
        scratch_shapes=[
            pltpu.VMEM((n, half - move, rows, BLOCK), frames.dtype),
            pltpu.SemaphoreType.DMA,
        ],
        bytes_accessed=4 * 1024 * 1024,
    )(meta, cm, frames)


def share_kernel(meta_ref, tail_ref, theirs_ref, *refs):
    _, out_hbm, out_ref, sems = refs
    n, move = out_ref.shape[:2]
    half = out_hbm.shape[1]
    lead = half - move
    counts = meta_ref[COUNT : COUNT + 1, 0:BLOCK]
    for q in range(n):
        count = jnp.broadcast_to(counts[:, q : q + 1], (1, BLOCK))
        used = jnp.maximum(count, lead) - lead
        block = [tail_ref[q, i] for i in range(move)]
        for skip in range(move):
            fits = ((used == skip) & (count < half)).astype(jnp.float32).astype(jnp.bfloat16)
            for i in range(skip, move):
                block[i] = block[i] + theirs_ref[q, i - skip] * fits
        for i in range(move):
            out_ref[q, i] = block[i]
        pltpu.make_async_copy(out_ref.at[q], out_hbm.at[q, lead:half], sems.at[q]).start()
    for q in range(n):
        pltpu.make_async_copy(out_ref.at[q], out_hbm.at[q, lead:half], sems.at[q]).wait()


def share(meta, packed, tail, theirs):
    return call(
        share_kernel,
        "share",
        pltpu.HBM(packed.shape, packed.dtype),
        in_specs=[WHOLE] * 3 + [ANYWHERE],
        out_specs=ANYWHERE,
        input_output_aliases={3: 0},
        scratch_shapes=[
            pltpu.VMEM(tail.shape, tail.dtype),
            pltpu.SemaphoreType.DMA((packed.shape[0],)),
        ],
        bytes_accessed=4 * 1024 * 1024,
    )(meta, tail, theirs, packed)


def lay_out(raw_ref, first, padded):
    n, _, rows, _ = raw_ref.shape
    total = n * rows
    zero = jnp.zeros((PAD, BLOCK), jnp.float32)
    for slot in range(padded.shape[0]):
        padded[slot, 0:PAD] = zero
        padded[slot, PAD + total : 2 * PAD + total] = zero
        for i in range(n):
            start = PAD + i * rows
            padded[slot, start : start + rows] = raw_ref[i, first + slot].astype(jnp.float32)


def norm_rows(padded, start, chunk, out_ref):
    total = out_ref.shape[0]
    base = PAD + start
    for slot in range(padded.shape[0]):
        raw = padded[slot, base : base + chunk]
        summed = raw
        for offset in range(1, HALF_WIN + 1):
            summed = summed + padded[slot, base - offset : base - offset + chunk]
            summed = summed + padded[slot, base + offset : base + offset + chunk]
        if start == 0 or start + chunk == total:
            frame = start + lax.broadcasted_iota(jnp.int32, (chunk, BLOCK), 0)
            upper = jnp.minimum(frame + HALF_WIN, total - 1)
            lower = jnp.maximum(frame - HALF_WIN, 0)
            mean = summed / (upper - lower + 1).astype(jnp.float32)
        else:
            mean = summed * (1.0 / (2 * HALF_WIN + 1))
        normed = jnp.where(summed > 0.0, raw / mean, 0.0)
        out_ref[start : start + chunk, slot * BLOCK : (slot + 1) * BLOCK] = normed.astype(
            jnp.bfloat16
        )


def norm_kernel(first, raw_ref, *refs):
    out_ref, padded = refs[-2:]
    lay_out(raw_ref, first, padded)
    for start in range(0, out_ref.shape[0], CHUNK):
        norm_rows(padded, start, CHUNK, out_ref)


def normalise(raw, first, slots, after=()):
    n, _, rows, _ = raw.shape
    total = n * rows
    return call(
        functools.partial(norm_kernel, first),
        "normalise",
        jax.ShapeDtypeStruct((total, slots * BLOCK), jnp.bfloat16),
        flops=12 * total * slots * BLOCK,
        bytes_accessed=4 * total * slots * BLOCK,
        in_specs=[WHOLE] + [ANYWHERE] * len(after),
        out_specs=WHOLE,
        scratch_shapes=[pltpu.VMEM((slots, total + 2 * PAD, BLOCK), jnp.float32)],
    )(raw, *after)


def dot_nt(a, b):
    return lax.dot_general(a, b, (((1,), (1,)), ((), ())), preferred_element_type=jnp.float32)


def set_left(ref, left_ref):
    rows = left_ref.shape[0] - ONES
    first_row = pl.multiple_of(lax.axis_index("pix") * rows, rows)
    left_ref[0:rows] = ref[pl.ds(first_row, rows), :]
    left_ref[rows : rows + ONES] = jnp.ones((ONES, ref.shape[1]), jnp.bfloat16)


def add_sums(pairs, sums, column):
    gram, frame = sums
    rows = pairs[0][0].shape[0] - ONES
    for left_ref, ref in pairs:
        both = dot_nt(left_ref[...], ref[column, :])
        gram = gram + both[0:rows]
        frame = frame + both[rows : rows + 8]
    return gram, frame


def partial_kernel(count, *refs):
    normed, lefts, (gram_out, frame_out) = refs[:count], refs[-count:], refs[-count - 2 : -count]
    before = refs[count : -count - 2]
    for ref, left_ref in zip(normed, lefts):
        set_left(ref, left_ref)
    for start in range(0, gram_out.shape[1], TILE):
        column = slice(start, start + TILE)
        sums = [ref[:, column] for ref in before] or [0.0, 0.0]
        gram_out[:, column], frame_out[:, column] = add_sums(
            list(zip(lefts, normed)), sums, column
        )


def sums_shape(total, parts):
    return [
        jax.ShapeDtypeStruct((total // parts, total), jnp.float32),
        jax.ShapeDtypeStruct((8, total), jnp.float32),
    ]


def partial_sums(normed, before, parts):
    total, width = normed[0].shape
    rows = total // parts
    return call(
        functools.partial(partial_kernel, len(normed)),
        "partial_sums",
        sums_shape(total, parts),
        flops=2 * rows * total * width * len(normed),
        bytes_accessed=4 * rows * total,
        in_specs=[WHOLE] * (len(normed) + len(before)),
        out_specs=[WHOLE] * 2,
        scratch_shapes=[pltpu.VMEM((rows + ONES, x.shape[1]), x.dtype) for x in normed],
    )(*normed, *before)


def norm_sums_kernel(first, raw_ref, done_ref, out_ref, gram_out, frame_out, padded, left_ref):
    total = out_ref.shape[0]
    tiles = total // TILE
    lay_out(raw_ref, first, padded)
    set_left(done_ref, left_ref)
    for i in range(tiles):
        column = slice(i * TILE, (i + 1) * TILE)
        gram_out[:, column], frame_out[:, column] = add_sums(
            [(left_ref, done_ref)], [0.0, 0.0], column
        )
        for start in range(i * TILE, (i + 1) * TILE, CHUNK):
            norm_rows(padded, start, CHUNK, out_ref)


def normalise_and_sum(raw, done, parts):
    n, slots, rows, _ = raw.shape
    total, width = done.shape
    first = width // BLOCK
    return call(
        functools.partial(norm_sums_kernel, first),
        "normalise_and_sum",
        [jax.ShapeDtypeStruct((total, (slots - first) * BLOCK), jnp.bfloat16)]
        + sums_shape(total, parts),
        flops=2 * total // parts * total * width,
        bytes_accessed=4 * total * total // parts,
        in_specs=[WHOLE] * 2,
        out_specs=[WHOLE] * 3,
        scratch_shapes=[
            pltpu.VMEM((slots - first, total + 2 * PAD, BLOCK), jnp.float32),
            pltpu.VMEM((total // parts + ONES, width), jnp.bfloat16),
        ],
    )(raw, done)


def result_kernel(meta_ref, their_meta_ref, normed_ref, gram_in, frame_in, out_hbm, *scratch):
    out_ref, frame_ref, sems = scratch
    rows, total = gram_in.shape
    pixels = meta_ref[PIXELS : PIXELS + 1, 0:BLOCK] + their_meta_ref[PIXELS : PIXELS + 1, 0:BLOCK]
    own = lax.broadcasted_iota(jnp.int32, (1, BLOCK), 1) == lax.axis_index("frame")
    number = jnp.sum(jnp.where(own, pixels, 0).astype(jnp.float32), axis=1, keepdims=True)
    ones = jnp.ones((8, normed_ref.shape[1]), jnp.bfloat16)
    frame_ref[...] = frame_in[...] + dot_nt(ones, normed_ref[...])
    first_row = pl.multiple_of(lax.axis_index("pix") * rows, rows)
    row_sum = jnp.broadcast_to(frame_ref[0:1, pl.ds(first_row, rows)], (BLOCK, rows)).T
    row_inv = 1.0 / row_sum[:, 0:1]
    left = normed_ref[pl.ds(first_row, rows), :]
    copies = []
    for i, start in enumerate(range(0, total, TILE)):
        column = slice(start, start + TILE)
        gram = gram_in[:, column] + dot_nt(left, normed_ref[column, :])
        col_inv = 1.0 / frame_ref[0:1, column]
        result = ((gram * row_inv) * col_inv) * number - 1.0
        out_ref[i] = result.astype(jnp.bfloat16)
        copies.append(
            pltpu.make_async_copy(out_ref.at[i], out_hbm.at[0, :, column], sems.at[i])
        )
        copies[-1].start()
    for copy in copies:
        copy.wait()


def correlate(metas, normed, before):
    rows, total = before[0].shape
    tiles = total // TILE
    return call(
        result_kernel,
        "correlate",
        pltpu.HBM((1, rows, total), jnp.bfloat16),
        flops=2 * rows * total * normed.shape[1],
        bytes_accessed=6 * rows * total,
        in_specs=[WHOLE] * 5,
        out_specs=ANYWHERE,
        scratch_shapes=[
            pltpu.VMEM((tiles, rows, TILE), jnp.bfloat16),
            pltpu.VMEM((8, total), jnp.float32),
            pltpu.SemaphoreType.DMA((tiles,)),
        ],
    )(*metas, normed, *before)


def body(frames, cycle_map):
    p_sec = frames.shape[1]
    n = lax.axis_size("frame")
    parts = lax.axis_size("pix")
    cap_blocks = p_sec // n // BLOCK
    half = (cap_blocks + 2) // 2
    move = cap_blocks - half
    lead = half - move
    early = half - half // 2
    cm = cycle_map.reshape(p_sec // BLOCK, BLOCK)

    def swap(x):
        return lax.ppermute(x, "pix", SWAP)

    def send(blocks):
        return lax.all_to_all(blocks, "frame", split_axis=0, concat_axis=0, tiled=True)

    moving, meta = pack_move(cm, frames, cap_blocks, move)
    theirs = swap(moving)
    packed, tail = pack_own(meta, cm, frames, cap_blocks, half, move)
    packed = share(meta, packed, tail, theirs)
    received = send(packed)

    meta, _ = lax.optimization_barrier((meta, packed))
    their_meta = swap(meta)
    counts, their_counts = meta[COUNT, :n], their_meta[COUNT, :n]
    overflow = jnp.max(counts + their_counts) > 2 * half

    first = normalise(received, 0, early, [overflow.astype(jnp.int32).reshape(1)])
    their_first = swap(first)
    last, *sums = normalise_and_sum(received, first, parts)
    their_last = swap(last)
    sums = partial_sums([last], sums, parts)
    sums = partial_sums([their_first], sums, parts)

    def spill(moving, meta, their_meta, their_last, *sums):
        moved = half - jnp.maximum(their_meta[COUNT, :n], lead)
        stays = jnp.arange(move, dtype=jnp.int32)[None, :] >= moved[:, None]
        rest = jnp.where(stays[:, :, None, None], moving, jnp.zeros((), moving.dtype))
        normed = normalise(send(rest), 0, move)
        sums = partial_sums([normed, swap(normed)], sums, parts)
        return correlate([meta, their_meta], their_last, sums)

    def fits(moving, meta, their_meta, their_last, *sums):
        return correlate([meta, their_meta], their_last, sums)

    return lax.cond(overflow, spill, fits, moving, meta, their_meta, their_last, *sums)


def solution(mesh):
    return jax.shard_map(
        body,
        mesh=mesh,
        in_specs=(P("frame", "pix"), P("pix")),
        out_specs=P("frame", "pix", None),
        check_vma=False,
    )
```

profile of v0, /device:TPU:11, one launch (start us, length us, event | category | flops | bytes accessed | tf_op | source)
XLA Modules:
  0.0 50.2 jit_solution(11741375931320614957)
XLA Ops:
  0.0 0.0 copy-start
  0.0 0.0 copy-start.1
  0.0 2.3 %pack_move.1 = (bf16[16,3,64,128]{3,2,1,0:T(8,128)(2,1)S(1)}, s32[8,128]{1,0:T(8,128)S(1)}) custom-call(s32[128,128]{1,0:T(8,128)} %bitcast.4, bf16[64,16384]{1,0:T(8,128)(2,1)} %frames_ref.1), custom_call_target="tpu_custom_call" | custom-call | tf_op jit(solution)/shard_map/pack_move/pallas_call | solution.py:96
  2.3 0.7 %collective-permute-start.1 = (bf16[16,3,64,128]{3,2,1,0:T(8,128)(2,1)S(1)}, bf16[16,3,64,128]{3,2,1,0:T(8,128)(2,1)S(1)}, u32[]{:S(2)}, u32[]{:S(2)}) collective-permute-start(bf16[16,3,64,128]{3,2,1,0:T(8,128)(2,1)S(1)} %get-tuple-element.57), channel_id=1, source_target_pairs={{0,1},{1,0},{2,3},{3,2},{4,5},{5,4},{6,7},{7,6},{8,9},{9,8},{10,11... | collective-permute-start | bytes 2359304 | tf_op jit(solution)/shard_map/ppermute | solution.py:393
  3.0 0.0 copy-done
  3.0 0.0 copy-done.1
  3.0 1.6 %pack_own.1 = (bf16[16,5,64,128]{3,2,1,0:T(8,128)(2,1)}, bf16[16,3,64,128]{3,2,1,0:T(8,128)(2,1)S(1)}) custom-call(s32[8,128]{1,0:T(8,128)S(1)} %get-tuple-element.59.meta_s.meta_ref, s32[128,128]{1,0:T(8,128)S(1)} %bitcast.5, bf16[64,16384]{1,0:T(8,128)(2,1)S(1)} %copy-done), custom_call_target="tpu_custom_call" | custom-call | bytes 4194304 | tf_op jit(solution)/shard_map/pack_own/pallas_call | solution.py:135
  4.6 0.3 collective-permute-done.1.theirs_ref
  4.9 1.2 %share.1 = bf16[16,5,64,128]{3,2,1,0:T(8,128)(2,1)} custom-call(s32[8,128]{1,0:T(8,128)S(1)} %get-tuple-element.59.meta_s.meta_ref, bf16[16,3,64,128]{3,2,1,0:T(8,128)(2,1)S(1)} %get-tuple-element.56.tail_ref, bf16[16,3,64,128]{3,2,1,0:T(8,128)(2,1)S(1)} %collective-permute-done.1.theirs_ref, ...), custom_call_target="tpu_custom_call", output_to_operand_aliasing={{}: (3, {})} | custom-call | bytes 4194304 | tf_op jit(solution)/shard_map/share/pallas_call | solution.py:174
  6.2 6.6 %all-to-all-start.1 = ((bf16[16,5,64,128]{3,2,1,0:T(8,128)(2,1)}), bf16[16,5,64,128]{3,2,1,0:T(8,128)(2,1)S(1)}, u32[]{:S(2)}, u32[]{:S(2)}) async-start(bf16[16,5,64,128]{3,2,1,0:T(8,128)(2,1)} %share.1), calls=%async_computation.1 | async-start | bytes 2621440 | tf_op jit(solution)/shard_map/all_to_all | solution.py:396
  12.8 0.9 %collective-permute-start.2 = (s32[8,128]{1,0:T(8,128)S(1)}, s32[8,128]{1,0:T(8,128)S(1)}, u32[]{:S(2)}, u32[]{:S(2)}) collective-permute-start(s32[8,128]{1,0:T(8,128)S(1)} %get-tuple-element.59.meta_s.meta_ref), channel_id=1, source_target_pairs={{0,1},{1,0},{2,3},{3,2},{4,5},{5,4},{6,7},{7,6},{8,9},{9,8},{10,11... | collective-permute-start | bytes 12296 | tf_op jit(solution)/shard_map/ppermute | solution.py:393
  13.8 0.8 %collective-permute-done.2 = s32[8,128]{1,0:T(8,128)S(1)} collective-permute-done((s32[8,128]{1,0:T(8,128)S(1)}, s32[8,128]{1,0:T(8,128)S(1)}, u32[]{:S(2)}, u32[]{:S(2)}) %collective-permute-start.2) | collective-permute-done | bytes 4128 | tf_op jit(solution)/shard_map/ppermute | solution.py:393
  14.6 0.6 %add_reduce_fusion = s32[]{:T(128)} fusion(s32[8,128]{1,0:T(8,128)S(1)} %collective-permute-done.2, s32[8,128]{1,0:T(8,128)S(1)} %get-tuple-element.59.meta_s.meta_ref), kind=kLoop, calls=%fused_computation.3 | loop fusion | flops 31 | bytes 132 | tf_op jit(solution)/shard_map/reduce_max | solution.py:407
  15.9 26.3 %all-to-all-done.1.raw_ref = bf16[16,5,64,128]{3,2,1,0:T(8,128)(2,1)S(1)} async-done(((bf16[16,5,64,128]{3,2,1,0:T(8,128)(2,1)}), bf16[16,5,64,128]{3,2,1,0:T(8,128)(2,1)S(1)}, u32[]{:S(2)}, u32[]{:S(2)}) %all-to-all-start.1) | async-done | bytes 1310752 | tf_op jit(solution)/shard_map/all_to_all | solution.py:396
  42.1 0.6 %normalise.3.done_ref = bf16[1024,384]{1,0:T(8,128)(2,1)S(1)} custom-call(bf16[16,5,64,128]{3,2,1,0:T(8,128)(2,1)S(1)} %all-to-all-done.1.raw_ref, s32[1]{0:T(128)} %bitcast.2.refs_0_), custom_call_target="tpu_custom_call" | custom-call | flops 4718592 | bytes 1572864 | tf_op jit(solution)/shard_map/normalise/pallas_call | solution.py:233
  42.8 2.6 %collective-permute-start.4 = (bf16[1024,384]{1,0:T(8,128)(2,1)S(1)}, bf16[1024,384]{1,0:T(8,128)(2,1)S(1)}, u32[]{:S(2)}, u32[]{:S(2)}) collective-permute-start(bf16[1024,384]{1,0:T(8,128)(2,1)S(1)} %normalise.3.done_ref), channel_id=1, source_target_pairs={{0,1},{1,0},{2,3},{3,2},{4,5},{5,4},{6,7},{7,6},{8,9},{9,8},{10,11... | collective-permute-start | bytes 2359304 | tf_op jit(solution)/shard_map/ppermute | solution.py:393
  45.4 1.0 %normalise_and_sum.1 = (bf16[1024,256]{1,0:T(8,128)(2,1)S(1)}, f32[512,1024]{1,0:T(8,128)S(1)}, f32[8,1024]{1,0:T(8,128)S(1)}) custom-call(bf16[16,5,64,128]{3,2,1,0:T(8,128)(2,1)S(1)} %all-to-all-done.1.raw_ref, bf16[1024,384]{1,0:T(8,128)(2,1)S(1)} %normalise.3.done_ref), custom_call_target="tpu_custom_call" | custom-call | flops 402653184 | bytes 2097152 | tf_op jit(solution)/shard_map/normalise_and_sum/pallas_call | solution.py:319
  46.4 0.1 collective-permute-start.3
  46.5 0.5 partial_sums.4
  47.0 0.3 collective-permute-done.4.refs_0_
  47.3 0.8 %partial_sums.5 = (f32[512,1024]{1,0:T(8,128)S(1)}, f32[8,1024]{1,0:T(8,128)S(1)}) custom-call(bf16[1024,384]{1,0:T(8,128)(2,1)S(1)} %collective-permute-done.4.refs_0_, f32[512,1024]{1,0:T(8,128)S(1)} %get-tuple-element.63.refs_1_, f32[8,1024]{1,0:T(8,128)S(1)} %get-tuple-element.64.refs_2_), custom_call_target="tpu_custom_call" | custom-call | flops 402653184 | bytes 2097152 | tf_op jit(solution)/shard_map/partial_sums/pallas_call | solution.py:289
  48.1 0.3 collective-permute-done.3
  48.4 1.8 %conditional.1 = (bf16[1,512,1024]{2,1,0:T(8,128)(2,1)}) conditional(s32[]{:T(128)} %convert_element_type.4, (s32[8,128]{1,0:T(8,128)S(1)}, s32[8,128]{1,0:T(8,128)S(1)}, bf16[1024,256]{1,0:T(8,128)(2,1)S(1)}, f32[512,1024]{1,0:T(8,128)S(1)}, f32[8,1024]{1,0:T(8,128)S(1)}) %tuple.13, (s32[8,128]{1,0:T(8,128)S(1)}, ...), branch_computations={%region_1.0_spmd, %region_2.3_spmd} | conditional | flops 1078853632 | bytes 13107536 | solution.py:427
  48.4 1.7 %correlate.2 = bf16[1,512,1024]{2,1,0:T(8,128)(2,1)} custom-call(s32[8,128]{1,0:T(8,128)S(1)} %get-tuple-element.30.meta_ref, s32[8,128]{1,0:T(8,128)S(1)} %get-tuple-element.31.their_meta_ref, bf16[1024,256]{1,0:T(8,128)(2,1)S(1)} %get-tuple-element.32.normed_ref, f32[512,1024]{1,0:T(8,128)S(1)} %get-tuple-element.33.gram_in, ...), custom_call_target="tpu_custom_call" | custom-call | flops 268435456 | bytes 3145728 | tf_op jit(solution)/shard_map/cond/branch_0_fun/correlate/pallas_call | solution.py:365
Async XLA Ops:
  0.0 3.0 %copy-start = (bf16[64,16384]{1,0:T(8,128)(2,1)S(1)}, bf16[64,16384]{1,0:T(8,128)(2,1)}, u32[]{:S(2)}) copy-start(bf16[64,16384]{1,0:T(8,128)(2,1)} %frames_ref.1) | copy-start | bytes 6291460
  0.0 3.0 %copy-start.1 = (s32[16384]{0:T(1024)S(1)}, s32[16384]{0:T(1024)}, u32[]{:S(2)}) copy-start(s32[16384]{0:T(1024)} %param.5) | copy-start | bytes 196612
  2.3 2.7 %collective-permute-start.1 = (bf16[16,3,64,128]{3,2,1,0:T(8,128)(2,1)S(1)}, bf16[16,3,64,128]{3,2,1,0:T(8,128)(2,1)S(1)}, u32[]{:S(2)}, u32[]{:S(2)}) collective-permute-start(bf16[16,3,64,128]{3,2,1,0:T(8,128)(2,1)S(1)} %get-tuple-element.57), channel_id=1, source_target_pairs={{0,1},{1,0},{2,3},{3,2},{4,5},{5,4},{6,7},{7,6},{8,9},{9,8},{10,11... | collective-permute-start | bytes 2359304 | tf_op jit(solution)/shard_map/ppermute | solution.py:393
  6.2 36.0 %all-to-all-start.1 = ((bf16[16,5,64,128]{3,2,1,0:T(8,128)(2,1)}), bf16[16,5,64,128]{3,2,1,0:T(8,128)(2,1)S(1)}, u32[]{:S(2)}, u32[]{:S(2)}) async-start(bf16[16,5,64,128]{3,2,1,0:T(8,128)(2,1)} %share.1), calls=%async_computation.1 | async-start | bytes 2621440 | tf_op jit(solution)/shard_map/all_to_all | solution.py:396
  12.8 1.8 %collective-permute-start.2 = (s32[8,128]{1,0:T(8,128)S(1)}, s32[8,128]{1,0:T(8,128)S(1)}, u32[]{:S(2)}, u32[]{:S(2)}) collective-permute-start(s32[8,128]{1,0:T(8,128)S(1)} %get-tuple-element.59.meta_s.meta_ref), channel_id=1, source_target_pairs={{0,1},{1,0},{2,3},{3,2},{4,5},{5,4},{6,7},{7,6},{8,9},{9,8},{10,11... | collective-permute-start | bytes 12296 | tf_op jit(solution)/shard_map/ppermute | solution.py:393
  42.8 4.6 %collective-permute-start.4 = (bf16[1024,384]{1,0:T(8,128)(2,1)S(1)}, bf16[1024,384]{1,0:T(8,128)(2,1)S(1)}, u32[]{:S(2)}, u32[]{:S(2)}) collective-permute-start(bf16[1024,384]{1,0:T(8,128)(2,1)S(1)} %normalise.3.done_ref), channel_id=1, source_target_pairs={{0,1},{1,0},{2,3},{3,2},{4,5},{5,4},{6,7},{7,6},{8,9},{9,8},{10,11... | collective-permute-start | bytes 2359304 | tf_op jit(solution)/shard_map/ppermute | solution.py:393
  46.4 2.0 %collective-permute-start.3 = (bf16[1024,256]{1,0:T(8,128)(2,1)S(1)}, bf16[1024,256]{1,0:T(8,128)(2,1)S(1)}, u32[]{:S(2)}, u32[]{:S(2)}) collective-permute-start(bf16[1024,256]{1,0:T(8,128)(2,1)S(1)} %get-tuple-element.60.refs_0_), channel_id=1, source_target_pairs={{0,1},{1,0},{2,3},{3,2},{4,5},{5,4},{6,7},{7,6},{8,9},{9,8},{10,11... | collective-permute-start | bytes 1572872 | tf_op jit(solution)/shard_map/ppermute | solution.py:393
where the time goes:
time: 51 us; the launch traced here: 50.2 us
  waiting for transfers between devices  28.1 us (55%)
  starting transfers between devices  11 us (22%)
  Pallas kernels  9.71 us (19%)
  between operations  0.71 us (1%)
  other arithmetic  0.63 us (1%)
    all_to_all x1, waiting for transfers between devices, send(): lax.all_to_all(blocks, 'frame', split_axis=0, concat_axis=0, tiled=True)  26.3 us
    all_to_all x1, starting transfers between devices, send(): lax.all_to_all(blocks, 'frame', split_axis=0, concat_axis=0, tiled=True)  6.65 us
    ppermute x4, starting transfers between devices, swap(): return lax.ppermute(x, 'pix', SWAP)  4.4 us
    pallas_call x1, Pallas kernels, pack_move(): call(functools.partial(move_kernel, cap_blocks), 'pack_move', [jax.ShapeD...  2.27 us
    ppermute x4, waiting for transfers between devices, swap(): return lax.ppermute(x, 'pix', SWAP)  1.78 us
    pallas_call x1, Pallas kernels, correlate(): call(result_kernel, 'correlate', pltpu.HBM((1, rows, total), jnp.bfloat16...  1.74 us
    pallas_call x1, Pallas kernels, pack_own(): call(functools.partial(own_kernel, cap_blocks), 'pack_own', [pltpu.HBM((n...  1.58 us
    pallas_call x2, Pallas kernels, partial_sums(): call(functools.partial(partial_kernel, len(normed)), 'partial_sums', sums...  1.24 us
  transfers between devices with their start and end apart: 5, of which 5 were waited for; matrix products, arithmetic and copies ran while one was open for 1% of the time, Pallas kernels for 8%

commit v1 on v0

--- a/solution.py
+++ b/solution.py
@@ -15,6 +15,7 @@
 ONES = 16
 VMEM_BYTES = 32 * 1024 * 1024
 LIST, COUNT, PIXELS = 0, 1, 2
+MERGED = 2
 SWAP = [(0, 1), (1, 0)]
 WHOLE = pl.BlockSpec(memory_space=pltpu.VMEM)
 ANYWHERE = pl.BlockSpec(memory_space=pl.ANY)
@@ -33,46 +34,98 @@
     )
 
 
-def keep(cm_ref, block, wanted):
-    valid = (cm_ref[pl.ds(block, 1), :] >= 0) & wanted
-    return valid.astype(jnp.float32).astype(jnp.bfloat16)
+def dot_nt(a, b):
+    return lax.dot_general(a, b, (((1,), (1,)), ((), ())), preferred_element_type=jnp.float32)
+
+
+def count_half_rows(rows):
+    return max(16, rows // 2)
+
+
+def gate(wanted):
+    wanted = jnp.broadcast_to(wanted, (1, BLOCK))
+    return wanted.astype(jnp.float32).astype(jnp.bfloat16)
 
 
 def take(frames_ref, block):
     return frames_ref[:, pl.ds(pl.multiple_of(block * BLOCK, BLOCK), BLOCK)]
+
+
+def fold(block, right):
+    rows = block.shape[0] // 2
+    half = BLOCK // 2
+    early, late = block[0:rows].astype(jnp.float32), block[rows:].astype(jnp.float32)
+    left = lax.broadcasted_iota(jnp.int32, (rows, BLOCK), 1) < half
+    if right:
+        folded = jnp.where(left, pltpu.roll(early, half, 1), late)
+    else:
+        folded = jnp.where(left, early, pltpu.roll(late, half, 1))
+    spare = count_half_rows(block.shape[0]) - rows
+    if spare:
+        folded = jnp.concatenate([folded, jnp.zeros((spare, BLOCK), jnp.float32)])
+    return folded.astype(jnp.bfloat16)
+
+
+def unfold(folded, rows):
+    half = BLOCK // 2
+    early = folded[0 : rows // 2].astype(jnp.float32)
+    left = lax.broadcasted_iota(jnp.int32, early.shape, 1) < half
+    return jnp.where(left, early, 0.0), jnp.where(left, pltpu.roll(early, half, 1), 0.0)
+
+
+def find_members(cm):
+    blocks = cm.shape[0]
+    first = cm[:, 0:1]
+    member = first == lax.broadcasted_iota(jnp.int32, (blocks, BLOCK), 1)
+    row = lax.broadcasted_iota(jnp.int32, (blocks, blocks), 0)
+    col = lax.broadcasted_iota(jnp.int32, (blocks, blocks), 1)
+    earlier = (col < row).astype(jnp.float32).astype(jnp.bfloat16)
+    pixels = jnp.sum((cm >= 0).astype(jnp.float32), axis=1, keepdims=True)
+    return first, member.astype(jnp.float32), earlier, pixels
+
+
+def sum_before(earlier, member, values):
+    before = jnp.dot(
+        earlier, (member * values).astype(jnp.bfloat16), preferred_element_type=jnp.float32
+    )
+    return jnp.sum(before * member, axis=1, keepdims=True)
 
 
 def find_blocks(cm, cap_blocks, meta_ref):
     blocks = cm.shape[0]
     width = meta_ref.shape[1]
-    first = cm[:, 0:1]
-    member = first == lax.broadcasted_iota(jnp.int32, (blocks, BLOCK), 1)
-    member_f = member.astype(jnp.float32)
-    row = lax.broadcasted_iota(jnp.int32, (blocks, blocks), 0)
-    col = lax.broadcasted_iota(jnp.int32, (blocks, blocks), 1)
-    earlier = (col < row).astype(jnp.float32).astype(jnp.bfloat16)
-    before = jnp.dot(earlier, member_f.astype(jnp.bfloat16), preferred_element_type=jnp.float32)
-    rank = jnp.sum(before * member_f, axis=1, keepdims=True).astype(jnp.int32)
+    first, member, earlier, pixels = find_members(cm)
+    rank = sum_before(earlier, member, 1.0).astype(jnp.int32)
     slot = jnp.where(first >= 0, first * cap_blocks + rank, -1)
     hit = slot == lax.broadcasted_iota(jnp.int32, (blocks, width), 1)
     index = lax.broadcasted_iota(jnp.int32, (blocks, width), 0).astype(jnp.float32)
-    pixels = jnp.sum((cm >= 0).astype(jnp.float32), axis=1, keepdims=True)
     meta_ref[...] = jnp.zeros_like(meta_ref)
     meta_ref[LIST : LIST + 1, :] = jnp.sum(
         jnp.where(hit, index, 0.0), axis=0, keepdims=True
     ).astype(jnp.int32)
-    meta_ref[COUNT : COUNT + 1, 0:BLOCK] = jnp.sum(member_f, axis=0, keepdims=True).astype(
+    meta_ref[COUNT : COUNT + 1, 0:BLOCK] = jnp.sum(member, axis=0, keepdims=True).astype(
         jnp.int32
     )
     meta_ref[PIXELS : PIXELS + 1, 0:BLOCK] = jnp.sum(
-        member_f * pixels, axis=0, keepdims=True
+        member * pixels, axis=0, keepdims=True
     ).astype(jnp.int32)
+
+
+def find_places(cm):
+    _, member, earlier, pixels = find_members(cm)
+    valid = (cm >= 0).astype(jnp.float32)
+    row = lax.broadcasted_iota(jnp.int32, (BLOCK, BLOCK), 0)
+    col = lax.broadcasted_iota(jnp.int32, (BLOCK, BLOCK), 1)
+    before = (row < col).astype(jnp.float32).astype(jnp.bfloat16)
+    place = jnp.dot(valid.astype(jnp.bfloat16), before, preferred_element_type=jnp.float32)
+    return jnp.where(cm >= 0, place + sum_before(earlier, member, pixels), -1.0)
 
 
 def move_kernel(cap_blocks, cm_hbm, frames_hbm, out_ref, meta_ref, *scratch):
     frames_ref, cm_ref, meta_s, sems = scratch
-    n, move = out_ref.shape[:2]
-    half = cap_blocks - move
+    n = out_ref.shape[0]
+    rows = frames_ref.shape[0]
+    kept = cap_blocks // 2
     get_cm = pltpu.make_async_copy(cm_hbm, cm_ref, sems.at[0])
     get_cm.start()
     get_frames = pltpu.make_async_copy(frames_hbm, frames_ref, sems.at[1])
@@ -84,19 +137,27 @@
     to_scalars.wait()
     get_frames.wait()
     for q in range(n):
-        count = meta_s[COUNT, q]
-        for i in range(move):
-            block = meta_s[LIST, q * cap_blocks + half + i]
-            out_ref[q, i] = take(frames_ref, block) * keep(cm_ref, block, half + i < count)
-
-
-def pack_move(cm, frames, cap_blocks, move):
+        full = gate(meta_s[PIXELS, q] == cap_blocks * BLOCK)
+        for i in range(kept + 1, cap_blocks):
+            block = meta_s[LIST, q * cap_blocks + i]
+            start = (i - kept - 1) * rows
+            out_ref[q, start : start + rows] = take(frames_ref, block) * full
+        start = (cap_blocks - kept - 1) * rows
+        end = start + count_half_rows(rows)
+        block = meta_s[LIST, q * cap_blocks + kept]
+        out_ref[q, start:end] = fold(take(frames_ref, block), True) * full
+        out_ref[q, end : end + 16] = jnp.broadcast_to(full, (16, BLOCK))
+
+
+def pack_move(cm, frames, cap_blocks):
+    rows = frames.shape[0]
     n = cm.shape[0] // cap_blocks
+    height = (cap_blocks - cap_blocks // 2 - 1) * rows + count_half_rows(rows) + 16
     meta = jax.ShapeDtypeStruct((8, cm.shape[0]), jnp.int32)
     return call(
         functools.partial(move_kernel, cap_blocks),
         "pack_move",
-        [jax.ShapeDtypeStruct((n, move, frames.shape[0], BLOCK), frames.dtype), meta],
+        [jax.ShapeDtypeStruct((n, height, BLOCK), frames.dtype), meta],
         in_specs=[ANYWHERE] * 2,
         out_specs=[WHOLE] * 2,
         scratch_shapes=[
@@ -111,91 +172,127 @@
     )
 
 
-def own_kernel(cap_blocks, meta_s, cm_ref, frames_ref, out_hbm, tail_ref, lead_ref, sem):
-    n, lead = lead_ref.shape[:2]
-
-    def put(out_ref, first):
-        for q in range(n):
-            count = meta_s[COUNT, q]
-            for i in range(out_ref.shape[1]):
-                block = meta_s[LIST, q * cap_blocks + first + i]
-                kept = take(frames_ref, block) * keep(cm_ref, block, first + i < count)
-                out_ref[q, i] = kept
-
-    put(lead_ref, 0)
-    write = pltpu.make_async_copy(lead_ref, out_hbm.at[:, 0:lead], sem)
-    write.start()
-    put(tail_ref, lead)
-    write.wait()
-
-
-def pack_own(meta, cm, frames, cap_blocks, half, move):
+def own_kernel(cap_blocks, meta_s, cm_ref, frames_ref, out_ref, place_ref):
+    n = out_ref.shape[0]
+    rows = frames_ref.shape[0]
+    kept = cap_blocks // 2
+    place_ref[...] = find_places(cm_ref[...])
+    target = lax.broadcasted_iota(jnp.int32, (BLOCK, BLOCK), 0).astype(jnp.float32)
+    for q in range(n):
+        count, pixels = meta_s[COUNT, q], meta_s[PIXELS, q]
+        is_full = pixels == cap_blocks * BLOCK
+        full = gate(is_full)
+        fits = (pixels <= BLOCK) & (count <= MERGED)
+        compact = 0.0
+        for i in range(MERGED):
+            block = meta_s[LIST, q * cap_blocks + i]
+            place = jnp.where(fits & (i < count), place_ref[pl.ds(block, 1), :], -1.0)
+            chosen = (target == place).astype(jnp.float32).astype(jnp.bfloat16)
+            compact = compact + dot_nt(take(frames_ref, block), chosen)
+        block = meta_s[LIST, q * cap_blocks]
+        out_ref[q, 0:rows] = compact.astype(jnp.bfloat16) + take(frames_ref, block) * full
+        for i in range(1, kept):
+            block = meta_s[LIST, q * cap_blocks + i]
+            out_ref[q, i * rows : (i + 1) * rows] = take(frames_ref, block) * full
+        block = meta_s[LIST, q * cap_blocks + kept]
+        out_ref[q, kept * rows :] = fold(take(frames_ref, block), False) * full
+
+
+def pack_own(meta, cm, frames, cap_blocks):
     rows = frames.shape[0]
     n = cm.shape[0] // cap_blocks
+    height = cap_blocks // 2 * rows + count_half_rows(rows)
     return call(
         functools.partial(own_kernel, cap_blocks),
         "pack_own",
-        [
-            pltpu.HBM((n, half, rows, BLOCK), frames.dtype),
-            jax.ShapeDtypeStruct((n, move, rows, BLOCK), frames.dtype),
-        ],
+        jax.ShapeDtypeStruct((n, height, BLOCK), frames.dtype),
         in_specs=[pl.BlockSpec(memory_space=pltpu.SMEM)] + [WHOLE] * 2,
-        out_specs=[ANYWHERE, WHOLE],
+        out_specs=WHOLE,
+        scratch_shapes=[pltpu.VMEM(cm.shape, jnp.float32)],
+        bytes_accessed=4 * 1024 * 1024,
+    )(meta, cm, frames)
+
+
+def share_kernel(cap_blocks, rows, meta_ref, own_ref, theirs_ref, out_hbm, out_ref, sems):
+    n, height, _ = out_ref.shape
+    second = lax.axis_index("pix") != 0
+    pixels = meta_ref[PIXELS : PIXELS + 1, 0:BLOCK]
+    for q in range(n):
+        mine = jnp.broadcast_to(pixels[:, q : q + 1], (1, BLOCK)) == cap_blocks * BLOCK
+        theirs = theirs_ref[q, height - rows : height - rows + 16][0:1].astype(jnp.float32) > 0.0
+        helps = theirs & (second | jnp.logical_not(mine))
+        first = gate(jnp.logical_not(helps & mine))
+        own, other = gate(jnp.logical_not(helps)), gate(helps)
+        out_ref[q, 0:rows] = own_ref[q, 0:rows] * first
+        out_ref[q, rows:] = own_ref[q, rows:] * own + theirs_ref[q, 0 : height - rows] * other
+        pltpu.make_async_copy(out_ref.at[q], out_hbm.at[q], sems.at[q]).start()
+    for q in range(n):
+        pltpu.make_async_copy(out_ref.at[q], out_hbm.at[q], sems.at[q]).wait()
+
+
+def share(meta, own, theirs, cap_blocks, rows):
+    return call(
+        functools.partial(share_kernel, cap_blocks, rows),
+        "share",
+        pltpu.HBM(own.shape, own.dtype),
+        in_specs=[WHOLE] * 3,
+        out_specs=ANYWHERE,
         scratch_shapes=[
-            pltpu.VMEM((n, half - move, rows, BLOCK), frames.dtype),
-            pltpu.SemaphoreType.DMA,
+            pltpu.VMEM(own.shape, own.dtype),
+            pltpu.SemaphoreType.DMA((own.shape[0],)),
         ],
         bytes_accessed=4 * 1024 * 1024,
-    )(meta, cm, frames)
-
-
-def share_kernel(meta_ref, tail_ref, theirs_ref, *refs):
-    _, out_hbm, out_ref, sems = refs
-    n, move = out_ref.shape[:2]
-    half = out_hbm.shape[1]
-    lead = half - move
-    counts = meta_ref[COUNT : COUNT + 1, 0:BLOCK]
+    )(meta, own, theirs)
+
+
+def left_out(meta, their_meta, cap, second):
+    mine, theirs = meta[PIXELS] == cap, their_meta[PIXELS] == cap
+    fits = (meta[PIXELS] <= BLOCK) & (meta[COUNT] <= MERGED)
+    return theirs & (second | jnp.logical_not(mine)) & jnp.logical_not(fits)
+
+
+def rest_kernel(cap_blocks, meta_s, their_meta_s, frames_ref, cm_ref, out_ref):
+    n, _, rows, _ = out_ref.shape
+    second = lax.axis_index("pix") != 0
     for q in range(n):
-        count = jnp.broadcast_to(counts[:, q : q + 1], (1, BLOCK))
-        used = jnp.maximum(count, lead) - lead
-        block = [tail_ref[q, i] for i in range(move)]
-        for skip in range(move):
-            fits = ((used == skip) & (count < half)).astype(jnp.float32).astype(jnp.bfloat16)
-            for i in range(skip, move):
-                block[i] = block[i] + theirs_ref[q, i - skip] * fits
-        for i in range(move):
-            out_ref[q, i] = block[i]
-        pltpu.make_async_copy(out_ref.at[q], out_hbm.at[q, lead:half], sems.at[q]).start()
-    for q in range(n):
-        pltpu.make_async_copy(out_ref.at[q], out_hbm.at[q, lead:half], sems.at[q]).wait()
-
-
-def share(meta, packed, tail, theirs):
-    return call(
-        share_kernel,
-        "share",
-        pltpu.HBM(packed.shape, packed.dtype),
-        in_specs=[WHOLE] * 3 + [ANYWHERE],
-        out_specs=ANYWHERE,
-        input_output_aliases={3: 0},
-        scratch_shapes=[
-            pltpu.VMEM(tail.shape, tail.dtype),
-            pltpu.SemaphoreType.DMA((packed.shape[0],)),
-        ],
-        bytes_accessed=4 * 1024 * 1024,
-    )(meta, tail, theirs, packed)
-
-
-def lay_out(raw_ref, first, padded):
-    n, _, rows, _ = raw_ref.shape
+        counts = [[ref[row, q] for row in range(PIXELS + 1)] for ref in (meta_s, their_meta_s)]
+        wanted = left_out(*counts, cap_blocks * BLOCK, second)
+        for i in range(cap_blocks):
+            block = meta_s[LIST, q * cap_blocks + i]
+            valid = cm_ref[pl.ds(block, 1), :] >= 0
+            out_ref[q, i] = take(frames_ref, block) * gate(
+                valid & wanted & (i < meta_s[COUNT, q])
+            )
+
+
+def pack_rest(meta, their_meta, frames, cm, cap_blocks):
+    n = cm.shape[0] // cap_blocks
+    return call(
+        functools.partial(rest_kernel, cap_blocks),
+        "pack_rest",
+        jax.ShapeDtypeStruct((n, cap_blocks, frames.shape[0], BLOCK), frames.dtype),
+        in_specs=[pl.BlockSpec(memory_space=pltpu.SMEM)] * 2 + [WHOLE] * 2,
+        out_specs=WHOLE,
+    )(meta, their_meta, frames, cm)
+
+
+def lay_out(raw_ref, rows, first, padded):
+    n, height, _ = raw_ref.shape
     total = n * rows
     zero = jnp.zeros((PAD, BLOCK), jnp.float32)
-    for slot in range(padded.shape[0]):
-        padded[slot, 0:PAD] = zero
-        padded[slot, PAD + total : 2 * PAD + total] = zero
-        for i in range(n):
-            start = PAD + i * rows
-            padded[slot, start : start + rows] = raw_ref[i, first + slot].astype(jnp.float32)
+    for i in range(padded.shape[0]):
+        slot = first + i
+        padded[i, 0:PAD] = zero
+        padded[i, PAD + total : 2 * PAD + total] = zero
+        for source in range(n):
+            start = PAD + source * rows
+            if (slot + 1) * rows <= height:
+                block = raw_ref[source, slot * rows : (slot + 1) * rows]
+                padded[i, start : start + rows] = block.astype(jnp.float32)
+            else:
+                early, late = unfold(raw_ref[source, slot * rows : height], rows)
+                padded[i, start : start + rows // 2] = early
+                padded[i, start + rows // 2 : start + rows] = late
 
 
 def norm_rows(padded, start, chunk, out_ref):
@@ -220,18 +317,16 @@
         )
 
 
-def norm_kernel(first, raw_ref, *refs):
+def norm_kernel(rows, raw_ref, *refs):
     out_ref, padded = refs[-2:]
-    lay_out(raw_ref, first, padded)
+    lay_out(raw_ref, rows, 0, padded)
     for start in range(0, out_ref.shape[0], CHUNK):
         norm_rows(padded, start, CHUNK, out_ref)
 
 
-def normalise(raw, first, slots, after=()):
-    n, _, rows, _ = raw.shape
-    total = n * rows
-    return call(
-        functools.partial(norm_kernel, first),
+def normalise(raw, total, slots, after=()):
+    return call(
+        functools.partial(norm_kernel, total // raw.shape[0]),
         "normalise",
         jax.ShapeDtypeStruct((total, slots * BLOCK), jnp.bfloat16),
         flops=12 * total * slots * BLOCK,
@@ -240,10 +335,6 @@
         out_specs=WHOLE,
         scratch_shapes=[pltpu.VMEM((slots, total + 2 * PAD, BLOCK), jnp.float32)],
     )(raw, *after)
-
-
-def dot_nt(a, b):
-    return lax.dot_general(a, b, (((1,), (1,)), ((), ())), preferred_element_type=jnp.float32)
 
 
 def set_left(ref, left_ref):
@@ -298,10 +389,10 @@
     )(*normed, *before)
 
 
-def norm_sums_kernel(first, raw_ref, done_ref, out_ref, gram_out, frame_out, padded, left_ref):
+def norm_sums_kernel(rows, first, raw_ref, done_ref, out_ref, gram_out, frame_out, padded, left_ref):
     total = out_ref.shape[0]
     tiles = total // TILE
-    lay_out(raw_ref, first, padded)
+    lay_out(raw_ref, rows, first, padded)
     set_left(done_ref, left_ref)
     for i in range(tiles):
         column = slice(i * TILE, (i + 1) * TILE)
@@ -312,12 +403,11 @@
             norm_rows(padded, start, CHUNK, out_ref)
 
 
-def normalise_and_sum(raw, done, parts):
-    n, slots, rows, _ = raw.shape
+def normalise_and_sum(raw, done, slots, parts):
     total, width = done.shape
     first = width // BLOCK
     return call(
-        functools.partial(norm_sums_kernel, first),
+        functools.partial(norm_sums_kernel, total // raw.shape[0], first),
         "normalise_and_sum",
         [jax.ShapeDtypeStruct((total, (slots - first) * BLOCK), jnp.bfloat16)]
         + sums_shape(total, parts),
@@ -379,14 +469,13 @@
 
 
 def body(frames, cycle_map):
-    p_sec = frames.shape[1]
+    rows, p_sec = frames.shape
     n = lax.axis_size("frame")
     parts = lax.axis_size("pix")
+    total = n * rows
     cap_blocks = p_sec // n // BLOCK
-    half = (cap_blocks + 2) // 2
-    move = cap_blocks - half
-    lead = half - move
-    early = half - half // 2
+    slots = cap_blocks // 2 + 1
+    early = slots - slots // 2
     cm = cycle_map.reshape(p_sec // BLOCK, BLOCK)
 
     def swap(x):
@@ -395,36 +484,35 @@
     def send(blocks):
         return lax.all_to_all(blocks, "frame", split_axis=0, concat_axis=0, tiled=True)
 
-    moving, meta = pack_move(cm, frames, cap_blocks, move)
+    moving, meta = pack_move(cm, frames, cap_blocks)
     theirs = swap(moving)
-    packed, tail = pack_own(meta, cm, frames, cap_blocks, half, move)
-    packed = share(meta, packed, tail, theirs)
+    packed = share(meta, pack_own(meta, cm, frames, cap_blocks), theirs, cap_blocks, rows)
     received = send(packed)
 
     meta, _ = lax.optimization_barrier((meta, packed))
     their_meta = swap(meta)
-    counts, their_counts = meta[COUNT, :n], their_meta[COUNT, :n]
-    overflow = jnp.max(counts + their_counts) > 2 * half
-
-    first = normalise(received, 0, early, [overflow.astype(jnp.int32).reshape(1)])
+    second = lax.axis_index("pix") != 0
+    spills = left_out(meta[:, :n], their_meta[:, :n], cap_blocks * BLOCK, second)
+    spills |= left_out(their_meta[:, :n], meta[:, :n], cap_blocks * BLOCK, jnp.logical_not(second))
+    overflow = jnp.any(spills)
+
+    first = normalise(received, total, early, [overflow.astype(jnp.int32).reshape(1)])
     their_first = swap(first)
-    last, *sums = normalise_and_sum(received, first, parts)
+    last, *sums = normalise_and_sum(received, first, slots, parts)
     their_last = swap(last)
     sums = partial_sums([last], sums, parts)
     sums = partial_sums([their_first], sums, parts)
 
-    def spill(moving, meta, their_meta, their_last, *sums):
-        moved = half - jnp.maximum(their_meta[COUNT, :n], lead)
-        stays = jnp.arange(move, dtype=jnp.int32)[None, :] >= moved[:, None]
-        rest = jnp.where(stays[:, :, None, None], moving, jnp.zeros((), moving.dtype))
-        normed = normalise(send(rest), 0, move)
+    def spill(frames, cm, meta, their_meta, their_last, *sums):
+        rest = send(pack_rest(meta, their_meta, frames, cm, cap_blocks))
+        normed = normalise(rest.reshape(n, cap_blocks * rows, BLOCK), total, cap_blocks)
         sums = partial_sums([normed, swap(normed)], sums, parts)
         return correlate([meta, their_meta], their_last, sums)
 
-    def fits(moving, meta, their_meta, their_last, *sums):
+    def fits(frames, cm, meta, their_meta, their_last, *sums):
         return correlate([meta, their_meta], their_last, sums)
 
-    return lax.cond(overflow, spill, fits, moving, meta, their_meta, their_last, *sums)
+    return lax.cond(overflow, spill, fits, frames, cm, meta, their_meta, their_last, *sums)
 
 
 def solution(mesh):

time: 51 us -> 48.7 us (0.955)
  waiting for transfers between devices: 28.1 us -> 25.2 us
    all_to_all x1, waiting for transfers between devices: 26.3 us -> 23.4 us  [send(): lax.all_to_all(blocks, 'frame', split_axis=0, concat_axis=0, tiled=True)]
    reduce_or x0 -> x1, other arithmetic: none -> 0.64 us  [body(): overflow = jnp.any(spills)]
    reduce_max x1 -> x0, other arithmetic: 0.63 us -> none  [body(): overflow = jnp.max(counts + their_counts) > 2 * half]
  transfers between devices with their start and end apart: 5 -> 5, of which waited for: 5 -> 5; matrix products, arithmetic and copies ran while one was open for 1% -> 1% of each run, Pallas kernels for 8% -> 9%
where the time goes in v1:
time: 48.7 us; the launch traced here: 47.8 us
  waiting for transfers between devices  25.2 us (52%)
  starting transfers between devices  11 us (23%)
  Pallas kernels  10.2 us (21%)
  between operations  0.71 us (1%)
  other arithmetic  0.64 us (1%)
    all_to_all x1, waiting for transfers between devices, send(): lax.all_to_all(blocks, 'frame', split_axis=0, concat_axis=0, tiled=True)  23.4 us
    all_to_all x1, starting transfers between devices, send(): lax.all_to_all(blocks, 'frame', split_axis=0, concat_axis=0, tiled=True)  6.65 us
    ppermute x4, starting transfers between devices, swap(): return lax.ppermute(x, 'pix', SWAP)  4.31 us
    pallas_call x1, Pallas kernels, pack_move(): call(functools.partial(move_kernel, cap_blocks), 'pack_move', [jax.ShapeD...  2.3 us
    ppermute x4, waiting for transfers between devices, swap(): return lax.ppermute(x, 'pix', SWAP)  1.84 us
    pallas_call x1, Pallas kernels, pack_own(): call(functools.partial(own_kernel, cap_blocks), 'pack_own', jax.ShapeDtyp...  1.8 us
    pallas_call x1, Pallas kernels, correlate(): call(result_kernel, 'correlate', pltpu.HBM((1, rows, total), jnp.bfloat16...  1.74 us
    pallas_call x1, Pallas kernels, share(): call(functools.partial(share_kernel, cap_blocks, rows), 'share', pltpu.HB...  1.43 us
  transfers between devices with their start and end apart: 5, of which 5 were waited for; matrix products, arithmetic and copies ran while one was open for 1% of the time, Pallas kernels for 9%

profile of v1, /device:TPU:11, one launch (start us, length us, event | category | flops | bytes accessed | tf_op | source)
XLA Modules:
  0.0 47.8 jit_solution(16629183696058723465)
XLA Ops:
  0.0 0.0 copy-start
  0.0 0.0 copy-start.1
  0.0 2.3 %pack_move.1 = (bf16[16,240,128]{2,1,0:T(8,128)(2,1)S(1)}, s32[8,128]{1,0:T(8,128)S(1)}) custom-call(s32[128,128]{1,0:T(8,128)} %bitcast.32, bf16[64,16384]{1,0:T(8,128)(2,1)} %frames_ref.1), custom_call_target="tpu_custom_call" | custom-call | tf_op jit(solution)/shard_map/pack_move/pallas_call | solution.py:157
  2.3 0.7 %collective-permute-start.1 = (bf16[16,240,128]{2,1,0:T(8,128)(2,1)S(1)}, bf16[16,240,128]{2,1,0:T(8,128)(2,1)S(1)}, u32[]{:S(2)}, u32[]{:S(2)}) collective-permute-start(bf16[16,240,128]{2,1,0:T(8,128)(2,1)S(1)} %get-tuple-element.57), channel_id=1, source_target_pairs={{0,1},{1,0},{2,3},{3,2},{4,5},{5,4},{6,7},{7,6},{8,9},{9,8},{10,11... | collective-permute-start | bytes 2949128 | tf_op jit(solution)/shard_map/ppermute | solution.py:482
  3.0 0.0 copy-done
  3.1 0.0 copy-done.1
  3.1 1.8 %pack_own.1.own_ref = bf16[16,288,128]{2,1,0:T(8,128)(2,1)S(1)} custom-call(s32[8,128]{1,0:T(8,128)S(1)} %get-tuple-element.58.meta_s.meta_ref, s32[128,128]{1,0:T(8,128)S(1)} %bitcast.33, bf16[64,16384]{1,0:T(8,128)(2,1)S(1)} %copy-done), custom_call_target="tpu_custom_call" | custom-call | bytes 4194304 | tf_op jit(solution)/shard_map/pack_own/pallas_call | solution.py:205
  4.9 0.4 collective-permute-done.1.theirs_ref
  5.2 1.4 %share.1 = bf16[16,288,128]{2,1,0:T(8,128)(2,1)} custom-call(s32[8,128]{1,0:T(8,128)S(1)} %get-tuple-element.58.meta_s.meta_ref, bf16[16,288,128]{2,1,0:T(8,128)(2,1)S(1)} %pack_own.1.own_ref, bf16[16,240,128]{2,1,0:T(8,128)(2,1)S(1)} %collective-permute-done.1.theirs_ref), custom_call_target="tpu_custom_call" | custom-call | bytes 4194304 | tf_op jit(solution)/shard_map/share/pallas_call | solution.py:234
  6.7 6.6 %all-to-all-start.1 = ((bf16[16,288,128]{2,1,0:T(8,128)(2,1)}), bf16[16,288,128]{2,1,0:T(8,128)(2,1)S(1)}, u32[]{:S(2)}, u32[]{:S(2)}) async-start(bf16[16,288,128]{2,1,0:T(8,128)(2,1)} %share.1), calls=%async_computation.1 | async-start | bytes 2359296 | tf_op jit(solution)/shard_map/all_to_all | solution.py:485
  13.3 0.9 %collective-permute-start.2 = (s32[8,128]{1,0:T(8,128)S(1)}, s32[8,128]{1,0:T(8,128)S(1)}, u32[]{:S(2)}, u32[]{:S(2)}) collective-permute-start(s32[8,128]{1,0:T(8,128)S(1)} %get-tuple-element.58.meta_s.meta_ref), channel_id=1, source_target_pairs={{0,1},{1,0},{2,3},{3,2},{4,5},{5,4},{6,7},{7,6},{8,9},{9,8},{10,11... | collective-permute-start | bytes 12296 | tf_op jit(solution)/shard_map/ppermute | solution.py:482
  14.3 0.8 %collective-permute-done.2 = s32[8,128]{1,0:T(8,128)S(1)} collective-permute-done((s32[8,128]{1,0:T(8,128)S(1)}, s32[8,128]{1,0:T(8,128)S(1)}, u32[]{:S(2)}, u32[]{:S(2)}) %collective-permute-start.2) | collective-permute-done | bytes 4128 | tf_op jit(solution)/shard_map/ppermute | solution.py:482
  15.1 0.6 %fusion.1 = pred[]{:T(512)} fusion(pred[]{:T(512)S(6)} %not.24, pred[]{:T(512)S(6)} %ne.3, s32[8,128]{1,0:T(8,128)S(1)} %collective-permute-done.2, s32[8,128]{1,0:T(8,128)S(1)} %get-tuple-element.58.meta_s.meta_ref), kind=kLoop, calls=%fused_computation.2 | loop fusion | flops 319 | bytes 259 | tf_op jit(solution)/shard_map/reduce_or | solution.py:497
  16.4 23.4 %all-to-all-done.1.raw_ref = bf16[16,288,128]{2,1,0:T(8,128)(2,1)S(1)} async-done(((bf16[16,288,128]{2,1,0:T(8,128)(2,1)}), bf16[16,288,128]{2,1,0:T(8,128)(2,1)S(1)}, u32[]{:S(2)}, u32[]{:S(2)}) %all-to-all-start.1) | async-done | bytes 1179680 | tf_op jit(solution)/shard_map/all_to_all | solution.py:485
  39.8 0.6 %normalise.3.done_ref = bf16[1024,384]{1,0:T(8,128)(2,1)S(1)} custom-call(bf16[16,288,128]{2,1,0:T(8,128)(2,1)S(1)} %all-to-all-done.1.raw_ref, s32[1]{0:T(128)} %bitcast.6.refs_0_), custom_call_target="tpu_custom_call" | custom-call | flops 4718592 | bytes 1572864 | tf_op jit(solution)/shard_map/normalise/pallas_call | solution.py:328
  40.4 2.6 %collective-permute-start.4 = (bf16[1024,384]{1,0:T(8,128)(2,1)S(1)}, bf16[1024,384]{1,0:T(8,128)(2,1)S(1)}, u32[]{:S(2)}, u32[]{:S(2)}) collective-permute-start(bf16[1024,384]{1,0:T(8,128)(2,1)S(1)} %normalise.3.done_ref), channel_id=1, source_target_pairs={{0,1},{1,0},{2,3},{3,2},{4,5},{5,4},{6,7},{7,6},{8,9},{9,8},{10,11... | collective-permute-start | bytes 2359304 | tf_op jit(solution)/shard_map/ppermute | solution.py:482
  43.0 1.1 %normalise_and_sum.1 = (bf16[1024,256]{1,0:T(8,128)(2,1)S(1)}, f32[512,1024]{1,0:T(8,128)S(1)}, f32[8,1024]{1,0:T(8,128)S(1)}) custom-call(bf16[16,288,128]{2,1,0:T(8,128)(2,1)S(1)} %all-to-all-done.1.raw_ref, bf16[1024,384]{1,0:T(8,128)(2,1)S(1)} %normalise.3.done_ref), custom_call_target="tpu_custom_call" | custom-call | flops 402653184 | bytes 2097152 | tf_op jit(solution)/shard_map/normalise_and_sum/pallas_call | solution.py:409
  44.1 0.1 collective-permute-start.3
  44.1 0.5 partial_sums.4
  44.6 0.3 collective-permute-done.4.refs_0_
  44.9 0.8 %partial_sums.5 = (f32[512,1024]{1,0:T(8,128)S(1)}, f32[8,1024]{1,0:T(8,128)S(1)}) custom-call(bf16[1024,384]{1,0:T(8,128)(2,1)S(1)} %collective-permute-done.4.refs_0_, f32[512,1024]{1,0:T(8,128)S(1)} %get-tuple-element.62.refs_1_, f32[8,1024]{1,0:T(8,128)S(1)} %get-tuple-element.63.refs_2_), custom_call_target="tpu_custom_call" | custom-call | flops 402653184 | bytes 2097152 | tf_op jit(solution)/shard_map/partial_sums/pallas_call | solution.py:380
  45.6 0.4 collective-permute-done.3
  46.0 1.7 %conditional.1 = (bf16[1,512,1024]{2,1,0:T(8,128)(2,1)}) conditional(s32[]{:T(128)} %convert_element_type.4, (s32[8,128]{1,0:T(8,128)S(1)}, s32[8,128]{1,0:T(8,128)S(1)}, bf16[1024,256]{1,0:T(8,128)(2,1)S(1)}, f32[512,1024]{1,0:T(8,128)S(1)}, f32[8,1024]{1,0:T(8,128)S(1)}) %tuple.13, (s32[8,128]{1,0:T(8,128)S(1)}, s32[8,128]{1,0:T(8,128)S(1)}, ...), branch_computations={%region_1.0_spmd, %region_2.0_spmd} | conditional | flops 2428502016 | bytes 22020144 | solution.py:515
  46.0 1.7 %correlate.2 = bf16[1,512,1024]{2,1,0:T(8,128)(2,1)} custom-call(s32[8,128]{1,0:T(8,128)S(1)} %get-tuple-element.32.meta_ref, s32[8,128]{1,0:T(8,128)S(1)} %get-tuple-element.33.their_meta_ref, bf16[1024,256]{1,0:T(8,128)(2,1)S(1)} %get-tuple-element.34.normed_ref, f32[512,1024]{1,0:T(8,128)S(1)} %get-tuple-element.35.gram_in, ...), custom_call_target="tpu_custom_call" | custom-call | flops 268435456 | bytes 3145728 | tf_op jit(solution)/shard_map/cond/branch_0_fun/correlate/pallas_call | solution.py:455
Async XLA Ops:
  0.0 3.1 %copy-start = (bf16[64,16384]{1,0:T(8,128)(2,1)S(1)}, bf16[64,16384]{1,0:T(8,128)(2,1)}, u32[]{:S(2)}) copy-start(bf16[64,16384]{1,0:T(8,128)(2,1)} %frames_ref.1) | copy-start | bytes 6291460
  0.0 3.1 %copy-start.1 = (s32[16384]{0:T(1024)S(1)}, s32[16384]{0:T(1024)}, u32[]{:S(2)}) copy-start(s32[16384]{0:T(1024)} %param.5) | copy-start | bytes 196612
  2.3 2.9 %collective-permute-start.1 = (bf16[16,240,128]{2,1,0:T(8,128)(2,1)S(1)}, bf16[16,240,128]{2,1,0:T(8,128)(2,1)S(1)}, u32[]{:S(2)}, u32[]{:S(2)}) collective-permute-start(bf16[16,240,128]{2,1,0:T(8,128)(2,1)S(1)} %get-tuple-element.57), channel_id=1, source_target_pairs={{0,1},{1,0},{2,3},{3,2},{4,5},{5,4},{6,7},{7,6},{8,9},{9,8},{10,11... | collective-permute-start | bytes 2949128 | tf_op jit(solution)/shard_map/ppermute | solution.py:482
  6.7 33.1 %all-to-all-start.1 = ((bf16[16,288,128]{2,1,0:T(8,128)(2,1)}), bf16[16,288,128]{2,1,0:T(8,128)(2,1)S(1)}, u32[]{:S(2)}, u32[]{:S(2)}) async-start(bf16[16,288,128]{2,1,0:T(8,128)(2,1)} %share.1), calls=%async_computation.1 | async-start | bytes 2359296 | tf_op jit(solution)/shard_map/all_to_all | solution.py:485
  13.3 1.8 %collective-permute-start.2 = (s32[8,128]{1,0:T(8,128)S(1)}, s32[8,128]{1,0:T(8,128)S(1)}, u32[]{:S(2)}, u32[]{:S(2)}) collective-permute-start(s32[8,128]{1,0:T(8,128)S(1)} %get-tuple-element.58.meta_s.meta_ref), channel_id=1, source_target_pairs={{0,1},{1,0},{2,3},{3,2},{4,5},{5,4},{6,7},{7,6},{8,9},{9,8},{10,11... | collective-permute-start | bytes 12296 | tf_op jit(solution)/shard_map/ppermute | solution.py:482
  40.4 4.5 %collective-permute-start.4 = (bf16[1024,384]{1,0:T(8,128)(2,1)S(1)}, bf16[1024,384]{1,0:T(8,128)(2,1)S(1)}, u32[]{:S(2)}, u32[]{:S(2)}) collective-permute-start(bf16[1024,384]{1,0:T(8,128)(2,1)S(1)} %normalise.3.done_ref), channel_id=1, source_target_pairs={{0,1},{1,0},{2,3},{3,2},{4,5},{5,4},{6,7},{7,6},{8,9},{9,8},{10,11... | collective-permute-start | bytes 2359304 | tf_op jit(solution)/shard_map/ppermute | solution.py:482
  44.1 2.0 %collective-permute-start.3 = (bf16[1024,256]{1,0:T(8,128)(2,1)S(1)}, bf16[1024,256]{1,0:T(8,128)(2,1)S(1)}, u32[]{:S(2)}, u32[]{:S(2)}) collective-permute-start(bf16[1024,256]{1,0:T(8,128)(2,1)S(1)} %get-tuple-element.59.refs_0_), channel_id=1, source_target_pairs={{0,1},{1,0},{2,3},{3,2},{4,5},{5,4},{6,7},{7,6},{8,9},{9,8},{10,11... | collective-permute-start | bytes 1572872 | tf_op jit(solution)/shard_map/ppermute | solution.py:482

commit v2 on v1

--- a/solution.py
+++ b/solution.py
@@ -213,7 +213,7 @@
     )(meta, cm, frames)
 
 
-def share_kernel(cap_blocks, rows, meta_ref, own_ref, theirs_ref, out_hbm, out_ref, sems):
+def share_kernel(cap_blocks, rows, meta_ref, own_ref, theirs_ref, out_ref):
     n, height, _ = out_ref.shape
     second = lax.axis_index("pix") != 0
     pixels = meta_ref[PIXELS : PIXELS + 1, 0:BLOCK]
@@ -225,22 +225,15 @@
         own, other = gate(jnp.logical_not(helps)), gate(helps)
         out_ref[q, 0:rows] = own_ref[q, 0:rows] * first
         out_ref[q, rows:] = own_ref[q, rows:] * own + theirs_ref[q, 0 : height - rows] * other
-        pltpu.make_async_copy(out_ref.at[q], out_hbm.at[q], sems.at[q]).start()
-    for q in range(n):
-        pltpu.make_async_copy(out_ref.at[q], out_hbm.at[q], sems.at[q]).wait()
 
 
 def share(meta, own, theirs, cap_blocks, rows):
     return call(
         functools.partial(share_kernel, cap_blocks, rows),
         "share",
-        pltpu.HBM(own.shape, own.dtype),
+        pltpu.VMEM(own.shape, own.dtype),
         in_specs=[WHOLE] * 3,
-        out_specs=ANYWHERE,
-        scratch_shapes=[
-            pltpu.VMEM(own.shape, own.dtype),
-            pltpu.SemaphoreType.DMA((own.shape[0],)),
-        ],
+        out_specs=WHOLE,
         bytes_accessed=4 * 1024 * 1024,
     )(meta, own, theirs)
 
@@ -251,8 +244,11 @@
     return theirs & (second | jnp.logical_not(mine)) & jnp.logical_not(fits)
 
 
-def rest_kernel(cap_blocks, meta_s, their_meta_s, frames_ref, cm_ref, out_ref):
+def rest_kernel(cap_blocks, meta_s, their_meta_s, frames_hbm, cm_hbm, out_ref, *scratch):
+    frames_ref, cm_ref = scratch
     n, _, rows, _ = out_ref.shape
+    pltpu.sync_copy(frames_hbm, frames_ref)
+    pltpu.sync_copy(cm_hbm, cm_ref)
     second = lax.axis_index("pix") != 0
     for q in range(n):
         counts = [[ref[row, q] for row in range(PIXELS + 1)] for ref in (meta_s, their_meta_s)]
@@ -271,9 +267,18 @@
         functools.partial(rest_kernel, cap_blocks),
         "pack_rest",
         jax.ShapeDtypeStruct((n, cap_blocks, frames.shape[0], BLOCK), frames.dtype),
-        in_specs=[pl.BlockSpec(memory_space=pltpu.SMEM)] * 2 + [WHOLE] * 2,
+        in_specs=[pl.BlockSpec(memory_space=pltpu.SMEM)] * 2 + [ANYWHERE] * 2,
         out_specs=WHOLE,
-    )(meta, their_meta, frames, cm)
+        scratch_shapes=[
+            pltpu.VMEM(frames.shape, frames.dtype),
+            pltpu.VMEM(cm.shape, cm.dtype),
+        ],
+    )(
+        meta,
+        their_meta,
+        pltpu.with_memory_space_constraint(frames, pltpu.HBM),
+        pltpu.with_memory_space_constraint(cm, pltpu.HBM),
+    )
 
 
 def lay_out(raw_ref, rows, first, padded):
@@ -317,16 +322,16 @@
         )
 
 
-def norm_kernel(rows, raw_ref, *refs):
+def norm_kernel(rows, first, raw_ref, *refs):
     out_ref, padded = refs[-2:]
-    lay_out(raw_ref, rows, 0, padded)
+    lay_out(raw_ref, rows, first, padded)
     for start in range(0, out_ref.shape[0], CHUNK):
         norm_rows(padded, start, CHUNK, out_ref)
 
 
-def normalise(raw, total, slots, after=()):
-    return call(
-        functools.partial(norm_kernel, total // raw.shape[0]),
+def normalise(raw, total, first, slots, after=()):
+    return call(
+        functools.partial(norm_kernel, total // raw.shape[0], first),
         "normalise",
         jax.ShapeDtypeStruct((total, slots * BLOCK), jnp.bfloat16),
         flops=12 * total * slots * BLOCK,
@@ -387,39 +392,6 @@
         out_specs=[WHOLE] * 2,
         scratch_shapes=[pltpu.VMEM((rows + ONES, x.shape[1]), x.dtype) for x in normed],
     )(*normed, *before)
-
-
-def norm_sums_kernel(rows, first, raw_ref, done_ref, out_ref, gram_out, frame_out, padded, left_ref):
-    total = out_ref.shape[0]
-    tiles = total // TILE
-    lay_out(raw_ref, rows, first, padded)
-    set_left(done_ref, left_ref)
-    for i in range(tiles):
-        column = slice(i * TILE, (i + 1) * TILE)
-        gram_out[:, column], frame_out[:, column] = add_sums(
-            [(left_ref, done_ref)], [0.0, 0.0], column
-        )
-        for start in range(i * TILE, (i + 1) * TILE, CHUNK):
-            norm_rows(padded, start, CHUNK, out_ref)
-
-
-def normalise_and_sum(raw, done, slots, parts):
-    total, width = done.shape
-    first = width // BLOCK
-    return call(
-        functools.partial(norm_sums_kernel, total // raw.shape[0], first),
-        "normalise_and_sum",
-        [jax.ShapeDtypeStruct((total, (slots - first) * BLOCK), jnp.bfloat16)]
-        + sums_shape(total, parts),
-        flops=2 * total // parts * total * width,
-        bytes_accessed=4 * total * total // parts,
-        in_specs=[WHOLE] * 2,
-        out_specs=[WHOLE] * 3,
-        scratch_shapes=[
-            pltpu.VMEM((slots - first, total + 2 * PAD, BLOCK), jnp.float32),
-            pltpu.VMEM((total // parts + ONES, width), jnp.bfloat16),
-        ],
-    )(raw, done)
 
 
 def result_kernel(meta_ref, their_meta_ref, normed_ref, gram_in, frame_in, out_hbm, *scratch):
@@ -496,16 +468,16 @@
     spills |= left_out(their_meta[:, :n], meta[:, :n], cap_blocks * BLOCK, jnp.logical_not(second))
     overflow = jnp.any(spills)
 
-    first = normalise(received, total, early, [overflow.astype(jnp.int32).reshape(1)])
+    first = normalise(received, total, 0, early, [overflow.astype(jnp.int32).reshape(1)])
     their_first = swap(first)
-    last, *sums = normalise_and_sum(received, first, slots, parts)
+    last = normalise(received, total, early, slots - early, [first])
     their_last = swap(last)
-    sums = partial_sums([last], sums, parts)
+    sums = partial_sums([first, last], [], parts)
     sums = partial_sums([their_first], sums, parts)
 
     def spill(frames, cm, meta, their_meta, their_last, *sums):
         rest = send(pack_rest(meta, their_meta, frames, cm, cap_blocks))
-        normed = normalise(rest.reshape(n, cap_blocks * rows, BLOCK), total, cap_blocks)
+        normed = normalise(rest.reshape(n, cap_blocks * rows, BLOCK), total, 0, cap_blocks)
         sums = partial_sums([normed, swap(normed)], sums, parts)
         return correlate([meta, their_meta], their_last, sums)
 

time: 48.7 us -> 48.3 us (level)
    pallas_call x3, Pallas kernels: 3.16 us -> 2.56 us  [the longest x1 1.44 us: share(): call(functools.partial(share_kernel, cap_blocks, rows), 'share', pltpu.VM...]
    pallas_call x2, Pallas kernels: 1.25 us -> 1.81 us  [partial_sums(): call(functools.partial(partial_kernel, len(normed)), 'partial_sums', sums...]
  transfers between devices with their start and end apart: 5 -> 5, of which waited for: 5 -> 4; matrix products, arithmetic and copies ran while one was open for 1% -> 1% of each run, Pallas kernels for 9% -> 9%
where the time goes in v2:
time: 48.3 us; the launch traced here: 47.4 us
  waiting for transfers between devices  24.9 us (52%)
  starting transfers between devices  10.9 us (23%)
  Pallas kernels  10.2 us (21%)
  between operations  0.71 us (1%)
  other arithmetic  0.64 us (1%)
    all_to_all x1, waiting for transfers between devices, send(): lax.all_to_all(blocks, 'frame', split_axis=0, concat_axis=0, tiled=True)  23.4 us
    all_to_all x1, starting transfers between devices, send(): lax.all_to_all(blocks, 'frame', split_axis=0, concat_axis=0, tiled=True)  6.64 us
    ppermute x4, starting transfers between devices, swap(): return lax.ppermute(x, 'pix', SWAP)  4.31 us
    pallas_call x1, Pallas kernels, pack_move(): call(functools.partial(move_kernel, cap_blocks), 'pack_move', [jax.ShapeD...  2.3 us
    pallas_call x2, Pallas kernels, partial_sums(): call(functools.partial(partial_kernel, len(normed)), 'partial_sums', sums...  1.81 us
    pallas_call x1, Pallas kernels, pack_own(): call(functools.partial(own_kernel, cap_blocks), 'pack_own', jax.ShapeDtyp...  1.8 us
    pallas_call x1, Pallas kernels, correlate(): call(result_kernel, 'correlate', pltpu.HBM((1, rows, total), jnp.bfloat16...  1.75 us
    ppermute x4, waiting for transfers between devices, swap(): return lax.ppermute(x, 'pix', SWAP)  1.51 us
  transfers between devices with their start and end apart: 5, of which 4 were waited for; matrix products, arithmetic and copies ran while one was open for 1% of the time, Pallas kernels for 9%

profile of v2, /device:TPU:11, one launch (start us, length us, event | category | flops | bytes accessed | tf_op | source)
XLA Modules:
  0.0 47.4 jit_solution(13233168958282090380)
XLA Ops:
  0.0 0.0 copy-start
  0.0 0.0 copy-start.2
  0.0 2.3 %pack_move.1 = (bf16[16,240,128]{2,1,0:T(8,128)(2,1)S(1)}, s32[8,128]{1,0:T(8,128)S(1)}) custom-call(s32[128,128]{1,0:T(8,128)} %bitcast.32, bf16[64,16384]{1,0:T(8,128)(2,1)} %frames_ref.1), custom_call_target="tpu_custom_call" | custom-call | tf_op jit(solution)/shard_map/pack_move/pallas_call | solution.py:157
  2.3 0.7 %collective-permute-start.1 = (bf16[16,240,128]{2,1,0:T(8,128)(2,1)S(1)}, bf16[16,240,128]{2,1,0:T(8,128)(2,1)S(1)}, u32[]{:S(2)}, u32[]{:S(2)}) collective-permute-start(bf16[16,240,128]{2,1,0:T(8,128)(2,1)S(1)} %get-tuple-element.54), channel_id=1, source_target_pairs={{0,1},{1,0},{2,3},{3,2},{4,5},{5,4},{6,7},{7,6},{8,9},{9,8},{10,11... | collective-permute-start | bytes 2949128 | tf_op jit(solution)/shard_map/ppermute | solution.py:454
  3.0 0.0 copy-done
  3.1 0.0 copy-done.2
  3.1 1.8 %pack_own.1.own_ref = bf16[16,288,128]{2,1,0:T(8,128)(2,1)S(1)} custom-call(s32[8,128]{1,0:T(8,128)S(1)} %get-tuple-element.55.meta_s.meta_ref, s32[128,128]{1,0:T(8,128)S(1)} %bitcast.33, bf16[64,16384]{1,0:T(8,128)(2,1)S(1)} %copy-done), custom_call_target="tpu_custom_call" | custom-call | bytes 4194304 | tf_op jit(solution)/shard_map/pack_own/pallas_call | solution.py:205
  4.9 0.4 collective-permute-done.1.theirs_ref
  5.2 1.4 %share.1 = bf16[16,288,128]{2,1,0:T(8,128)(2,1)} custom-call(s32[8,128]{1,0:T(8,128)S(1)} %get-tuple-element.55.meta_s.meta_ref, bf16[16,288,128]{2,1,0:T(8,128)(2,1)S(1)} %pack_own.1.own_ref, bf16[16,240,128]{2,1,0:T(8,128)(2,1)S(1)} %collective-permute-done.1.theirs_ref), custom_call_target="tpu_custom_call" | custom-call | bytes 4194304 | tf_op jit(solution)/shard_map/share/pallas_call | solution.py:231
  6.7 6.6 %all-to-all-start.1 = ((bf16[16,288,128]{2,1,0:T(8,128)(2,1)}), bf16[16,288,128]{2,1,0:T(8,128)(2,1)S(1)}, u32[]{:S(2)}, u32[]{:S(2)}) async-start(bf16[16,288,128]{2,1,0:T(8,128)(2,1)} %share.1), calls=%async_computation.1 | async-start | bytes 2359296 | tf_op jit(solution)/shard_map/all_to_all | solution.py:457
  13.3 0.9 %collective-permute-start.2 = (s32[8,128]{1,0:T(8,128)S(1)}, s32[8,128]{1,0:T(8,128)S(1)}, u32[]{:S(2)}, u32[]{:S(2)}) collective-permute-start(s32[8,128]{1,0:T(8,128)S(1)} %get-tuple-element.55.meta_s.meta_ref), channel_id=1, source_target_pairs={{0,1},{1,0},{2,3},{3,2},{4,5},{5,4},{6,7},{7,6},{8,9},{9,8},{10,11... | collective-permute-start | bytes 12296 | tf_op jit(solution)/shard_map/ppermute | solution.py:454
  14.3 0.8 %collective-permute-done.2 = s32[8,128]{1,0:T(8,128)S(1)} collective-permute-done((s32[8,128]{1,0:T(8,128)S(1)}, s32[8,128]{1,0:T(8,128)S(1)}, u32[]{:S(2)}, u32[]{:S(2)}) %collective-permute-start.2) | collective-permute-done | bytes 4128 | tf_op jit(solution)/shard_map/ppermute | solution.py:454
  15.1 0.6 %fusion.1 = pred[]{:T(512)} fusion(pred[]{:T(512)S(6)} %not.24, pred[]{:T(512)S(6)} %ne.3, s32[8,128]{1,0:T(8,128)S(1)} %collective-permute-done.2, s32[8,128]{1,0:T(8,128)S(1)} %get-tuple-element.55.meta_s.meta_ref), kind=kLoop, calls=%fused_computation.2 | loop fusion | flops 319 | bytes 259 | tf_op jit(solution)/shard_map/reduce_or | solution.py:469
  16.4 23.4 %all-to-all-done.1.raw_ref = bf16[16,288,128]{2,1,0:T(8,128)(2,1)S(1)} async-done(((bf16[16,288,128]{2,1,0:T(8,128)(2,1)}), bf16[16,288,128]{2,1,0:T(8,128)(2,1)S(1)}, u32[]{:S(2)}, u32[]{:S(2)}) %all-to-all-start.1) | async-done | bytes 1179680 | tf_op jit(solution)/shard_map/all_to_all | solution.py:457
  39.7 0.6 %normalise.4.refs_0_ = bf16[1024,384]{1,0:T(8,128)(2,1)S(1)} custom-call(bf16[16,288,128]{2,1,0:T(8,128)(2,1)S(1)} %all-to-all-done.1.raw_ref, s32[1]{0:T(128)} %bitcast.6.refs_0_), custom_call_target="tpu_custom_call" | custom-call | flops 4718592 | bytes 1572864 | tf_op jit(solution)/shard_map/normalise/pallas_call | solution.py:333
  40.4 2.6 %collective-permute-start.4 = (bf16[1024,384]{1,0:T(8,128)(2,1)S(1)}, bf16[1024,384]{1,0:T(8,128)(2,1)S(1)}, u32[]{:S(2)}, u32[]{:S(2)}) collective-permute-start(bf16[1024,384]{1,0:T(8,128)(2,1)S(1)} %normalise.4.refs_0_), channel_id=1, source_target_pairs={{0,1},{1,0},{2,3},{3,2},{4,5},{5,4},{6,7},{7,6},{8,9},{9,8},{10,11... | collective-permute-start | bytes 2359304 | tf_op jit(solution)/shard_map/ppermute | solution.py:454
  42.9 0.5 %normalise.5.refs_1_ = bf16[1024,256]{1,0:T(8,128)(2,1)S(1)} custom-call(bf16[16,288,128]{2,1,0:T(8,128)(2,1)S(1)} %all-to-all-done.1.raw_ref, bf16[1024,384]{1,0:T(8,128)(2,1)S(1)} %normalise.4.refs_0_), custom_call_target="tpu_custom_call" | custom-call | flops 3145728 | bytes 1048576 | tf_op jit(solution)/shard_map/normalise/pallas_call | solution.py:333
  43.4 0.1 collective-permute-start.3
  43.5 1.0 %partial_sums.4 = (f32[512,1024]{1,0:T(8,128)S(1)}, f32[8,1024]{1,0:T(8,128)S(1)}) custom-call(bf16[1024,384]{1,0:T(8,128)(2,1)S(1)} %normalise.4.refs_0_, bf16[1024,256]{1,0:T(8,128)(2,1)S(1)} %normalise.5.refs_1_), custom_call_target="tpu_custom_call" | custom-call | flops 805306368 | bytes 2097152 | tf_op jit(solution)/shard_map/partial_sums/pallas_call | solution.py:385
  44.6 0.3 collective-permute-done.4.refs_0_
  44.9 0.8 %partial_sums.5 = (f32[512,1024]{1,0:T(8,128)S(1)}, f32[8,1024]{1,0:T(8,128)S(1)}) custom-call(bf16[1024,384]{1,0:T(8,128)(2,1)S(1)} %collective-permute-done.4.refs_0_, f32[512,1024]{1,0:T(8,128)S(1)} %get-tuple-element.56.refs_1_, f32[8,1024]{1,0:T(8,128)S(1)} %get-tuple-element.57.refs_2_), custom_call_target="tpu_custom_call" | custom-call | flops 402653184 | bytes 2097152 | tf_op jit(solution)/shard_map/partial_sums/pallas_call | solution.py:385
  45.6 0.0 collective-permute-done.3
  45.6 1.8 %conditional.1 = (bf16[1,512,1024]{2,1,0:T(8,128)(2,1)}) conditional(s32[]{:T(128)} %convert_element_type.4, (s32[8,128]{1,0:T(8,128)S(1)}, s32[8,128]{1,0:T(8,128)S(1)}, bf16[1024,256]{1,0:T(8,128)(2,1)S(1)}, f32[512,1024]{1,0:T(8,128)S(1)}, f32[8,1024]{1,0:T(8,128)S(1)}) %tuple.13, (s32[8,128]{1,0:T(8,128)S(1)}, s32[8,128]{1,0:T(8,128)S(1)}, ...), branch_computations={%region_1.0_spmd, %region_2.0_spmd} | conditional | flops 2428502016 | bytes 30670952 | solution.py:487
  45.7 1.7 %correlate.2 = bf16[1,512,1024]{2,1,0:T(8,128)(2,1)} custom-call(s32[8,128]{1,0:T(8,128)S(1)} %get-tuple-element.32.meta_ref, s32[8,128]{1,0:T(8,128)S(1)} %get-tuple-element.33.their_meta_ref, bf16[1024,256]{1,0:T(8,128)(2,1)S(1)} %get-tuple-element.34.normed_ref, f32[512,1024]{1,0:T(8,128)S(1)} %get-tuple-element.35.gram_in, ...), custom_call_target="tpu_custom_call" | custom-call | flops 268435456 | bytes 3145728 | tf_op jit(solution)/shard_map/cond/branch_0_fun/correlate/pallas_call | solution.py:427
Async XLA Ops:
  0.0 3.0 %copy-start = (bf16[64,16384]{1,0:T(8,128)(2,1)S(1)}, bf16[64,16384]{1,0:T(8,128)(2,1)}, u32[]{:S(2)}) copy-start(bf16[64,16384]{1,0:T(8,128)(2,1)} %frames_ref.1) | copy-start | bytes 6291460
  0.0 3.0 %copy-start.2 = (s32[16384]{0:T(1024)S(1)}, s32[16384]{0:T(1024)}, u32[]{:S(2)}) copy-start(s32[16384]{0:T(1024)} %param.5) | copy-start | bytes 196612
  2.3 2.9 %collective-permute-start.1 = (bf16[16,240,128]{2,1,0:T(8,128)(2,1)S(1)}, bf16[16,240,128]{2,1,0:T(8,128)(2,1)S(1)}, u32[]{:S(2)}, u32[]{:S(2)}) collective-permute-start(bf16[16,240,128]{2,1,0:T(8,128)(2,1)S(1)} %get-tuple-element.54), channel_id=1, source_target_pairs={{0,1},{1,0},{2,3},{3,2},{4,5},{5,4},{6,7},{7,6},{8,9},{9,8},{10,11... | collective-permute-start | bytes 2949128 | tf_op jit(solution)/shard_map/ppermute | solution.py:454
  6.7 33.1 %all-to-all-start.1 = ((bf16[16,288,128]{2,1,0:T(8,128)(2,1)}), bf16[16,288,128]{2,1,0:T(8,128)(2,1)S(1)}, u32[]{:S(2)}, u32[]{:S(2)}) async-start(bf16[16,288,128]{2,1,0:T(8,128)(2,1)} %share.1), calls=%async_computation.1 | async-start | bytes 2359296 | tf_op jit(solution)/shard_map/all_to_all | solution.py:457
  13.3 1.8 %collective-permute-start.2 = (s32[8,128]{1,0:T(8,128)S(1)}, s32[8,128]{1,0:T(8,128)S(1)}, u32[]{:S(2)}, u32[]{:S(2)}) collective-permute-start(s32[8,128]{1,0:T(8,128)S(1)} %get-tuple-element.55.meta_s.meta_ref), channel_id=1, source_target_pairs={{0,1},{1,0},{2,3},{3,2},{4,5},{5,4},{6,7},{7,6},{8,9},{9,8},{10,11... | collective-permute-start | bytes 12296 | tf_op jit(solution)/shard_map/ppermute | solution.py:454
  40.4 4.5 %collective-permute-start.4 = (bf16[1024,384]{1,0:T(8,128)(2,1)S(1)}, bf16[1024,384]{1,0:T(8,128)(2,1)S(1)}, u32[]{:S(2)}, u32[]{:S(2)}) collective-permute-start(bf16[1024,384]{1,0:T(8,128)(2,1)S(1)} %normalise.4.refs_0_), channel_id=1, source_target_pairs={{0,1},{1,0},{2,3},{3,2},{4,5},{5,4},{6,7},{7,6},{8,9},{9,8},{10,11... | collective-permute-start | bytes 2359304 | tf_op jit(solution)/shard_map/ppermute | solution.py:454
  43.4 2.2 %collective-permute-start.3 = (bf16[1024,256]{1,0:T(8,128)(2,1)S(1)}, bf16[1024,256]{1,0:T(8,128)(2,1)S(1)}, u32[]{:S(2)}, u32[]{:S(2)}) collective-permute-start(bf16[1024,256]{1,0:T(8,128)(2,1)S(1)} %normalise.5.refs_1_), channel_id=1, source_target_pairs={{0,1},{1,0},{2,3},{3,2},{4,5},{5,4},{6,7},{7,6},{8,9},{9,8},{10,11... | collective-permute-start | bytes 1572872 | tf_op jit(solution)/shard_map/ppermute | solution.py:454

commit v3 on v2

--- a/solution.py
+++ b/solution.py
@@ -36,6 +36,11 @@
 
 def dot_nt(a, b):
     return lax.dot_general(a, b, (((1,), (1,)), ((), ())), preferred_element_type=jnp.float32)
+
+
+def place(i, n):
+    quarter = n // 4
+    return i % quarter * 4 + i // quarter
 
 
 def count_half_rows(rows):
@@ -68,9 +73,13 @@
 
 def unfold(folded, rows):
     half = BLOCK // 2
-    early = folded[0 : rows // 2].astype(jnp.float32)
-    left = lax.broadcasted_iota(jnp.int32, early.shape, 1) < half
-    return jnp.where(left, early, 0.0), jnp.where(left, pltpu.roll(early, half, 1), 0.0)
+    folded = folded[0 : rows // 2].astype(jnp.float32)
+    turned = pltpu.roll(folded, half, 1)
+    second = lax.axis_index("pix") != 0
+    left = lax.broadcasted_iota(jnp.int32, folded.shape, 1) < half
+    used = left != second
+    early, late = jnp.where(second, turned, folded), jnp.where(second, folded, turned)
+    return jnp.where(used, early, 0.0), jnp.where(used, late, 0.0)
 
 
 def find_members(cm):
@@ -223,8 +232,9 @@
         helps = theirs & (second | jnp.logical_not(mine))
         first = gate(jnp.logical_not(helps & mine))
         own, other = gate(jnp.logical_not(helps)), gate(helps)
-        out_ref[q, 0:rows] = own_ref[q, 0:rows] * first
-        out_ref[q, rows:] = own_ref[q, rows:] * own + theirs_ref[q, 0 : height - rows] * other
+        to = place(q, n)
+        out_ref[to, 0:rows] = own_ref[q, 0:rows] * first
+        out_ref[to, rows:] = own_ref[q, rows:] * own + theirs_ref[q, 0 : height - rows] * other
 
 
 def share(meta, own, theirs, cap_blocks, rows):
@@ -256,7 +266,7 @@
         for i in range(cap_blocks):
             block = meta_s[LIST, q * cap_blocks + i]
             valid = cm_ref[pl.ds(block, 1), :] >= 0
-            out_ref[q, i] = take(frames_ref, block) * gate(
+            out_ref[place(q, n), i] = take(frames_ref, block) * gate(
                 valid & wanted & (i < meta_s[COUNT, q])
             )
 
@@ -292,10 +302,10 @@
         for source in range(n):
             start = PAD + source * rows
             if (slot + 1) * rows <= height:
-                block = raw_ref[source, slot * rows : (slot + 1) * rows]
+                block = raw_ref[place(source, n), slot * rows : (slot + 1) * rows]
                 padded[i, start : start + rows] = block.astype(jnp.float32)
             else:
-                early, late = unfold(raw_ref[source, slot * rows : height], rows)
+                early, late = unfold(raw_ref[place(source, n), slot * rows : height], rows)
                 padded[i, start : start + rows // 2] = early
                 padded[i, start + rows // 2 : start + rows] = late
 
@@ -343,17 +353,17 @@
 
 
 def set_left(ref, left_ref):
-    rows = left_ref.shape[0] - ONES
+    rows, width = left_ref.shape[0] - ONES, left_ref.shape[1]
     first_row = pl.multiple_of(lax.axis_index("pix") * rows, rows)
-    left_ref[0:rows] = ref[pl.ds(first_row, rows), :]
-    left_ref[rows : rows + ONES] = jnp.ones((ONES, ref.shape[1]), jnp.bfloat16)
+    left_ref[0:rows] = ref[pl.ds(first_row, rows), 0:width]
+    left_ref[rows : rows + ONES] = jnp.ones((ONES, width), jnp.bfloat16)
 
 
 def add_sums(pairs, sums, column):
     gram, frame = sums
     rows = pairs[0][0].shape[0] - ONES
     for left_ref, ref in pairs:
-        both = dot_nt(left_ref[...], ref[column, :])
+        both = dot_nt(left_ref[...], ref[column, 0 : left_ref.shape[1]])
         gram = gram + both[0:rows]
         frame = frame + both[rows : rows + 8]
     return gram, frame
@@ -379,23 +389,27 @@
     ]
 
 
-def partial_sums(normed, before, parts):
-    total, width = normed[0].shape
+def partial_sums(normed, before, parts, widths=None):
+    widths = widths or [x.shape[1] for x in normed]
+    total = normed[0].shape[0]
     rows = total // parts
     return call(
         functools.partial(partial_kernel, len(normed)),
         "partial_sums",
         sums_shape(total, parts),
-        flops=2 * rows * total * width * len(normed),
+        flops=2 * rows * total * sum(widths),
         bytes_accessed=4 * rows * total,
         in_specs=[WHOLE] * (len(normed) + len(before)),
         out_specs=[WHOLE] * 2,
-        scratch_shapes=[pltpu.VMEM((rows + ONES, x.shape[1]), x.dtype) for x in normed],
+        scratch_shapes=[pltpu.VMEM((rows + ONES, width), jnp.bfloat16) for width in widths],
     )(*normed, *before)
 
 
-def result_kernel(meta_ref, their_meta_ref, normed_ref, gram_in, frame_in, out_hbm, *scratch):
-    out_ref, frame_ref, sems = scratch
+def result_kernel(meta_ref, their_meta_ref, mine_ref, theirs_ref, gram_in, frame_in, *refs):
+    out_hbm, out_ref, frame_ref, normed_ref, sems = refs
+    last = slice(mine_ref.shape[1] - BLOCK, mine_ref.shape[1])
+    normed_ref[:, 0 : last.start] = theirs_ref[:, 0 : last.start]
+    normed_ref[:, last] = theirs_ref[:, last] + mine_ref[:, last]
     rows, total = gram_in.shape
     pixels = meta_ref[PIXELS : PIXELS + 1, 0:BLOCK] + their_meta_ref[PIXELS : PIXELS + 1, 0:BLOCK]
     own = lax.broadcasted_iota(jnp.int32, (1, BLOCK), 1) == lax.axis_index("frame")
@@ -421,23 +435,24 @@
         copy.wait()
 
 
-def correlate(metas, normed, before):
+def correlate(metas, mine, theirs, before):
     rows, total = before[0].shape
     tiles = total // TILE
     return call(
         result_kernel,
         "correlate",
         pltpu.HBM((1, rows, total), jnp.bfloat16),
-        flops=2 * rows * total * normed.shape[1],
+        flops=2 * rows * total * theirs.shape[1],
         bytes_accessed=6 * rows * total,
-        in_specs=[WHOLE] * 5,
+        in_specs=[WHOLE] * 6,
         out_specs=ANYWHERE,
         scratch_shapes=[
             pltpu.VMEM((tiles, rows, TILE), jnp.bfloat16),
             pltpu.VMEM((8, total), jnp.float32),
+            pltpu.VMEM(theirs.shape, theirs.dtype),
             pltpu.SemaphoreType.DMA((tiles,)),
         ],
-    )(*metas, normed, *before)
+    )(*metas, mine, theirs, *before)
 
 
 def body(frames, cycle_map):
@@ -454,7 +469,10 @@
         return lax.ppermute(x, "pix", SWAP)
 
     def send(blocks):
-        return lax.all_to_all(blocks, "frame", split_axis=0, concat_axis=0, tiled=True)
+        group = sorted(range(n), key=lambda i: place(i, n))
+        return lax.all_to_all(
+            blocks, "frame", split_axis=0, concat_axis=0, axis_index_groups=[group], tiled=True
+        )
 
     moving, meta = pack_move(cm, frames, cap_blocks)
     theirs = swap(moving)
@@ -472,19 +490,21 @@
     their_first = swap(first)
     last = normalise(received, total, early, slots - early, [first])
     their_last = swap(last)
-    sums = partial_sums([first, last], [], parts)
+    widths = [early * BLOCK, (slots - early - 1) * BLOCK]
+    sums = partial_sums([first, last], [], parts, widths)
     sums = partial_sums([their_first], sums, parts)
 
-    def spill(frames, cm, meta, their_meta, their_last, *sums):
+    def spill(frames, cm, meta, their_meta, last, their_last, *sums):
         rest = send(pack_rest(meta, their_meta, frames, cm, cap_blocks))
         normed = normalise(rest.reshape(n, cap_blocks * rows, BLOCK), total, 0, cap_blocks)
         sums = partial_sums([normed, swap(normed)], sums, parts)
-        return correlate([meta, their_meta], their_last, sums)
-
-    def fits(frames, cm, meta, their_meta, their_last, *sums):
-        return correlate([meta, their_meta], their_last, sums)
-
-    return lax.cond(overflow, spill, fits, frames, cm, meta, their_meta, their_last, *sums)
+        return correlate([meta, their_meta], last, their_last, sums)
+
+    def fits(frames, cm, meta, their_meta, last, their_last, *sums):
+        return correlate([meta, their_meta], last, their_last, sums)
+
+    operands = frames, cm, meta, their_meta, last, their_last, *sums
+    return lax.cond(overflow, spill, fits, *operands)
 
 
 def solution(mesh):

time: 48.3 us -> 51.1 us (1.058)
  the two profiles are of different devices: /device:TPU:11 before, /device:TPU:0 now
where the time goes in v3:
time: 51.1 us; the launch traced here: 50.9 us
  waiting for transfers between devices  29.7 us (58%)
  Pallas kernels  10.3 us (20%)
  starting transfers between devices  9.45 us (18%)
  between operations  0.73 us (1%)
  other arithmetic  0.64 us (1%)
    all_to_all x1, waiting for transfers between devices, send(): lax.all_to_all(blocks, 'frame', split_axis=0, concat_axis=0, axis_index_g...  28.1 us
    all_to_all x1, starting transfers between devices, send(): lax.all_to_all(blocks, 'frame', split_axis=0, concat_axis=0, axis_index_g...  8.24 us
    pallas_call x1, Pallas kernels, pack_move(): call(functools.partial(move_kernel, cap_blocks), 'pack_move', [jax.ShapeD...  2.3 us
    pallas_call x2, Pallas kernels, partial_sums(): call(functools.partial(partial_kernel, len(normed)), 'partial_sums', sums...  1.81 us
    pallas_call x1, Pallas kernels, pack_own(): call(functools.partial(own_kernel, cap_blocks), 'pack_own', jax.ShapeDtyp...  1.8 us
    pallas_call x1, Pallas kernels, correlate(): call(result_kernel, 'correlate', pltpu.HBM((1, rows, total), jnp.bfloat16...  1.77 us
    ppermute x4, waiting for transfers between devices, swap(): return lax.ppermute(x, 'pix', SWAP)  1.67 us
    pallas_call x1, Pallas kernels, share(): call(functools.partial(share_kernel, cap_blocks, rows), 'share', pltpu.VM...  1.44 us
  transfers between devices with their start and end apart: 5, of which 4 were waited for; matrix products, arithmetic and copies ran while one was open for 1% of the time, Pallas kernels for 8%

profile of v3, /device:TPU:0, one launch (start us, length us, event | category | flops | bytes accessed | tf_op | source)
XLA Modules:
  0.0 50.9 jit_solution(18225069806462969024)
XLA Ops:
  0.0 0.0 copy-start
  0.0 0.0 copy-start.2
  0.0 2.3 %pack_move.1 = (bf16[16,240,128]{2,1,0:T(8,128)(2,1)S(1)}, s32[8,128]{1,0:T(8,128)S(1)}) custom-call(s32[128,128]{1,0:T(8,128)} %bitcast.32, bf16[64,16384]{1,0:T(8,128)(2,1)} %frames_ref.1), custom_call_target="tpu_custom_call" | custom-call | tf_op jit(solution)/shard_map/pack_move/pallas_call | solution.py:166
  2.3 0.5 %collective-permute-start.1 = (bf16[16,240,128]{2,1,0:T(8,128)(2,1)S(1)}, bf16[16,240,128]{2,1,0:T(8,128)(2,1)S(1)}, u32[]{:S(2)}, u32[]{:S(2)}) collective-permute-start(bf16[16,240,128]{2,1,0:T(8,128)(2,1)S(1)} %get-tuple-element.60), channel_id=1, source_target_pairs={{0,1},{1,0},{2,3},{3,2},{4,5},{5,4},{6,7},{7,6},{8,9},{9,8},{10,11... | collective-permute-start | bytes 2949128 | tf_op jit(solution)/shard_map/ppermute | solution.py:469
  2.8 0.0 copy-done
  2.8 0.0 copy-done.2
  2.8 1.8 %pack_own.1.own_ref = bf16[16,288,128]{2,1,0:T(8,128)(2,1)S(1)} custom-call(s32[8,128]{1,0:T(8,128)S(1)} %get-tuple-element.61.meta_s.meta_ref, s32[128,128]{1,0:T(8,128)S(1)} %bitcast.33, bf16[64,16384]{1,0:T(8,128)(2,1)S(1)} %copy-done), custom_call_target="tpu_custom_call" | custom-call | bytes 4194304 | tf_op jit(solution)/shard_map/pack_own/pallas_call | solution.py:214
  4.6 0.4 collective-permute-done.1.theirs_ref
  5.0 1.4 %share.1 = bf16[16,288,128]{2,1,0:T(8,128)(2,1)} custom-call(s32[8,128]{1,0:T(8,128)S(1)} %get-tuple-element.61.meta_s.meta_ref, bf16[16,288,128]{2,1,0:T(8,128)(2,1)S(1)} %pack_own.1.own_ref, bf16[16,240,128]{2,1,0:T(8,128)(2,1)S(1)} %collective-permute-done.1.theirs_ref), custom_call_target="tpu_custom_call" | custom-call | bytes 4194304 | tf_op jit(solution)/shard_map/share/pallas_call | solution.py:241
  6.5 8.2 %all-to-all-start.1 = ((bf16[16,288,128]{2,1,0:T(8,128)(2,1)}), bf16[16,288,128]{2,1,0:T(8,128)(2,1)S(1)}, u32[]{:S(2)}, u32[]{:S(2)}) async-start(bf16[16,288,128]{2,1,0:T(8,128)(2,1)} %share.1), calls=%async_computation.1 | async-start | bytes 2359296 | tf_op jit(solution)/shard_map/all_to_all | solution.py:473
  14.7 0.1 collective-permute-start.2
  14.8 1.1 %collective-permute-done.2 = s32[8,128]{1,0:T(8,128)S(1)} collective-permute-done((s32[8,128]{1,0:T(8,128)S(1)}, s32[8,128]{1,0:T(8,128)S(1)}, u32[]{:S(2)}, u32[]{:S(2)}) %collective-permute-start.2) | collective-permute-done | bytes 4128 | tf_op jit(solution)/shard_map/ppermute | solution.py:469
  15.9 0.6 %fusion.1 = pred[]{:T(512)} fusion(pred[]{:T(512)S(6)} %not.24, pred[]{:T(512)S(6)} %ne.3, s32[8,128]{1,0:T(8,128)S(1)} %collective-permute-done.2, s32[8,128]{1,0:T(8,128)S(1)} %get-tuple-element.61.meta_s.meta_ref), kind=kLoop, calls=%fused_computation.2 | loop fusion | flops 319 | bytes 259 | tf_op jit(solution)/shard_map/reduce_or | solution.py:487
  17.2 28.1 %all-to-all-done.1.raw_ref = bf16[16,288,128]{2,1,0:T(8,128)(2,1)S(1)} async-done(((bf16[16,288,128]{2,1,0:T(8,128)(2,1)}), bf16[16,288,128]{2,1,0:T(8,128)(2,1)S(1)}, u32[]{:S(2)}, u32[]{:S(2)}) %all-to-all-start.1) | async-done | bytes 1179680 | tf_op jit(solution)/shard_map/all_to_all | solution.py:473
  45.3 0.6 %normalise.4.refs_0_ = bf16[1024,384]{1,0:T(8,128)(2,1)S(1)} custom-call(bf16[16,288,128]{2,1,0:T(8,128)(2,1)S(1)} %all-to-all-done.1.raw_ref, s32[1]{0:T(128)} %bitcast.6.refs_0_), custom_call_target="tpu_custom_call" | custom-call | flops 4718592 | bytes 1572864 | tf_op jit(solution)/shard_map/normalise/pallas_call | solution.py:343
  45.9 0.1 collective-permute-start.4
  46.0 0.5 %normalise.5.refs_1_ = bf16[1024,256]{1,0:T(8,128)(2,1)S(1)} custom-call(bf16[16,288,128]{2,1,0:T(8,128)(2,1)S(1)} %all-to-all-done.1.raw_ref, bf16[1024,384]{1,0:T(8,128)(2,1)S(1)} %normalise.4.refs_0_), custom_call_target="tpu_custom_call" | custom-call | flops 3145728 | bytes 1048576 | tf_op jit(solution)/shard_map/normalise/pallas_call | solution.py:343
  46.5 0.6 %collective-permute-start.3 = (bf16[1024,256]{1,0:T(8,128)(2,1)S(1)}, bf16[1024,256]{1,0:T(8,128)(2,1)S(1)}, u32[]{:S(2)}, u32[]{:S(2)}) collective-permute-start(bf16[1024,256]{1,0:T(8,128)(2,1)S(1)} %normalise.5.refs_1_), channel_id=1, source_target_pairs={{0,1},{1,0},{2,3},{3,2},{4,5},{5,4},{6,7},{7,6},{8,9},{9,8},{10,11... | collective-permute-start | bytes 1572872 | tf_op jit(solution)/shard_map/ppermute | solution.py:469
  47.1 1.0 %partial_sums.4 = (f32[512,1024]{1,0:T(8,128)S(1)}, f32[8,1024]{1,0:T(8,128)S(1)}) custom-call(bf16[1024,384]{1,0:T(8,128)(2,1)S(1)} %normalise.4.refs_0_, bf16[1024,256]{1,0:T(8,128)(2,1)S(1)} %normalise.5.refs_1_), custom_call_target="tpu_custom_call" | custom-call | flops 536870912 | bytes 2097152 | tf_op jit(solution)/shard_map/partial_sums/pallas_call | solution.py:396
  48.1 0.1 collective-permute-done.4.refs_0_
  48.3 0.8 %partial_sums.5 = (f32[512,1024]{1,0:T(8,128)S(1)}, f32[8,1024]{1,0:T(8,128)S(1)}) custom-call(bf16[1024,384]{1,0:T(8,128)(2,1)S(1)} %collective-permute-done.4.refs_0_, f32[512,1024]{1,0:T(8,128)S(1)} %get-tuple-element.62.refs_1_, f32[8,1024]{1,0:T(8,128)S(1)} %get-tuple-element.63.refs_2_), custom_call_target="tpu_custom_call" | custom-call | flops 402653184 | bytes 2097152 | tf_op jit(solution)/shard_map/partial_sums/pallas_call | solution.py:396
  49.1 0.0 collective-permute-done.3
  49.1 1.8 %conditional.1 = (bf16[1,512,1024]{2,1,0:T(8,128)(2,1)}) conditional(s32[]{:T(128)} %convert_element_type.4, (s32[8,128]{1,0:T(8,128)S(1)}, s32[8,128]{1,0:T(8,128)S(1)}, bf16[1024,256]{1,0:T(8,128)(2,1)S(1)}, bf16[1024,256]{1,0:T(8,128)(2,1)S(1)}, f32[512,1024]{1,0:T(8,128)S(1)}, /*index=5*/f32[8,1024]{1,0:T(8,128)S(1)}) %tuple.13, ...), branch_computations={%region_1.0_spmd, %region_2.0_spmd} | conditional | flops 2428502016 | bytes 30670952 | solution.py:507
  49.1 1.8 %correlate.2 = bf16[1,512,1024]{2,1,0:T(8,128)(2,1)} custom-call(s32[8,128]{1,0:T(8,128)S(1)} %get-tuple-element.36.meta_ref, s32[8,128]{1,0:T(8,128)S(1)} %get-tuple-element.37.their_meta_ref, bf16[1024,256]{1,0:T(8,128)(2,1)S(1)} %get-tuple-element.38.mine_ref, bf16[1024,256]{1,0:T(8,128)(2,1)S(1)} %get-tuple-element.39.theirs_ref, ...), custom_call_target="tpu_custom_call" | custom-call | flops 268435456 | bytes 3145728 | tf_op jit(solution)/shard_map/cond/branch_0_fun/correlate/pallas_call | solution.py:441
Async XLA Ops:
  0.0 2.8 %copy-start = (bf16[64,16384]{1,0:T(8,128)(2,1)S(1)}, bf16[64,16384]{1,0:T(8,128)(2,1)}, u32[]{:S(2)}) copy-start(bf16[64,16384]{1,0:T(8,128)(2,1)} %frames_ref.1) | copy-start | bytes 6291460
  0.0 2.8 %copy-start.2 = (s32[16384]{0:T(1024)S(1)}, s32[16384]{0:T(1024)}, u32[]{:S(2)}) copy-start(s32[16384]{0:T(1024)} %param.5) | copy-start | bytes 196612
  2.3 2.7 %collective-permute-start.1 = (bf16[16,240,128]{2,1,0:T(8,128)(2,1)S(1)}, bf16[16,240,128]{2,1,0:T(8,128)(2,1)S(1)}, u32[]{:S(2)}, u32[]{:S(2)}) collective-permute-start(bf16[16,240,128]{2,1,0:T(8,128)(2,1)S(1)} %get-tuple-element.60), channel_id=1, source_target_pairs={{0,1},{1,0},{2,3},{3,2},{4,5},{5,4},{6,7},{7,6},{8,9},{9,8},{10,11... | collective-permute-start | bytes 2949128 | tf_op jit(solution)/shard_map/ppermute | solution.py:469
  6.5 38.8 %all-to-all-start.1 = ((bf16[16,288,128]{2,1,0:T(8,128)(2,1)}), bf16[16,288,128]{2,1,0:T(8,128)(2,1)S(1)}, u32[]{:S(2)}, u32[]{:S(2)}) async-start(bf16[16,288,128]{2,1,0:T(8,128)(2,1)} %share.1), calls=%async_computation.1 | async-start | bytes 2359296 | tf_op jit(solution)/shard_map/all_to_all | solution.py:473
  14.7 1.2 %collective-permute-start.2 = (s32[8,128]{1,0:T(8,128)S(1)}, s32[8,128]{1,0:T(8,128)S(1)}, u32[]{:S(2)}, u32[]{:S(2)}) collective-permute-start(s32[8,128]{1,0:T(8,128)S(1)} %get-tuple-element.61.meta_s.meta_ref), channel_id=1, source_target_pairs={{0,1},{1,0},{2,3},{3,2},{4,5},{5,4},{6,7},{7,6},{8,9},{9,8},{10,11... | collective-permute-start | bytes 12296 | tf_op jit(solution)/shard_map/ppermute | solution.py:469
  45.9 2.4 %collective-permute-start.4 = (bf16[1024,384]{1,0:T(8,128)(2,1)S(1)}, bf16[1024,384]{1,0:T(8,128)(2,1)S(1)}, u32[]{:S(2)}, u32[]{:S(2)}) collective-permute-start(bf16[1024,384]{1,0:T(8,128)(2,1)S(1)} %normalise.4.refs_0_), channel_id=1, source_target_pairs={{0,1},{1,0},{2,3},{3,2},{4,5},{5,4},{6,7},{7,6},{8,9},{9,8},{10,11... | collective-permute-start | bytes 2359304 | tf_op jit(solution)/shard_map/ppermute | solution.py:469
  46.5 2.5 %collective-permute-start.3 = (bf16[1024,256]{1,0:T(8,128)(2,1)S(1)}, bf16[1024,256]{1,0:T(8,128)(2,1)S(1)}, u32[]{:S(2)}, u32[]{:S(2)}) collective-permute-start(bf16[1024,256]{1,0:T(8,128)(2,1)S(1)} %normalise.5.refs_1_), channel_id=1, source_target_pairs={{0,1},{1,0},{2,3},{3,2},{4,5},{5,4},{6,7},{7,6},{8,9},{9,8},{10,11... | collective-permute-start | bytes 1572872 | tf_op jit(solution)/shard_map/ppermute | solution.py:469

commit v4 on v2

--- a/solution.py
+++ b/solution.py
@@ -16,6 +16,7 @@
 VMEM_BYTES = 32 * 1024 * 1024
 LIST, COUNT, PIXELS = 0, 1, 2
 MERGED = 2
+BITS = 16
 SWAP = [(0, 1), (1, 0)]
 WHOLE = pl.BlockSpec(memory_space=pltpu.VMEM)
 ANYWHERE = pl.BlockSpec(memory_space=pl.ANY)
@@ -137,22 +138,19 @@
     to_scalars.wait()
     get_frames.wait()
     for q in range(n):
-        full = gate(meta_s[PIXELS, q] == cap_blocks * BLOCK)
         for i in range(kept + 1, cap_blocks):
             block = meta_s[LIST, q * cap_blocks + i]
             start = (i - kept - 1) * rows
-            out_ref[q, start : start + rows] = take(frames_ref, block) * full
+            out_ref[q, start : start + rows] = take(frames_ref, block)
         start = (cap_blocks - kept - 1) * rows
-        end = start + count_half_rows(rows)
         block = meta_s[LIST, q * cap_blocks + kept]
-        out_ref[q, start:end] = fold(take(frames_ref, block), True) * full
-        out_ref[q, end : end + 16] = jnp.broadcast_to(full, (16, BLOCK))
+        out_ref[q, start:] = fold(take(frames_ref, block), True)
 
 
 def pack_move(cm, frames, cap_blocks):
     rows = frames.shape[0]
     n = cm.shape[0] // cap_blocks
-    height = (cap_blocks - cap_blocks // 2 - 1) * rows + count_half_rows(rows) + 16
+    height = (cap_blocks - cap_blocks // 2 - 1) * rows + count_half_rows(rows)
     meta = jax.ShapeDtypeStruct((8, cm.shape[0]), jnp.int32)
     return call(
         functools.partial(move_kernel, cap_blocks),
@@ -172,7 +170,7 @@
     )
 
 
-def own_kernel(cap_blocks, meta_s, cm_ref, frames_ref, out_ref, place_ref):
+def own_kernel(cap_blocks, meta_s, cm_ref, frames_ref, out_hbm, out_ref, place_ref, sems):
     n = out_ref.shape[0]
     rows = frames_ref.shape[0]
     kept = cap_blocks // 2
@@ -193,72 +191,95 @@
         out_ref[q, 0:rows] = compact.astype(jnp.bfloat16) + take(frames_ref, block) * full
         for i in range(1, kept):
             block = meta_s[LIST, q * cap_blocks + i]
-            out_ref[q, i * rows : (i + 1) * rows] = take(frames_ref, block) * full
+            out_ref[q, i * rows : (i + 1) * rows] = take(frames_ref, block)
         block = meta_s[LIST, q * cap_blocks + kept]
-        out_ref[q, kept * rows :] = fold(take(frames_ref, block), False) * full
+        out_ref[q, kept * rows :] = fold(take(frames_ref, block), False)
+        pltpu.make_async_copy(out_ref.at[q], out_hbm.at[q], sems.at[q]).start()
+    for q in range(n):
+        pltpu.make_async_copy(out_ref.at[q], out_hbm.at[q], sems.at[q]).wait()
 
 
 def pack_own(meta, cm, frames, cap_blocks):
     rows = frames.shape[0]
     n = cm.shape[0] // cap_blocks
-    height = cap_blocks // 2 * rows + count_half_rows(rows)
+    shape = (n, cap_blocks // 2 * rows + count_half_rows(rows), BLOCK)
     return call(
         functools.partial(own_kernel, cap_blocks),
         "pack_own",
-        jax.ShapeDtypeStruct((n, height, BLOCK), frames.dtype),
+        pltpu.HBM(shape, frames.dtype),
         in_specs=[pl.BlockSpec(memory_space=pltpu.SMEM)] + [WHOLE] * 2,
-        out_specs=WHOLE,
-        scratch_shapes=[pltpu.VMEM(cm.shape, jnp.float32)],
+        out_specs=ANYWHERE,
+        scratch_shapes=[
+            pltpu.VMEM(shape, frames.dtype),
+            pltpu.VMEM(cm.shape, jnp.float32),
+            pltpu.SemaphoreType.DMA((n,)),
+        ],
         bytes_accessed=4 * 1024 * 1024,
     )(meta, cm, frames)
 
 
-def share_kernel(cap_blocks, rows, meta_ref, own_ref, theirs_ref, out_ref):
-    n, height, _ = out_ref.shape
-    second = lax.axis_index("pix") != 0
-    pixels = meta_ref[PIXELS : PIXELS + 1, 0:BLOCK]
-    for q in range(n):
-        mine = jnp.broadcast_to(pixels[:, q : q + 1], (1, BLOCK)) == cap_blocks * BLOCK
-        theirs = theirs_ref[q, height - rows : height - rows + 16][0:1].astype(jnp.float32) > 0.0
-        helps = theirs & (second | jnp.logical_not(mine))
-        first = gate(jnp.logical_not(helps & mine))
-        own, other = gate(jnp.logical_not(helps)), gate(helps)
-        out_ref[q, 0:rows] = own_ref[q, 0:rows] * first
-        out_ref[q, rows:] = own_ref[q, rows:] * own + theirs_ref[q, 0 : height - rows] * other
-
-
-def share(meta, own, theirs, cap_blocks, rows):
-    return call(
-        functools.partial(share_kernel, cap_blocks, rows),
+def share_kernel(cap_blocks, meta_ref, theirs_ref, _, out_hbm, sems):
+    n, height, _ = out_hbm.shape
+    rows = height - theirs_ref.shape[1]
+    lane = lax.broadcasted_iota(jnp.int32, (1, BLOCK), 1)
+    helped = meta_ref[PIXELS : PIXELS + 1, 0:BLOCK] != cap_blocks * BLOCK
+    masks = []
+    for base in range(0, n, BITS):
+        inside = helped & (lane >= base) & (lane < base + BITS)
+        bits = jnp.left_shift(1, jnp.clip(lane - base, 0, BITS - 1))
+        masks.append(jnp.sum(jnp.where(inside, bits, 0).astype(jnp.float32)).astype(jnp.int32))
+
+    def copies(act):
+        for q in range(n):
+
+            @pl.when((masks[q // BITS] >> (q % BITS)) & 1 == 1)
+            def _():
+                act(
+                    pltpu.make_async_copy(
+                        theirs_ref.at[q], out_hbm.at[q, rows:height], sems.at[q]
+                    )
+                )
+
+    copies(lambda copy: copy.start())
+    copies(lambda copy: copy.wait())
+
+
+def share(meta, own, theirs, cap_blocks):
+    return call(
+        functools.partial(share_kernel, cap_blocks),
         "share",
-        pltpu.VMEM(own.shape, own.dtype),
-        in_specs=[WHOLE] * 3,
-        out_specs=WHOLE,
+        pltpu.HBM(own.shape, own.dtype),
+        in_specs=[WHOLE] * 2 + [ANYWHERE],
+        out_specs=ANYWHERE,
+        input_output_aliases={2: 0},
+        scratch_shapes=[pltpu.SemaphoreType.DMA((own.shape[0],))],
         bytes_accessed=4 * 1024 * 1024,
-    )(meta, own, theirs)
-
-
-def left_out(meta, their_meta, cap, second):
+    )(meta, theirs, own)
+
+
+def left_out(meta, their_meta, cap):
     mine, theirs = meta[PIXELS] == cap, their_meta[PIXELS] == cap
     fits = (meta[PIXELS] <= BLOCK) & (meta[COUNT] <= MERGED)
-    return theirs & (second | jnp.logical_not(mine)) & jnp.logical_not(fits)
+    return jnp.logical_not(mine | fits), mine & theirs
 
 
 def rest_kernel(cap_blocks, meta_s, their_meta_s, frames_hbm, cm_hbm, out_ref, *scratch):
     frames_ref, cm_ref = scratch
     n, _, rows, _ = out_ref.shape
+    kept = cap_blocks // 2
     pltpu.sync_copy(frames_hbm, frames_ref)
     pltpu.sync_copy(cm_hbm, cm_ref)
-    second = lax.axis_index("pix") != 0
+    right = lax.broadcasted_iota(jnp.int32, (1, BLOCK), 1) >= BLOCK // 2
     for q in range(n):
         counts = [[ref[row, q] for row in range(PIXELS + 1)] for ref in (meta_s, their_meta_s)]
-        wanted = left_out(*counts, cap_blocks * BLOCK, second)
+        large, twice = left_out(*counts, cap_blocks * BLOCK)
         for i in range(cap_blocks):
             block = meta_s[LIST, q * cap_blocks + i]
-            valid = cm_ref[pl.ds(block, 1), :] >= 0
-            out_ref[q, i] = take(frames_ref, block) * gate(
-                valid & wanted & (i < meta_s[COUNT, q])
-            )
+            wanted = jnp.broadcast_to(large, (1, BLOCK))
+            if i >= kept:
+                wanted |= twice & right if i == kept else twice
+            valid = (cm_ref[pl.ds(block, 1), :] >= 0) & (i < meta_s[COUNT, q])
+            out_ref[q, i] = take(frames_ref, block) * gate(valid & wanted)
 
 
 def pack_rest(meta, their_meta, frames, cm, cap_blocks):
@@ -458,15 +479,14 @@
 
     moving, meta = pack_move(cm, frames, cap_blocks)
     theirs = swap(moving)
-    packed = share(meta, pack_own(meta, cm, frames, cap_blocks), theirs, cap_blocks, rows)
+    packed = share(meta, pack_own(meta, cm, frames, cap_blocks), theirs, cap_blocks)
     received = send(packed)
 
     meta, _ = lax.optimization_barrier((meta, packed))
     their_meta = swap(meta)
-    second = lax.axis_index("pix") != 0
-    spills = left_out(meta[:, :n], their_meta[:, :n], cap_blocks * BLOCK, second)
-    spills |= left_out(their_meta[:, :n], meta[:, :n], cap_blocks * BLOCK, jnp.logical_not(second))
-    overflow = jnp.any(spills)
+    cap = cap_blocks * BLOCK
+    large, twice = left_out(meta[:, :n], their_meta[:, :n], cap)
+    overflow = jnp.any(large | twice | left_out(their_meta[:, :n], meta[:, :n], cap)[0])
 
     first = normalise(received, total, 0, early, [overflow.astype(jnp.int32).reshape(1)])
     their_first = swap(first)

time: 48.3 us -> 48.4 us (level)
  transfers between devices with their start and end apart: 5 -> 5, of which waited for: 4 -> 3; matrix products, arithmetic and copies ran while one was open for 1% -> 1% of each run, Pallas kernels for 9% -> 10%
where the time goes in v4:
time: 48.4 us; the launch traced here: 47.5 us
  waiting for transfers between devices  25 us (52%)
  Pallas kernels  10.6 us (22%)
  starting transfers between devices  10.6 us (22%)
  between operations  0.72 us (1%)
  other arithmetic  0.64 us (1%)
    all_to_all x1, waiting for transfers between devices, send(): lax.all_to_all(blocks, 'frame', split_axis=0, concat_axis=0, tiled=True)  23.8 us
    all_to_all x1, starting transfers between devices, send(): lax.all_to_all(blocks, 'frame', split_axis=0, concat_axis=0, tiled=True)  6.65 us
    ppermute x4, starting transfers between devices, swap(): return lax.ppermute(x, 'pix', SWAP)  3.97 us
    pallas_call x1, Pallas kernels, pack_own(): call(functools.partial(own_kernel, cap_blocks), 'pack_own', pltpu.HBM(sha...  2.57 us
    pallas_call x1, Pallas kernels, pack_move(): call(functools.partial(move_kernel, cap_blocks), 'pack_move', [jax.ShapeD...  2.33 us
    pallas_call x2, Pallas kernels, partial_sums(): call(functools.partial(partial_kernel, len(normed)), 'partial_sums', sums...  1.81 us
    pallas_call x1, Pallas kernels, correlate(): call(result_kernel, 'correlate', pltpu.HBM((1, rows, total), jnp.bfloat16...  1.75 us
    ppermute x4, waiting for transfers between devices, swap(): return lax.ppermute(x, 'pix', SWAP)  1.12 us
  transfers between devices with their start and end apart: 5, of which 3 were waited for; matrix products, arithmetic and copies ran while one was open for 1% of the time, Pallas kernels for 10%

profile of v4, /device:TPU:11, one launch (start us, length us, event | category | flops | bytes accessed | tf_op | source)
XLA Modules:
  0.0 47.5 jit_solution(2549747514133105774)
XLA Ops:
  0.0 0.0 copy-start
  0.0 0.0 copy-start.2
  0.0 2.3 %pack_move.1 = (bf16[16,224,128]{2,1,0:T(8,128)(2,1)S(1)}, s32[8,128]{1,0:T(8,128)S(1)}) custom-call(s32[128,128]{1,0:T(8,128)} %bitcast.4, bf16[64,16384]{1,0:T(8,128)(2,1)} %frames_ref.1), custom_call_target="tpu_custom_call" | custom-call | tf_op jit(solution)/shard_map/pack_move/pallas_call | solution.py:155
  2.3 0.7 %collective-permute-start.1 = (bf16[16,224,128]{2,1,0:T(8,128)(2,1)S(1)}, bf16[16,224,128]{2,1,0:T(8,128)(2,1)S(1)}, u32[]{:S(2)}, u32[]{:S(2)}) collective-permute-start(bf16[16,224,128]{2,1,0:T(8,128)(2,1)S(1)} %get-tuple-element.54), channel_id=1, source_target_pairs={{0,1},{1,0},{2,3},{3,2},{4,5},{5,4},{6,7},{7,6},{8,9},{9,8},{10,11... | collective-permute-start | bytes 2752520 | tf_op jit(solution)/shard_map/ppermute | solution.py:475
  3.1 0.0 copy-done
  3.1 0.0 copy-done.2
  3.1 2.6 %pack_own.1._ = bf16[16,288,128]{2,1,0:T(8,128)(2,1)} custom-call(s32[8,128]{1,0:T(8,128)S(1)} %get-tuple-element.55.meta_s.meta_ref, s32[128,128]{1,0:T(8,128)S(1)} %bitcast.5, bf16[64,16384]{1,0:T(8,128)(2,1)S(1)} %copy-done), custom_call_target="tpu_custom_call" | custom-call | bytes 4194304 | tf_op jit(solution)/shard_map/pack_own/pallas_call | solution.py:206
  5.7 0.0 collective-permute-done.1.theirs_ref
  5.7 1.0 %share.1 = bf16[16,288,128]{2,1,0:T(8,128)(2,1)} custom-call(s32[8,128]{1,0:T(8,128)S(1)} %get-tuple-element.55.meta_s.meta_ref, bf16[16,224,128]{2,1,0:T(8,128)(2,1)S(1)} %collective-permute-done.1.theirs_ref, bf16[16,288,128]{2,1,0:T(8,128)(2,1)} %pack_own.1._), custom_call_target="tpu_custom_call", output_to_operand_aliasing={{}: (2, {})} | custom-call | bytes 4194304 | tf_op jit(solution)/shard_map/share/pallas_call | solution.py:248
  6.7 6.6 %all-to-all-start.1 = ((bf16[16,288,128]{2,1,0:T(8,128)(2,1)}), bf16[16,288,128]{2,1,0:T(8,128)(2,1)S(1)}, u32[]{:S(2)}, u32[]{:S(2)}) async-start(bf16[16,288,128]{2,1,0:T(8,128)(2,1)} %share.1), calls=%async_computation.1 | async-start | bytes 2359296 | tf_op jit(solution)/shard_map/all_to_all | solution.py:478
  13.3 0.7 %collective-permute-start.2 = (s32[8,128]{1,0:T(8,128)S(1)}, s32[8,128]{1,0:T(8,128)S(1)}, u32[]{:S(2)}, u32[]{:S(2)}) collective-permute-start(s32[8,128]{1,0:T(8,128)S(1)} %get-tuple-element.55.meta_s.meta_ref), channel_id=1, source_target_pairs={{0,1},{1,0},{2,3},{3,2},{4,5},{5,4},{6,7},{7,6},{8,9},{9,8},{10,11... | collective-permute-start | bytes 12296 | tf_op jit(solution)/shard_map/ppermute | solution.py:475
  14.0 0.8 %collective-permute-done.2 = s32[8,128]{1,0:T(8,128)S(1)} collective-permute-done((s32[8,128]{1,0:T(8,128)S(1)}, s32[8,128]{1,0:T(8,128)S(1)}, u32[]{:S(2)}, u32[]{:S(2)}) %collective-permute-start.2) | collective-permute-done | bytes 4128 | tf_op jit(solution)/shard_map/ppermute | solution.py:475
  14.9 0.6 %or_reduce_fusion = pred[]{:T(512)} fusion(s32[8,128]{1,0:T(8,128)S(1)} %collective-permute-done.2, s32[8,128]{1,0:T(8,128)S(1)} %get-tuple-element.55.meta_s.meta_ref), kind=kLoop, calls=%fused_computation | loop fusion | flops 255 | bytes 257 | tf_op jit(solution)/shard_map/reduce_or | solution.py:489
  16.2 23.8 %all-to-all-done.1.raw_ref = bf16[16,288,128]{2,1,0:T(8,128)(2,1)S(1)} async-done(((bf16[16,288,128]{2,1,0:T(8,128)(2,1)}), bf16[16,288,128]{2,1,0:T(8,128)(2,1)S(1)}, u32[]{:S(2)}, u32[]{:S(2)}) %all-to-all-start.1) | async-done | bytes 1179680 | tf_op jit(solution)/shard_map/all_to_all | solution.py:478
  40.0 0.6 %normalise.4.refs_0_ = bf16[1024,384]{1,0:T(8,128)(2,1)S(1)} custom-call(bf16[16,288,128]{2,1,0:T(8,128)(2,1)S(1)} %all-to-all-done.1.raw_ref, s32[1]{0:T(128)} %bitcast.2.refs_0_), custom_call_target="tpu_custom_call" | custom-call | flops 4718592 | bytes 1572864 | tf_op jit(solution)/shard_map/normalise/pallas_call | solution.py:354
  40.6 2.4 %collective-permute-start.4 = (bf16[1024,384]{1,0:T(8,128)(2,1)S(1)}, bf16[1024,384]{1,0:T(8,128)(2,1)S(1)}, u32[]{:S(2)}, u32[]{:S(2)}) collective-permute-start(bf16[1024,384]{1,0:T(8,128)(2,1)S(1)} %normalise.4.refs_0_), channel_id=1, source_target_pairs={{0,1},{1,0},{2,3},{3,2},{4,5},{5,4},{6,7},{7,6},{8,9},{9,8},{10,11... | collective-permute-start | bytes 2359304 | tf_op jit(solution)/shard_map/ppermute | solution.py:475
  43.1 0.5 %normalise.5.refs_1_ = bf16[1024,256]{1,0:T(8,128)(2,1)S(1)} custom-call(bf16[16,288,128]{2,1,0:T(8,128)(2,1)S(1)} %all-to-all-done.1.raw_ref, bf16[1024,384]{1,0:T(8,128)(2,1)S(1)} %normalise.4.refs_0_), custom_call_target="tpu_custom_call" | custom-call | flops 3145728 | bytes 1048576 | tf_op jit(solution)/shard_map/normalise/pallas_call | solution.py:354
  43.6 0.1 collective-permute-start.3
  43.6 1.0 %partial_sums.4 = (f32[512,1024]{1,0:T(8,128)S(1)}, f32[8,1024]{1,0:T(8,128)S(1)}) custom-call(bf16[1024,384]{1,0:T(8,128)(2,1)S(1)} %normalise.4.refs_0_, bf16[1024,256]{1,0:T(8,128)(2,1)S(1)} %normalise.5.refs_1_), custom_call_target="tpu_custom_call" | custom-call | flops 805306368 | bytes 2097152 | tf_op jit(solution)/shard_map/partial_sums/pallas_call | solution.py:406
  44.7 0.3 collective-permute-done.4.refs_0_
  45.0 0.8 %partial_sums.5 = (f32[512,1024]{1,0:T(8,128)S(1)}, f32[8,1024]{1,0:T(8,128)S(1)}) custom-call(bf16[1024,384]{1,0:T(8,128)(2,1)S(1)} %collective-permute-done.4.refs_0_, f32[512,1024]{1,0:T(8,128)S(1)} %get-tuple-element.56.refs_1_, f32[8,1024]{1,0:T(8,128)S(1)} %get-tuple-element.57.refs_2_), custom_call_target="tpu_custom_call" | custom-call | flops 402653184 | bytes 2097152 | tf_op jit(solution)/shard_map/partial_sums/pallas_call | solution.py:406
  45.8 0.0 collective-permute-done.3
  45.8 1.8 %conditional.1 = (bf16[1,512,1024]{2,1,0:T(8,128)(2,1)}) conditional(s32[]{:T(128)} %convert_element_type.4, (s32[8,128]{1,0:T(8,128)S(1)}, s32[8,128]{1,0:T(8,128)S(1)}, bf16[1024,256]{1,0:T(8,128)(2,1)S(1)}, f32[512,1024]{1,0:T(8,128)S(1)}, f32[8,1024]{1,0:T(8,128)S(1)}) %tuple.13, (s32[8,128]{1,0:T(8,128)S(1)}, s32[8,128]{1,0:T(8,128)S(1)}, ...), branch_computations={%region_1.0_spmd, %region_2.0_spmd} | conditional | flops 2428502016 | bytes 30670952 | solution.py:507
  45.8 1.8 %correlate.2 = bf16[1,512,1024]{2,1,0:T(8,128)(2,1)} custom-call(s32[8,128]{1,0:T(8,128)S(1)} %get-tuple-element.32.meta_ref, s32[8,128]{1,0:T(8,128)S(1)} %get-tuple-element.33.their_meta_ref, bf16[1024,256]{1,0:T(8,128)(2,1)S(1)} %get-tuple-element.34.normed_ref, f32[512,1024]{1,0:T(8,128)S(1)} %get-tuple-element.35.gram_in, ...), custom_call_target="tpu_custom_call" | custom-call | flops 268435456 | bytes 3145728 | tf_op jit(solution)/shard_map/cond/branch_0_fun/correlate/pallas_call | solution.py:448
Async XLA Ops:
  0.0 3.1 %copy-start = (bf16[64,16384]{1,0:T(8,128)(2,1)S(1)}, bf16[64,16384]{1,0:T(8,128)(2,1)}, u32[]{:S(2)}) copy-start(bf16[64,16384]{1,0:T(8,128)(2,1)} %frames_ref.1) | copy-start | bytes 6291460
  0.0 3.1 %copy-start.2 = (s32[16384]{0:T(1024)S(1)}, s32[16384]{0:T(1024)}, u32[]{:S(2)}) copy-start(s32[16384]{0:T(1024)} %param.5) | copy-start | bytes 196612
  2.3 3.3 %collective-permute-start.1 = (bf16[16,224,128]{2,1,0:T(8,128)(2,1)S(1)}, bf16[16,224,128]{2,1,0:T(8,128)(2,1)S(1)}, u32[]{:S(2)}, u32[]{:S(2)}) collective-permute-start(bf16[16,224,128]{2,1,0:T(8,128)(2,1)S(1)} %get-tuple-element.54), channel_id=1, source_target_pairs={{0,1},{1,0},{2,3},{3,2},{4,5},{5,4},{6,7},{7,6},{8,9},{9,8},{10,11... | collective-permute-start | bytes 2752520 | tf_op jit(solution)/shard_map/ppermute | solution.py:475
  6.7 33.3 %all-to-all-start.1 = ((bf16[16,288,128]{2,1,0:T(8,128)(2,1)}), bf16[16,288,128]{2,1,0:T(8,128)(2,1)S(1)}, u32[]{:S(2)}, u32[]{:S(2)}) async-start(bf16[16,288,128]{2,1,0:T(8,128)(2,1)} %share.1), calls=%async_computation.1 | async-start | bytes 2359296 | tf_op jit(solution)/shard_map/all_to_all | solution.py:478
  13.3 1.5 %collective-permute-start.2 = (s32[8,128]{1,0:T(8,128)S(1)}, s32[8,128]{1,0:T(8,128)S(1)}, u32[]{:S(2)}, u32[]{:S(2)}) collective-permute-start(s32[8,128]{1,0:T(8,128)S(1)} %get-tuple-element.55.meta_s.meta_ref), channel_id=1, source_target_pairs={{0,1},{1,0},{2,3},{3,2},{4,5},{5,4},{6,7},{7,6},{8,9},{9,8},{10,11... | collective-permute-start | bytes 12296 | tf_op jit(solution)/shard_map/ppermute | solution.py:475
  40.6 4.3 %collective-permute-start.4 = (bf16[1024,384]{1,0:T(8,128)(2,1)S(1)}, bf16[1024,384]{1,0:T(8,128)(2,1)S(1)}, u32[]{:S(2)}, u32[]{:S(2)}) collective-permute-start(bf16[1024,384]{1,0:T(8,128)(2,1)S(1)} %normalise.4.refs_0_), channel_id=1, source_target_pairs={{0,1},{1,0},{2,3},{3,2},{4,5},{5,4},{6,7},{7,6},{8,9},{9,8},{10,11... | collective-permute-start | bytes 2359304 | tf_op jit(solution)/shard_map/ppermute | solution.py:475
  43.6 2.2 %collective-permute-start.3 = (bf16[1024,256]{1,0:T(8,128)(2,1)S(1)}, bf16[1024,256]{1,0:T(8,128)(2,1)S(1)}, u32[]{:S(2)}, u32[]{:S(2)}) collective-permute-start(bf16[1024,256]{1,0:T(8,128)(2,1)S(1)} %normalise.5.refs_1_), channel_id=1, source_target_pairs={{0,1},{1,0},{2,3},{3,2},{4,5},{5,4},{6,7},{7,6},{8,9},{9,8},{10,11... | collective-permute-start | bytes 1572872 | tf_op jit(solution)/shard_map/ppermute | solution.py:475

commit v5 on v4

--- a/solution.py
+++ b/solution.py
@@ -16,7 +16,6 @@
 VMEM_BYTES = 32 * 1024 * 1024
 LIST, COUNT, PIXELS = 0, 1, 2
 MERGED = 2
-BITS = 16
 SWAP = [(0, 1), (1, 0)]
 WHOLE = pl.BlockSpec(memory_space=pltpu.VMEM)
 ANYWHERE = pl.BlockSpec(memory_space=pl.ANY)
@@ -170,7 +169,7 @@
     )
 
 
-def own_kernel(cap_blocks, meta_s, cm_ref, frames_ref, out_hbm, out_ref, place_ref, sems):
+def own_kernel(cap_blocks, meta_s, cm_ref, frames_ref, out_ref, place_ref):
     n = out_ref.shape[0]
     rows = frames_ref.shape[0]
     kept = cap_blocks // 2
@@ -191,70 +190,45 @@
         out_ref[q, 0:rows] = compact.astype(jnp.bfloat16) + take(frames_ref, block) * full
         for i in range(1, kept):
             block = meta_s[LIST, q * cap_blocks + i]
-            out_ref[q, i * rows : (i + 1) * rows] = take(frames_ref, block)
+            out_ref[q, i * rows : (i + 1) * rows] = take(frames_ref, block) * full
         block = meta_s[LIST, q * cap_blocks + kept]
-        out_ref[q, kept * rows :] = fold(take(frames_ref, block), False)
-        pltpu.make_async_copy(out_ref.at[q], out_hbm.at[q], sems.at[q]).start()
-    for q in range(n):
-        pltpu.make_async_copy(out_ref.at[q], out_hbm.at[q], sems.at[q]).wait()
+        out_ref[q, kept * rows :] = fold(take(frames_ref, block), False) * full
 
 
 def pack_own(meta, cm, frames, cap_blocks):
     rows = frames.shape[0]
     n = cm.shape[0] // cap_blocks
-    shape = (n, cap_blocks // 2 * rows + count_half_rows(rows), BLOCK)
+    height = cap_blocks // 2 * rows + count_half_rows(rows)
     return call(
         functools.partial(own_kernel, cap_blocks),
         "pack_own",
-        pltpu.HBM(shape, frames.dtype),
+        jax.ShapeDtypeStruct((n, height, BLOCK), frames.dtype),
         in_specs=[pl.BlockSpec(memory_space=pltpu.SMEM)] + [WHOLE] * 2,
-        out_specs=ANYWHERE,
-        scratch_shapes=[
-            pltpu.VMEM(shape, frames.dtype),
-            pltpu.VMEM(cm.shape, jnp.float32),
-            pltpu.SemaphoreType.DMA((n,)),
-        ],
+        out_specs=WHOLE,
+        scratch_shapes=[pltpu.VMEM(cm.shape, jnp.float32)],
         bytes_accessed=4 * 1024 * 1024,
     )(meta, cm, frames)
 
 
-def share_kernel(cap_blocks, meta_ref, theirs_ref, _, out_hbm, sems):
-    n, height, _ = out_hbm.shape
+def share_kernel(cap_blocks, meta_ref, own_ref, theirs_ref, out_ref):
+    n, height, _ = out_ref.shape
     rows = height - theirs_ref.shape[1]
-    lane = lax.broadcasted_iota(jnp.int32, (1, BLOCK), 1)
     helped = meta_ref[PIXELS : PIXELS + 1, 0:BLOCK] != cap_blocks * BLOCK
-    masks = []
-    for base in range(0, n, BITS):
-        inside = helped & (lane >= base) & (lane < base + BITS)
-        bits = jnp.left_shift(1, jnp.clip(lane - base, 0, BITS - 1))
-        masks.append(jnp.sum(jnp.where(inside, bits, 0).astype(jnp.float32)).astype(jnp.int32))
-
-    def copies(act):
-        for q in range(n):
-
-            @pl.when((masks[q // BITS] >> (q % BITS)) & 1 == 1)
-            def _():
-                act(
-                    pltpu.make_async_copy(
-                        theirs_ref.at[q], out_hbm.at[q, rows:height], sems.at[q]
-                    )
-                )
-
-    copies(lambda copy: copy.start())
-    copies(lambda copy: copy.wait())
+    out_ref[:, 0:rows] = own_ref[:, 0:rows]
+    for q in range(n):
+        other = gate(helped[:, q : q + 1])
+        out_ref[q, rows:] = own_ref[q, rows:] + theirs_ref[q] * other
 
 
 def share(meta, own, theirs, cap_blocks):
     return call(
         functools.partial(share_kernel, cap_blocks),
         "share",
-        pltpu.HBM(own.shape, own.dtype),
-        in_specs=[WHOLE] * 2 + [ANYWHERE],
-        out_specs=ANYWHERE,
-        input_output_aliases={2: 0},
-        scratch_shapes=[pltpu.SemaphoreType.DMA((own.shape[0],))],
+        jax.ShapeDtypeStruct(own.shape, own.dtype),
+        in_specs=[WHOLE] * 3,
+        out_specs=WHOLE,
         bytes_accessed=4 * 1024 * 1024,
-    )(meta, theirs, own)
+    )(meta, own, theirs)
 
 
 def left_out(meta, their_meta, cap):

time: 48.4 us -> 48.1 us (level)
  Pallas kernels: 10.6 us -> 10.1 us
  transfers between devices with their start and end apart: 5 -> 5, of which waited for: 3 -> 4; matrix products, arithmetic and copies ran while one was open for 1% -> 1% of each run, Pallas kernels for 10% -> 9%
where the time goes in v5:
time: 48.1 us; the launch traced here: 47.2 us
  waiting for transfers between devices  24.8 us (52%)
  starting transfers between devices  11 us (23%)
  Pallas kernels  10.1 us (21%)
  between operations  0.71 us (1%)
  other arithmetic  0.64 us (1%)
    all_to_all x1, waiting for transfers between devices, send(): lax.all_to_all(blocks, 'frame', split_axis=0, concat_axis=0, tiled=True)  23.4 us
    all_to_all x1, starting transfers between devices, send(): lax.all_to_all(blocks, 'frame', split_axis=0, concat_axis=0, tiled=True)  6.64 us
    ppermute x4, starting transfers between devices, swap(): return lax.ppermute(x, 'pix', SWAP)  4.32 us
    pallas_call x1, Pallas kernels, pack_move(): call(functools.partial(move_kernel, cap_blocks), 'pack_move', [jax.ShapeD...  2.32 us
    pallas_call x2, Pallas kernels, partial_sums(): call(functools.partial(partial_kernel, len(normed)), 'partial_sums', sums...  1.81 us
    pallas_call x1, Pallas kernels, pack_own(): call(functools.partial(own_kernel, cap_blocks), 'pack_own', jax.ShapeDtyp...  1.8 us
    pallas_call x1, Pallas kernels, correlate(): call(result_kernel, 'correlate', pltpu.HBM((1, rows, total), jnp.bfloat16...  1.75 us
    ppermute x4, waiting for transfers between devices, swap(): return lax.ppermute(x, 'pix', SWAP)  1.41 us
  transfers between devices with their start and end apart: 5, of which 4 were waited for; matrix products, arithmetic and copies ran while one was open for 1% of the time, Pallas kernels for 9%

profile of v5, /device:TPU:11, one launch (start us, length us, event | category | flops | bytes accessed | tf_op | source)
XLA Modules:
  0.0 47.2 jit_solution(15365195223915198650)
XLA Ops:
  0.0 0.0 copy-start
  0.0 0.0 copy-start.2
  0.0 2.3 %pack_move.1 = (bf16[16,224,128]{2,1,0:T(8,128)(2,1)S(1)}, s32[8,128]{1,0:T(8,128)S(1)}) custom-call(s32[128,128]{1,0:T(8,128)} %bitcast.4, bf16[64,16384]{1,0:T(8,128)(2,1)} %frames_ref.1), custom_call_target="tpu_custom_call" | custom-call | tf_op jit(solution)/shard_map/pack_move/pallas_call | solution.py:154
  2.3 0.7 %collective-permute-start.1 = (bf16[16,224,128]{2,1,0:T(8,128)(2,1)S(1)}, bf16[16,224,128]{2,1,0:T(8,128)(2,1)S(1)}, u32[]{:S(2)}, u32[]{:S(2)}) collective-permute-start(bf16[16,224,128]{2,1,0:T(8,128)(2,1)S(1)} %get-tuple-element.54), channel_id=1, source_target_pairs={{0,1},{1,0},{2,3},{3,2},{4,5},{5,4},{6,7},{7,6},{8,9},{9,8},{10,11... | collective-permute-start | bytes 2752520 | tf_op jit(solution)/shard_map/ppermute | solution.py:449
  3.1 0.0 copy-done
  3.1 0.0 copy-done.2
  3.1 1.8 %pack_own.1.own_ref = bf16[16,288,128]{2,1,0:T(8,128)(2,1)S(1)} custom-call(s32[8,128]{1,0:T(8,128)S(1)} %get-tuple-element.55.meta_s.meta_ref, s32[128,128]{1,0:T(8,128)S(1)} %bitcast.5, bf16[64,16384]{1,0:T(8,128)(2,1)S(1)} %copy-done), custom_call_target="tpu_custom_call" | custom-call | bytes 4194304 | tf_op jit(solution)/shard_map/pack_own/pallas_call | solution.py:202
  4.9 0.3 collective-permute-done.1.theirs_ref
  5.2 1.3 %share.1 = bf16[16,288,128]{2,1,0:T(8,128)(2,1)} custom-call(s32[8,128]{1,0:T(8,128)S(1)} %get-tuple-element.55.meta_s.meta_ref, bf16[16,288,128]{2,1,0:T(8,128)(2,1)S(1)} %pack_own.1.own_ref, bf16[16,224,128]{2,1,0:T(8,128)(2,1)S(1)} %collective-permute-done.1.theirs_ref), custom_call_target="tpu_custom_call" | custom-call | bytes 4194304 | tf_op jit(solution)/shard_map/share/pallas_call | solution.py:224
  6.5 6.6 %all-to-all-start.1 = ((bf16[16,288,128]{2,1,0:T(8,128)(2,1)}), bf16[16,288,128]{2,1,0:T(8,128)(2,1)S(1)}, u32[]{:S(2)}, u32[]{:S(2)}) async-start(bf16[16,288,128]{2,1,0:T(8,128)(2,1)} %share.1), calls=%async_computation.1 | async-start | bytes 2359296 | tf_op jit(solution)/shard_map/all_to_all | solution.py:452
  13.1 0.9 %collective-permute-start.2 = (s32[8,128]{1,0:T(8,128)S(1)}, s32[8,128]{1,0:T(8,128)S(1)}, u32[]{:S(2)}, u32[]{:S(2)}) collective-permute-start(s32[8,128]{1,0:T(8,128)S(1)} %get-tuple-element.55.meta_s.meta_ref), channel_id=1, source_target_pairs={{0,1},{1,0},{2,3},{3,2},{4,5},{5,4},{6,7},{7,6},{8,9},{9,8},{10,11... | collective-permute-start | bytes 12296 | tf_op jit(solution)/shard_map/ppermute | solution.py:449
  14.1 0.8 %collective-permute-done.2 = s32[8,128]{1,0:T(8,128)S(1)} collective-permute-done((s32[8,128]{1,0:T(8,128)S(1)}, s32[8,128]{1,0:T(8,128)S(1)}, u32[]{:S(2)}, u32[]{:S(2)}) %collective-permute-start.2) | collective-permute-done | bytes 4128 | tf_op jit(solution)/shard_map/ppermute | solution.py:449
  14.9 0.6 %or_reduce_fusion = pred[]{:T(512)} fusion(s32[8,128]{1,0:T(8,128)S(1)} %collective-permute-done.2, s32[8,128]{1,0:T(8,128)S(1)} %get-tuple-element.55.meta_s.meta_ref), kind=kLoop, calls=%fused_computation | loop fusion | flops 255 | bytes 257 | tf_op jit(solution)/shard_map/reduce_or | solution.py:463
  16.2 23.4 %all-to-all-done.1.raw_ref = bf16[16,288,128]{2,1,0:T(8,128)(2,1)S(1)} async-done(((bf16[16,288,128]{2,1,0:T(8,128)(2,1)}), bf16[16,288,128]{2,1,0:T(8,128)(2,1)S(1)}, u32[]{:S(2)}, u32[]{:S(2)}) %all-to-all-start.1) | async-done | bytes 1179680 | tf_op jit(solution)/shard_map/all_to_all | solution.py:452
  39.6 0.6 %normalise.4.refs_0_ = bf16[1024,384]{1,0:T(8,128)(2,1)S(1)} custom-call(bf16[16,288,128]{2,1,0:T(8,128)(2,1)S(1)} %all-to-all-done.1.raw_ref, s32[1]{0:T(128)} %bitcast.2.refs_0_), custom_call_target="tpu_custom_call" | custom-call | flops 4718592 | bytes 1572864 | tf_op jit(solution)/shard_map/normalise/pallas_call | solution.py:328
  40.2 2.6 %collective-permute-start.4 = (bf16[1024,384]{1,0:T(8,128)(2,1)S(1)}, bf16[1024,384]{1,0:T(8,128)(2,1)S(1)}, u32[]{:S(2)}, u32[]{:S(2)}) collective-permute-start(bf16[1024,384]{1,0:T(8,128)(2,1)S(1)} %normalise.4.refs_0_), channel_id=1, source_target_pairs={{0,1},{1,0},{2,3},{3,2},{4,5},{5,4},{6,7},{7,6},{8,9},{9,8},{10,11... | collective-permute-start | bytes 2359304 | tf_op jit(solution)/shard_map/ppermute | solution.py:449
  42.8 0.5 %normalise.5.refs_1_ = bf16[1024,256]{1,0:T(8,128)(2,1)S(1)} custom-call(bf16[16,288,128]{2,1,0:T(8,128)(2,1)S(1)} %all-to-all-done.1.raw_ref, bf16[1024,384]{1,0:T(8,128)(2,1)S(1)} %normalise.4.refs_0_), custom_call_target="tpu_custom_call" | custom-call | flops 3145728 | bytes 1048576 | tf_op jit(solution)/shard_map/normalise/pallas_call | solution.py:328
  43.2 0.1 collective-permute-start.3
  43.3 1.0 %partial_sums.4 = (f32[512,1024]{1,0:T(8,128)S(1)}, f32[8,1024]{1,0:T(8,128)S(1)}) custom-call(bf16[1024,384]{1,0:T(8,128)(2,1)S(1)} %normalise.4.refs_0_, bf16[1024,256]{1,0:T(8,128)(2,1)S(1)} %normalise.5.refs_1_), custom_call_target="tpu_custom_call" | custom-call | flops 805306368 | bytes 2097152 | tf_op jit(solution)/shard_map/partial_sums/pallas_call | solution.py:380
  44.4 0.3 collective-permute-done.4.refs_0_
  44.7 0.8 %partial_sums.5 = (f32[512,1024]{1,0:T(8,128)S(1)}, f32[8,1024]{1,0:T(8,128)S(1)}) custom-call(bf16[1024,384]{1,0:T(8,128)(2,1)S(1)} %collective-permute-done.4.refs_0_, f32[512,1024]{1,0:T(8,128)S(1)} %get-tuple-element.56.refs_1_, f32[8,1024]{1,0:T(8,128)S(1)} %get-tuple-element.57.refs_2_), custom_call_target="tpu_custom_call" | custom-call | flops 402653184 | bytes 2097152 | tf_op jit(solution)/shard_map/partial_sums/pallas_call | solution.py:380
  45.4 0.0 collective-permute-done.3
  45.5 1.8 %conditional.1 = (bf16[1,512,1024]{2,1,0:T(8,128)(2,1)}) conditional(s32[]{:T(128)} %convert_element_type.4, (s32[8,128]{1,0:T(8,128)S(1)}, s32[8,128]{1,0:T(8,128)S(1)}, bf16[1024,256]{1,0:T(8,128)(2,1)S(1)}, f32[512,1024]{1,0:T(8,128)S(1)}, f32[8,1024]{1,0:T(8,128)S(1)}) %tuple.13, (s32[8,128]{1,0:T(8,128)S(1)}, s32[8,128]{1,0:T(8,128)S(1)}, ...), branch_computations={%region_1.0_spmd, %region_2.0_spmd} | conditional | flops 2428502016 | bytes 30670952 | solution.py:481
  45.5 1.7 %correlate.2 = bf16[1,512,1024]{2,1,0:T(8,128)(2,1)} custom-call(s32[8,128]{1,0:T(8,128)S(1)} %get-tuple-element.32.meta_ref, s32[8,128]{1,0:T(8,128)S(1)} %get-tuple-element.33.their_meta_ref, bf16[1024,256]{1,0:T(8,128)(2,1)S(1)} %get-tuple-element.34.normed_ref, f32[512,1024]{1,0:T(8,128)S(1)} %get-tuple-element.35.gram_in, ...), custom_call_target="tpu_custom_call" | custom-call | flops 268435456 | bytes 3145728 | tf_op jit(solution)/shard_map/cond/branch_0_fun/correlate/pallas_call | solution.py:422
Async XLA Ops:
  0.0 3.1 %copy-start = (bf16[64,16384]{1,0:T(8,128)(2,1)S(1)}, bf16[64,16384]{1,0:T(8,128)(2,1)}, u32[]{:S(2)}) copy-start(bf16[64,16384]{1,0:T(8,128)(2,1)} %frames_ref.1) | copy-start | bytes 6291460
  0.0 3.1 %copy-start.2 = (s32[16384]{0:T(1024)S(1)}, s32[16384]{0:T(1024)}, u32[]{:S(2)}) copy-start(s32[16384]{0:T(1024)} %param.5) | copy-start | bytes 196612
  2.3 2.8 %collective-permute-start.1 = (bf16[16,224,128]{2,1,0:T(8,128)(2,1)S(1)}, bf16[16,224,128]{2,1,0:T(8,128)(2,1)S(1)}, u32[]{:S(2)}, u32[]{:S(2)}) collective-permute-start(bf16[16,224,128]{2,1,0:T(8,128)(2,1)S(1)} %get-tuple-element.54), channel_id=1, source_target_pairs={{0,1},{1,0},{2,3},{3,2},{4,5},{5,4},{6,7},{7,6},{8,9},{9,8},{10,11... | collective-permute-start | bytes 2752520 | tf_op jit(solution)/shard_map/ppermute | solution.py:449
  6.5 33.1 %all-to-all-start.1 = ((bf16[16,288,128]{2,1,0:T(8,128)(2,1)}), bf16[16,288,128]{2,1,0:T(8,128)(2,1)S(1)}, u32[]{:S(2)}, u32[]{:S(2)}) async-start(bf16[16,288,128]{2,1,0:T(8,128)(2,1)} %share.1), calls=%async_computation.1 | async-start | bytes 2359296 | tf_op jit(solution)/shard_map/all_to_all | solution.py:452
  13.1 1.8 %collective-permute-start.2 = (s32[8,128]{1,0:T(8,128)S(1)}, s32[8,128]{1,0:T(8,128)S(1)}, u32[]{:S(2)}, u32[]{:S(2)}) collective-permute-start(s32[8,128]{1,0:T(8,128)S(1)} %get-tuple-element.55.meta_s.meta_ref), channel_id=1, source_target_pairs={{0,1},{1,0},{2,3},{3,2},{4,5},{5,4},{6,7},{7,6},{8,9},{9,8},{10,11... | collective-permute-start | bytes 12296 | tf_op jit(solution)/shard_map/ppermute | solution.py:449
  40.2 4.5 %collective-permute-start.4 = (bf16[1024,384]{1,0:T(8,128)(2,1)S(1)}, bf16[1024,384]{1,0:T(8,128)(2,1)S(1)}, u32[]{:S(2)}, u32[]{:S(2)}) collective-permute-start(bf16[1024,384]{1,0:T(8,128)(2,1)S(1)} %normalise.4.refs_0_), channel_id=1, source_target_pairs={{0,1},{1,0},{2,3},{3,2},{4,5},{5,4},{6,7},{7,6},{8,9},{9,8},{10,11... | collective-permute-start | bytes 2359304 | tf_op jit(solution)/shard_map/ppermute | solution.py:449
  43.2 2.2 %collective-permute-start.3 = (bf16[1024,256]{1,0:T(8,128)(2,1)S(1)}, bf16[1024,256]{1,0:T(8,128)(2,1)S(1)}, u32[]{:S(2)}, u32[]{:S(2)}) collective-permute-start(bf16[1024,256]{1,0:T(8,128)(2,1)S(1)} %normalise.5.refs_1_), channel_id=1, source_target_pairs={{0,1},{1,0},{2,3},{3,2},{4,5},{5,4},{6,7},{7,6},{8,9},{9,8},{10,11... | collective-permute-start | bytes 1572872 | tf_op jit(solution)/shard_map/ppermute | solution.py:449

commit v6 on v5

--- a/solution.py
+++ b/solution.py
@@ -276,7 +276,7 @@
     )
 
 
-def lay_out(raw_ref, rows, first, padded):
+def lay_out(raw_ref, rows, first, whole, padded):
     n, height, _ = raw_ref.shape
     total = n * rows
     zero = jnp.zeros((PAD, BLOCK), jnp.float32)
@@ -286,7 +286,7 @@
         padded[i, PAD + total : 2 * PAD + total] = zero
         for source in range(n):
             start = PAD + source * rows
-            if (slot + 1) * rows <= height:
+            if slot < whole:
                 block = raw_ref[source, slot * rows : (slot + 1) * rows]
                 padded[i, start : start + rows] = block.astype(jnp.float32)
             else:
@@ -317,16 +317,16 @@
         )
 
 
-def norm_kernel(rows, first, raw_ref, *refs):
+def norm_kernel(rows, first, whole, raw_ref, *refs):
     out_ref, padded = refs[-2:]
-    lay_out(raw_ref, rows, first, padded)
+    lay_out(raw_ref, rows, first, whole, padded)
     for start in range(0, out_ref.shape[0], CHUNK):
         norm_rows(padded, start, CHUNK, out_ref)
 
 
-def normalise(raw, total, first, slots, after=()):
-    return call(
-        functools.partial(norm_kernel, total // raw.shape[0], first),
+def normalise(raw, total, first, slots, whole, after=()):
+    return call(
+        functools.partial(norm_kernel, total // raw.shape[0], first, whole),
         "normalise",
         jax.ShapeDtypeStruct((total, slots * BLOCK), jnp.bfloat16),
         flops=12 * total * slots * BLOCK,
@@ -462,16 +462,18 @@
     large, twice = left_out(meta[:, :n], their_meta[:, :n], cap)
     overflow = jnp.any(large | twice | left_out(their_meta[:, :n], meta[:, :n], cap)[0])
 
-    first = normalise(received, total, 0, early, [overflow.astype(jnp.int32).reshape(1)])
+    flag = overflow.astype(jnp.int32).reshape(1)
+    first = normalise(received, total, 0, early, slots - 1, [flag])
     their_first = swap(first)
-    last = normalise(received, total, early, slots - early, [first])
+    last = normalise(received, total, early, slots - early, slots - 1, [first])
     their_last = swap(last)
     sums = partial_sums([first, last], [], parts)
     sums = partial_sums([their_first], sums, parts)
 
     def spill(frames, cm, meta, their_meta, their_last, *sums):
         rest = send(pack_rest(meta, their_meta, frames, cm, cap_blocks))
-        normed = normalise(rest.reshape(n, cap_blocks * rows, BLOCK), total, 0, cap_blocks)
+        rest = rest.reshape(n, cap_blocks * rows, BLOCK)
+        normed = normalise(rest, total, 0, cap_blocks, cap_blocks)
         sums = partial_sums([normed, swap(normed)], sums, parts)
         return correlate([meta, their_meta], their_last, sums)
 

time: 48.1 us -> 48.1 us (level)
  no operation moved by 1% of the time
where the time goes in v6:
time: 48.1 us; the launch traced here: 47.2 us
  waiting for transfers between devices  24.8 us (52%)
  starting transfers between devices  11 us (23%)
  Pallas kernels  10.1 us (21%)
  between operations  0.71 us (1%)
  other arithmetic  0.64 us (1%)
    all_to_all x1, waiting for transfers between devices, send(): lax.all_to_all(blocks, 'frame', split_axis=0, concat_axis=0, tiled=True)  23.4 us
    all_to_all x1, starting transfers between devices, send(): lax.all_to_all(blocks, 'frame', split_axis=0, concat_axis=0, tiled=True)  6.64 us
    ppermute x4, starting transfers between devices, swap(): return lax.ppermute(x, 'pix', SWAP)  4.32 us
    pallas_call x1, Pallas kernels, pack_move(): call(functools.partial(move_kernel, cap_blocks), 'pack_move', [jax.ShapeD...  2.32 us
    pallas_call x2, Pallas kernels, partial_sums(): call(functools.partial(partial_kernel, len(normed)), 'partial_sums', sums...  1.81 us
    pallas_call x1, Pallas kernels, pack_own(): call(functools.partial(own_kernel, cap_blocks), 'pack_own', jax.ShapeDtyp...  1.8 us
    pallas_call x1, Pallas kernels, correlate(): call(result_kernel, 'correlate', pltpu.HBM((1, rows, total), jnp.bfloat16...  1.75 us
    ppermute x4, waiting for transfers between devices, swap(): return lax.ppermute(x, 'pix', SWAP)  1.41 us
  transfers between devices with their start and end apart: 5, of which 4 were waited for; matrix products, arithmetic and copies ran while one was open for 1% of the time, Pallas kernels for 9%

profile of v6, /device:TPU:11, one launch (start us, length us, event | category | flops | bytes accessed | tf_op | source)
XLA Modules:
  0.0 47.2 jit_solution(15365195223915198650)
XLA Ops:
  0.0 0.0 copy-start
  0.0 0.0 copy-start.2
  0.0 2.3 %pack_move.1 = (bf16[16,224,128]{2,1,0:T(8,128)(2,1)S(1)}, s32[8,128]{1,0:T(8,128)S(1)}) custom-call(s32[128,128]{1,0:T(8,128)} %bitcast.4, bf16[64,16384]{1,0:T(8,128)(2,1)} %frames_ref.1), custom_call_target="tpu_custom_call" | custom-call | tf_op jit(solution)/shard_map/pack_move/pallas_call | solution.py:154
  2.3 0.7 %collective-permute-start.1 = (bf16[16,224,128]{2,1,0:T(8,128)(2,1)S(1)}, bf16[16,224,128]{2,1,0:T(8,128)(2,1)S(1)}, u32[]{:S(2)}, u32[]{:S(2)}) collective-permute-start(bf16[16,224,128]{2,1,0:T(8,128)(2,1)S(1)} %get-tuple-element.54), channel_id=1, source_target_pairs={{0,1},{1,0},{2,3},{3,2},{4,5},{5,4},{6,7},{7,6},{8,9},{9,8},{10,11... | collective-permute-start | bytes 2752520 | tf_op jit(solution)/shard_map/ppermute | solution.py:449
  3.1 0.0 copy-done
  3.1 0.0 copy-done.2
  3.1 1.8 %pack_own.1.own_ref = bf16[16,288,128]{2,1,0:T(8,128)(2,1)S(1)} custom-call(s32[8,128]{1,0:T(8,128)S(1)} %get-tuple-element.55.meta_s.meta_ref, s32[128,128]{1,0:T(8,128)S(1)} %bitcast.5, bf16[64,16384]{1,0:T(8,128)(2,1)S(1)} %copy-done), custom_call_target="tpu_custom_call" | custom-call | bytes 4194304 | tf_op jit(solution)/shard_map/pack_own/pallas_call | solution.py:202
  4.9 0.3 collective-permute-done.1.theirs_ref
  5.2 1.3 %share.1 = bf16[16,288,128]{2,1,0:T(8,128)(2,1)} custom-call(s32[8,128]{1,0:T(8,128)S(1)} %get-tuple-element.55.meta_s.meta_ref, bf16[16,288,128]{2,1,0:T(8,128)(2,1)S(1)} %pack_own.1.own_ref, bf16[16,224,128]{2,1,0:T(8,128)(2,1)S(1)} %collective-permute-done.1.theirs_ref), custom_call_target="tpu_custom_call" | custom-call | bytes 4194304 | tf_op jit(solution)/shard_map/share/pallas_call | solution.py:224
  6.5 6.6 %all-to-all-start.1 = ((bf16[16,288,128]{2,1,0:T(8,128)(2,1)}), bf16[16,288,128]{2,1,0:T(8,128)(2,1)S(1)}, u32[]{:S(2)}, u32[]{:S(2)}) async-start(bf16[16,288,128]{2,1,0:T(8,128)(2,1)} %share.1), calls=%async_computation.1 | async-start | bytes 2359296 | tf_op jit(solution)/shard_map/all_to_all | solution.py:452
  13.1 0.9 %collective-permute-start.2 = (s32[8,128]{1,0:T(8,128)S(1)}, s32[8,128]{1,0:T(8,128)S(1)}, u32[]{:S(2)}, u32[]{:S(2)}) collective-permute-start(s32[8,128]{1,0:T(8,128)S(1)} %get-tuple-element.55.meta_s.meta_ref), channel_id=1, source_target_pairs={{0,1},{1,0},{2,3},{3,2},{4,5},{5,4},{6,7},{7,6},{8,9},{9,8},{10,11... | collective-permute-start | bytes 12296 | tf_op jit(solution)/shard_map/ppermute | solution.py:449
  14.1 0.8 %collective-permute-done.2 = s32[8,128]{1,0:T(8,128)S(1)} collective-permute-done((s32[8,128]{1,0:T(8,128)S(1)}, s32[8,128]{1,0:T(8,128)S(1)}, u32[]{:S(2)}, u32[]{:S(2)}) %collective-permute-start.2) | collective-permute-done | bytes 4128 | tf_op jit(solution)/shard_map/ppermute | solution.py:449
  14.9 0.6 %or_reduce_fusion = pred[]{:T(512)} fusion(s32[8,128]{1,0:T(8,128)S(1)} %collective-permute-done.2, s32[8,128]{1,0:T(8,128)S(1)} %get-tuple-element.55.meta_s.meta_ref), kind=kLoop, calls=%fused_computation | loop fusion | flops 255 | bytes 257 | tf_op jit(solution)/shard_map/reduce_or | solution.py:463
  16.2 23.4 %all-to-all-done.1.raw_ref = bf16[16,288,128]{2,1,0:T(8,128)(2,1)S(1)} async-done(((bf16[16,288,128]{2,1,0:T(8,128)(2,1)}), bf16[16,288,128]{2,1,0:T(8,128)(2,1)S(1)}, u32[]{:S(2)}, u32[]{:S(2)}) %all-to-all-start.1) | async-done | bytes 1179680 | tf_op jit(solution)/shard_map/all_to_all | solution.py:452
  39.6 0.6 %normalise.4.refs_0_ = bf16[1024,384]{1,0:T(8,128)(2,1)S(1)} custom-call(bf16[16,288,128]{2,1,0:T(8,128)(2,1)S(1)} %all-to-all-done.1.raw_ref, s32[1]{0:T(128)} %bitcast.2.refs_0_), custom_call_target="tpu_custom_call" | custom-call | flops 4718592 | bytes 1572864 | tf_op jit(solution)/shard_map/normalise/pallas_call | solution.py:328
  40.2 2.6 %collective-permute-start.4 = (bf16[1024,384]{1,0:T(8,128)(2,1)S(1)}, bf16[1024,384]{1,0:T(8,128)(2,1)S(1)}, u32[]{:S(2)}, u32[]{:S(2)}) collective-permute-start(bf16[1024,384]{1,0:T(8,128)(2,1)S(1)} %normalise.4.refs_0_), channel_id=1, source_target_pairs={{0,1},{1,0},{2,3},{3,2},{4,5},{5,4},{6,7},{7,6},{8,9},{9,8},{10,11... | collective-permute-start | bytes 2359304 | tf_op jit(solution)/shard_map/ppermute | solution.py:449
  42.8 0.5 %normalise.5.refs_1_ = bf16[1024,256]{1,0:T(8,128)(2,1)S(1)} custom-call(bf16[16,288,128]{2,1,0:T(8,128)(2,1)S(1)} %all-to-all-done.1.raw_ref, bf16[1024,384]{1,0:T(8,128)(2,1)S(1)} %normalise.4.refs_0_), custom_call_target="tpu_custom_call" | custom-call | flops 3145728 | bytes 1048576 | tf_op jit(solution)/shard_map/normalise/pallas_call | solution.py:328
  43.2 0.1 collective-permute-start.3
  43.3 1.0 %partial_sums.4 = (f32[512,1024]{1,0:T(8,128)S(1)}, f32[8,1024]{1,0:T(8,128)S(1)}) custom-call(bf16[1024,384]{1,0:T(8,128)(2,1)S(1)} %normalise.4.refs_0_, bf16[1024,256]{1,0:T(8,128)(2,1)S(1)} %normalise.5.refs_1_), custom_call_target="tpu_custom_call" | custom-call | flops 805306368 | bytes 2097152 | tf_op jit(solution)/shard_map/partial_sums/pallas_call | solution.py:380
  44.4 0.3 collective-permute-done.4.refs_0_
  44.7 0.8 %partial_sums.5 = (f32[512,1024]{1,0:T(8,128)S(1)}, f32[8,1024]{1,0:T(8,128)S(1)}) custom-call(bf16[1024,384]{1,0:T(8,128)(2,1)S(1)} %collective-permute-done.4.refs_0_, f32[512,1024]{1,0:T(8,128)S(1)} %get-tuple-element.56.refs_1_, f32[8,1024]{1,0:T(8,128)S(1)} %get-tuple-element.57.refs_2_), custom_call_target="tpu_custom_call" | custom-call | flops 402653184 | bytes 2097152 | tf_op jit(solution)/shard_map/partial_sums/pallas_call | solution.py:380
  45.4 0.0 collective-permute-done.3
  45.5 1.8 %conditional.1 = (bf16[1,512,1024]{2,1,0:T(8,128)(2,1)}) conditional(s32[]{:T(128)} %convert_element_type.4, (s32[8,128]{1,0:T(8,128)S(1)}, s32[8,128]{1,0:T(8,128)S(1)}, bf16[1024,256]{1,0:T(8,128)(2,1)S(1)}, f32[512,1024]{1,0:T(8,128)S(1)}, f32[8,1024]{1,0:T(8,128)S(1)}) %tuple.13, (s32[8,128]{1,0:T(8,128)S(1)}, s32[8,128]{1,0:T(8,128)S(1)}, ...), branch_computations={%region_1.0_spmd, %region_2.0_spmd} | conditional | flops 2428502016 | bytes 30670952 | solution.py:483
  45.5 1.7 %correlate.2 = bf16[1,512,1024]{2,1,0:T(8,128)(2,1)} custom-call(s32[8,128]{1,0:T(8,128)S(1)} %get-tuple-element.32.meta_ref, s32[8,128]{1,0:T(8,128)S(1)} %get-tuple-element.33.their_meta_ref, bf16[1024,256]{1,0:T(8,128)(2,1)S(1)} %get-tuple-element.34.normed_ref, f32[512,1024]{1,0:T(8,128)S(1)} %get-tuple-element.35.gram_in, ...), custom_call_target="tpu_custom_call" | custom-call | flops 268435456 | bytes 3145728 | tf_op jit(solution)/shard_map/cond/branch_0_fun/correlate/pallas_call | solution.py:422
Async XLA Ops:
  0.0 3.1 %copy-start = (bf16[64,16384]{1,0:T(8,128)(2,1)S(1)}, bf16[64,16384]{1,0:T(8,128)(2,1)}, u32[]{:S(2)}) copy-start(bf16[64,16384]{1,0:T(8,128)(2,1)} %frames_ref.1) | copy-start | bytes 6291460
  0.0 3.1 %copy-start.2 = (s32[16384]{0:T(1024)S(1)}, s32[16384]{0:T(1024)}, u32[]{:S(2)}) copy-start(s32[16384]{0:T(1024)} %param.5) | copy-start | bytes 196612
  2.3 2.8 %collective-permute-start.1 = (bf16[16,224,128]{2,1,0:T(8,128)(2,1)S(1)}, bf16[16,224,128]{2,1,0:T(8,128)(2,1)S(1)}, u32[]{:S(2)}, u32[]{:S(2)}) collective-permute-start(bf16[16,224,128]{2,1,0:T(8,128)(2,1)S(1)} %get-tuple-element.54), channel_id=1, source_target_pairs={{0,1},{1,0},{2,3},{3,2},{4,5},{5,4},{6,7},{7,6},{8,9},{9,8},{10,11... | collective-permute-start | bytes 2752520 | tf_op jit(solution)/shard_map/ppermute | solution.py:449
  6.5 33.1 %all-to-all-start.1 = ((bf16[16,288,128]{2,1,0:T(8,128)(2,1)}), bf16[16,288,128]{2,1,0:T(8,128)(2,1)S(1)}, u32[]{:S(2)}, u32[]{:S(2)}) async-start(bf16[16,288,128]{2,1,0:T(8,128)(2,1)} %share.1), calls=%async_computation.1 | async-start | bytes 2359296 | tf_op jit(solution)/shard_map/all_to_all | solution.py:452
  13.1 1.8 %collective-permute-start.2 = (s32[8,128]{1,0:T(8,128)S(1)}, s32[8,128]{1,0:T(8,128)S(1)}, u32[]{:S(2)}, u32[]{:S(2)}) collective-permute-start(s32[8,128]{1,0:T(8,128)S(1)} %get-tuple-element.55.meta_s.meta_ref), channel_id=1, source_target_pairs={{0,1},{1,0},{2,3},{3,2},{4,5},{5,4},{6,7},{7,6},{8,9},{9,8},{10,11... | collective-permute-start | bytes 12296 | tf_op jit(solution)/shard_map/ppermute | solution.py:449
  40.2 4.5 %collective-permute-start.4 = (bf16[1024,384]{1,0:T(8,128)(2,1)S(1)}, bf16[1024,384]{1,0:T(8,128)(2,1)S(1)}, u32[]{:S(2)}, u32[]{:S(2)}) collective-permute-start(bf16[1024,384]{1,0:T(8,128)(2,1)S(1)} %normalise.4.refs_0_), channel_id=1, source_target_pairs={{0,1},{1,0},{2,3},{3,2},{4,5},{5,4},{6,7},{7,6},{8,9},{9,8},{10,11... | collective-permute-start | bytes 2359304 | tf_op jit(solution)/shard_map/ppermute | solution.py:449
  43.2 2.2 %collective-permute-start.3 = (bf16[1024,256]{1,0:T(8,128)(2,1)S(1)}, bf16[1024,256]{1,0:T(8,128)(2,1)S(1)}, u32[]{:S(2)}, u32[]{:S(2)}) collective-permute-start(bf16[1024,256]{1,0:T(8,128)(2,1)S(1)} %normalise.5.refs_1_), channel_id=1, source_target_pairs={{0,1},{1,0},{2,3},{3,2},{4,5},{5,4},{6,7},{7,6},{8,9},{9,8},{10,11... | collective-permute-start | bytes 1572872 | tf_op jit(solution)/shard_map/ppermute | solution.py:449

commit v7 on v6

--- a/solution.py
+++ b/solution.py
@@ -91,24 +91,14 @@
     return jnp.sum(before * member, axis=1, keepdims=True)
 
 
-def find_blocks(cm, cap_blocks, meta_ref):
-    blocks = cm.shape[0]
-    width = meta_ref.shape[1]
-    first, member, earlier, pixels = find_members(cm)
+def find_blocks(members, cap_blocks, width):
+    first, member, earlier, _ = members
+    blocks = first.shape[0]
     rank = sum_before(earlier, member, 1.0).astype(jnp.int32)
     slot = jnp.where(first >= 0, first * cap_blocks + rank, -1)
     hit = slot == lax.broadcasted_iota(jnp.int32, (blocks, width), 1)
     index = lax.broadcasted_iota(jnp.int32, (blocks, width), 0).astype(jnp.float32)
-    meta_ref[...] = jnp.zeros_like(meta_ref)
-    meta_ref[LIST : LIST + 1, :] = jnp.sum(
-        jnp.where(hit, index, 0.0), axis=0, keepdims=True
-    ).astype(jnp.int32)
-    meta_ref[COUNT : COUNT + 1, 0:BLOCK] = jnp.sum(member, axis=0, keepdims=True).astype(
-        jnp.int32
-    )
-    meta_ref[PIXELS : PIXELS + 1, 0:BLOCK] = jnp.sum(
-        member * pixels, axis=0, keepdims=True
-    ).astype(jnp.int32)
+    return jnp.sum(jnp.where(hit, index, 0.0), axis=0, keepdims=True).astype(jnp.int32)
 
 
 def find_places(cm):
@@ -121,8 +111,8 @@
     return jnp.where(cm >= 0, place + sum_before(earlier, member, pixels), -1.0)
 
 
-def move_kernel(cap_blocks, cm_hbm, frames_hbm, out_ref, meta_ref, *scratch):
-    frames_ref, cm_ref, meta_s, sems = scratch
+def move_kernel(cap_blocks, cm_hbm, frames_hbm, out_ref, meta_ref, frames_ref, cm_ref, *scratch):
+    list_ref, list_s, sems = scratch
     n = out_ref.shape[0]
     rows = frames_ref.shape[0]
     kept = cap_blocks // 2
@@ -131,18 +121,26 @@
     get_frames = pltpu.make_async_copy(frames_hbm, frames_ref, sems.at[1])
     get_frames.start()
     get_cm.wait()
-    find_blocks(cm_ref[...], cap_blocks, meta_ref)
-    to_scalars = pltpu.make_async_copy(meta_ref, meta_s, sems.at[2])
+    members = find_members(cm_ref[...])
+    found = find_blocks(members, cap_blocks, meta_ref.shape[1])
+    list_ref[...] = jnp.broadcast_to(found, list_ref.shape)
+    to_scalars = pltpu.make_async_copy(list_ref, list_s, sems.at[2])
     to_scalars.start()
+    _, member, _, pixels = members
+    meta_ref[...] = jnp.zeros_like(meta_ref)
+    meta_ref[LIST : LIST + 1, :] = found
+    for row, values in ((COUNT, member), (PIXELS, member * pixels)):
+        totals = jnp.sum(values, axis=0, keepdims=True)
+        meta_ref[row : row + 1, 0:BLOCK] = totals.astype(jnp.int32)
     to_scalars.wait()
     get_frames.wait()
     for q in range(n):
         for i in range(kept + 1, cap_blocks):
-            block = meta_s[LIST, q * cap_blocks + i]
+            block = list_s[0, q * cap_blocks + i]
             start = (i - kept - 1) * rows
             out_ref[q, start : start + rows] = take(frames_ref, block)
         start = (cap_blocks - kept - 1) * rows
-        block = meta_s[LIST, q * cap_blocks + kept]
+        block = list_s[0, q * cap_blocks + kept]
         out_ref[q, start:] = fold(take(frames_ref, block), True)
 
 
@@ -154,12 +152,16 @@
     return call(
         functools.partial(move_kernel, cap_blocks),
         "pack_move",
-        [jax.ShapeDtypeStruct((n, height, BLOCK), frames.dtype), meta],
+        [
+            jax.ShapeDtypeStruct((n, height, BLOCK), frames.dtype),
+            meta,
+            jax.ShapeDtypeStruct(frames.shape, frames.dtype),
+            jax.ShapeDtypeStruct(cm.shape, cm.dtype),
+        ],
         in_specs=[ANYWHERE] * 2,
-        out_specs=[WHOLE] * 2,
+        out_specs=[WHOLE] * 4,
         scratch_shapes=[
-            pltpu.VMEM(frames.shape, frames.dtype),
-            pltpu.VMEM(cm.shape, cm.dtype),
+            pltpu.VMEM(meta.shape, meta.dtype),
             pltpu.SMEM(meta.shape, meta.dtype),
             pltpu.SemaphoreType.DMA((3,)),
         ],
@@ -451,9 +453,10 @@
     def send(blocks):
         return lax.all_to_all(blocks, "frame", split_axis=0, concat_axis=0, tiled=True)
 
-    moving, meta = pack_move(cm, frames, cap_blocks)
+    moving, meta, near_frames, near_cm = pack_move(cm, frames, cap_blocks)
     theirs = swap(moving)
-    packed = share(meta, pack_own(meta, cm, frames, cap_blocks), theirs, cap_blocks)
+    own = pack_own(meta, near_cm, near_frames, cap_blocks)
+    packed = share(meta, own, theirs, cap_blocks)
     received = send(packed)
 
     meta, _ = lax.optimization_barrier((meta, packed))

time: 48.1 us -> 48 us (level)
  no operation moved by 1% of the time
where the time goes in v7:
time: 48 us; the launch traced here: 47 us
  waiting for transfers between devices  24.8 us (52%)
  starting transfers between devices  10.9 us (23%)
  Pallas kernels  9.94 us (21%)
  between operations  0.71 us (1%)
  other arithmetic  0.64 us (1%)
    all_to_all x1, waiting for transfers between devices, send(): lax.all_to_all(blocks, 'frame', split_axis=0, concat_axis=0, tiled=True)  23.4 us
    all_to_all x1, starting transfers between devices, send(): lax.all_to_all(blocks, 'frame', split_axis=0, concat_axis=0, tiled=True)  6.64 us
    ppermute x4, starting transfers between devices, swap(): return lax.ppermute(x, 'pix', SWAP)  4.31 us
    pallas_call x1, Pallas kernels, pack_move(): call(functools.partial(move_kernel, cap_blocks), 'pack_move', [jax.ShapeD...  2.16 us
    pallas_call x2, Pallas kernels, partial_sums(): call(functools.partial(partial_kernel, len(normed)), 'partial_sums', sums...  1.81 us
    pallas_call x1, Pallas kernels, pack_own(): call(functools.partial(own_kernel, cap_blocks), 'pack_own', jax.ShapeDtyp...  1.8 us
    pallas_call x1, Pallas kernels, correlate(): call(result_kernel, 'correlate', pltpu.HBM((1, rows, total), jnp.bfloat16...  1.75 us
    ppermute x4, waiting for transfers between devices, swap(): return lax.ppermute(x, 'pix', SWAP)  1.41 us
  transfers between devices with their start and end apart: 5, of which 4 were waited for; matrix products, arithmetic and copies ran while one was open for 1% of the time, Pallas kernels for 9%

profile of v7, /device:TPU:11, one launch (start us, length us, event | category | flops | bytes accessed | tf_op | source)
XLA Modules:
  0.0 47.0 jit_solution(2092396826719947966)
XLA Ops:
  0.0 2.2 %pack_move.1 = (bf16[16,224,128]{2,1,0:T(8,128)(2,1)S(1)}, s32[8,128]{1,0:T(8,128)S(1)}, bf16[64,16384]{1,0:T(8,128)(2,1)S(1)}, s32[128,128]{1,0:T(8,128)S(1)}) custom-call(s32[128,128]{1,0:T(8,128)} %bitcast.4, bf16[64,16384]{1,0:T(8,128)(2,1)} %frames_hbm.1), custom_call_target="tpu_custom_call" | custom-call | tf_op jit(solution)/shard_map/pack_move/pallas_call | solution.py:152
  2.2 0.7 %collective-permute-start.1 = (bf16[16,224,128]{2,1,0:T(8,128)(2,1)S(1)}, bf16[16,224,128]{2,1,0:T(8,128)(2,1)S(1)}, u32[]{:S(2)}, u32[]{:S(2)}) collective-permute-start(bf16[16,224,128]{2,1,0:T(8,128)(2,1)S(1)} %get-tuple-element.58), channel_id=1, source_target_pairs={{0,1},{1,0},{2,3},{3,2},{4,5},{5,4},{6,7},{7,6},{8,9},{9,8},{10,11... | collective-permute-start | bytes 2752520 | tf_op jit(solution)/shard_map/ppermute | solution.py:451
  2.9 1.8 %pack_own.1.own_ref = bf16[16,288,128]{2,1,0:T(8,128)(2,1)S(1)} custom-call(s32[8,128]{1,0:T(8,128)S(1)} %get-tuple-element.59.meta_s.meta_ref, s32[128,128]{1,0:T(8,128)S(1)} %get-tuple-element.56.cm_ref, bf16[64,16384]{1,0:T(8,128)(2,1)S(1)} %get-tuple-element.57.frames_ref), custom_call_target="tpu_custom_call" | custom-call | bytes 4194304 | tf_op jit(solution)/shard_map/pack_own/pallas_call | solution.py:204
  4.7 0.3 collective-permute-done.1.theirs_ref
  5.0 1.3 %share.1 = bf16[16,288,128]{2,1,0:T(8,128)(2,1)} custom-call(s32[8,128]{1,0:T(8,128)S(1)} %get-tuple-element.59.meta_s.meta_ref, bf16[16,288,128]{2,1,0:T(8,128)(2,1)S(1)} %pack_own.1.own_ref, bf16[16,224,128]{2,1,0:T(8,128)(2,1)S(1)} %collective-permute-done.1.theirs_ref), custom_call_target="tpu_custom_call" | custom-call | bytes 4194304 | tf_op jit(solution)/shard_map/share/pallas_call | solution.py:226
  6.3 6.6 %all-to-all-start.1 = ((bf16[16,288,128]{2,1,0:T(8,128)(2,1)}), bf16[16,288,128]{2,1,0:T(8,128)(2,1)S(1)}, u32[]{:S(2)}, u32[]{:S(2)}) async-start(bf16[16,288,128]{2,1,0:T(8,128)(2,1)} %share.1), calls=%async_computation.1 | async-start | bytes 2359296 | tf_op jit(solution)/shard_map/all_to_all | solution.py:454
  13.0 0.9 %collective-permute-start.2 = (s32[8,128]{1,0:T(8,128)S(1)}, s32[8,128]{1,0:T(8,128)S(1)}, u32[]{:S(2)}, u32[]{:S(2)}) collective-permute-start(s32[8,128]{1,0:T(8,128)S(1)} %get-tuple-element.59.meta_s.meta_ref), channel_id=1, source_target_pairs={{0,1},{1,0},{2,3},{3,2},{4,5},{5,4},{6,7},{7,6},{8,9},{9,8},{10,11... | collective-permute-start | bytes 12296 | tf_op jit(solution)/shard_map/ppermute | solution.py:451
  13.9 0.8 %collective-permute-done.2 = s32[8,128]{1,0:T(8,128)S(1)} collective-permute-done((s32[8,128]{1,0:T(8,128)S(1)}, s32[8,128]{1,0:T(8,128)S(1)}, u32[]{:S(2)}, u32[]{:S(2)}) %collective-permute-start.2) | collective-permute-done | bytes 4128 | tf_op jit(solution)/shard_map/ppermute | solution.py:451
  14.7 0.6 %or_reduce_fusion = pred[]{:T(512)} fusion(s32[8,128]{1,0:T(8,128)S(1)} %collective-permute-done.2, s32[8,128]{1,0:T(8,128)S(1)} %get-tuple-element.59.meta_s.meta_ref), kind=kLoop, calls=%fused_computation | loop fusion | flops 255 | bytes 257 | tf_op jit(solution)/shard_map/reduce_or | solution.py:466
  16.0 23.4 %all-to-all-done.1.raw_ref = bf16[16,288,128]{2,1,0:T(8,128)(2,1)S(1)} async-done(((bf16[16,288,128]{2,1,0:T(8,128)(2,1)}), bf16[16,288,128]{2,1,0:T(8,128)(2,1)S(1)}, u32[]{:S(2)}, u32[]{:S(2)}) %all-to-all-start.1) | async-done | bytes 1179680 | tf_op jit(solution)/shard_map/all_to_all | solution.py:454
  39.4 0.6 %normalise.4.refs_0_ = bf16[1024,384]{1,0:T(8,128)(2,1)S(1)} custom-call(bf16[16,288,128]{2,1,0:T(8,128)(2,1)S(1)} %all-to-all-done.1.raw_ref, s32[1]{0:T(128)} %bitcast.2.refs_0_), custom_call_target="tpu_custom_call" | custom-call | flops 4718592 | bytes 1572864 | tf_op jit(solution)/shard_map/normalise/pallas_call | solution.py:330
  40.0 2.6 %collective-permute-start.4 = (bf16[1024,384]{1,0:T(8,128)(2,1)S(1)}, bf16[1024,384]{1,0:T(8,128)(2,1)S(1)}, u32[]{:S(2)}, u32[]{:S(2)}) collective-permute-start(bf16[1024,384]{1,0:T(8,128)(2,1)S(1)} %normalise.4.refs_0_), channel_id=1, source_target_pairs={{0,1},{1,0},{2,3},{3,2},{4,5},{5,4},{6,7},{7,6},{8,9},{9,8},{10,11... | collective-permute-start | bytes 2359304 | tf_op jit(solution)/shard_map/ppermute | solution.py:451
  42.6 0.5 %normalise.5.refs_1_ = bf16[1024,256]{1,0:T(8,128)(2,1)S(1)} custom-call(bf16[16,288,128]{2,1,0:T(8,128)(2,1)S(1)} %all-to-all-done.1.raw_ref, bf16[1024,384]{1,0:T(8,128)(2,1)S(1)} %normalise.4.refs_0_), custom_call_target="tpu_custom_call" | custom-call | flops 3145728 | bytes 1048576 | tf_op jit(solution)/shard_map/normalise/pallas_call | solution.py:330
  43.1 0.1 collective-permute-start.3
  43.1 1.0 %partial_sums.4 = (f32[512,1024]{1,0:T(8,128)S(1)}, f32[8,1024]{1,0:T(8,128)S(1)}) custom-call(bf16[1024,384]{1,0:T(8,128)(2,1)S(1)} %normalise.4.refs_0_, bf16[1024,256]{1,0:T(8,128)(2,1)S(1)} %normalise.5.refs_1_), custom_call_target="tpu_custom_call" | custom-call | flops 805306368 | bytes 2097152 | tf_op jit(solution)/shard_map/partial_sums/pallas_call | solution.py:382
  44.2 0.3 collective-permute-done.4.refs_0_
  44.5 0.8 %partial_sums.5 = (f32[512,1024]{1,0:T(8,128)S(1)}, f32[8,1024]{1,0:T(8,128)S(1)}) custom-call(bf16[1024,384]{1,0:T(8,128)(2,1)S(1)} %collective-permute-done.4.refs_0_, f32[512,1024]{1,0:T(8,128)S(1)} %get-tuple-element.60.refs_1_, f32[8,1024]{1,0:T(8,128)S(1)} %get-tuple-element.61.refs_2_), custom_call_target="tpu_custom_call" | custom-call | flops 402653184 | bytes 2097152 | tf_op jit(solution)/shard_map/partial_sums/pallas_call | solution.py:382
  45.3 0.0 collective-permute-done.3
  45.3 1.8 %conditional.1 = (bf16[1,512,1024]{2,1,0:T(8,128)(2,1)}) conditional(s32[]{:T(128)} %convert_element_type.4, (s32[8,128]{1,0:T(8,128)S(1)}, s32[8,128]{1,0:T(8,128)S(1)}, bf16[1024,256]{1,0:T(8,128)(2,1)S(1)}, f32[512,1024]{1,0:T(8,128)S(1)}, f32[8,1024]{1,0:T(8,128)S(1)}) %tuple.13, (s32[8,128]{1,0:T(8,128)S(1)}, s32[8,128]{1,0:T(8,128)S(1)}, ...), branch_computations={%region_1.0_spmd, %region_2.0_spmd} | conditional | flops 2428502016 | bytes 22020144 | solution.py:486
  45.3 1.7 %correlate.2 = bf16[1,512,1024]{2,1,0:T(8,128)(2,1)} custom-call(s32[8,128]{1,0:T(8,128)S(1)} %get-tuple-element.32.meta_ref, s32[8,128]{1,0:T(8,128)S(1)} %get-tuple-element.33.their_meta_ref, bf16[1024,256]{1,0:T(8,128)(2,1)S(1)} %get-tuple-element.34.normed_ref, f32[512,1024]{1,0:T(8,128)S(1)} %get-tuple-element.35.gram_in, ...), custom_call_target="tpu_custom_call" | custom-call | flops 268435456 | bytes 3145728 | tf_op jit(solution)/shard_map/cond/branch_0_fun/correlate/pallas_call | solution.py:424
Async XLA Ops:
  2.2 2.8 %collective-permute-start.1 = (bf16[16,224,128]{2,1,0:T(8,128)(2,1)S(1)}, bf16[16,224,128]{2,1,0:T(8,128)(2,1)S(1)}, u32[]{:S(2)}, u32[]{:S(2)}) collective-permute-start(bf16[16,224,128]{2,1,0:T(8,128)(2,1)S(1)} %get-tuple-element.58), channel_id=1, source_target_pairs={{0,1},{1,0},{2,3},{3,2},{4,5},{5,4},{6,7},{7,6},{8,9},{9,8},{10,11... | collective-permute-start | bytes 2752520 | tf_op jit(solution)/shard_map/ppermute | solution.py:451
  6.3 33.1 %all-to-all-start.1 = ((bf16[16,288,128]{2,1,0:T(8,128)(2,1)}), bf16[16,288,128]{2,1,0:T(8,128)(2,1)S(1)}, u32[]{:S(2)}, u32[]{:S(2)}) async-start(bf16[16,288,128]{2,1,0:T(8,128)(2,1)} %share.1), calls=%async_computation.1 | async-start | bytes 2359296 | tf_op jit(solution)/shard_map/all_to_all | solution.py:454
  13.0 1.8 %collective-permute-start.2 = (s32[8,128]{1,0:T(8,128)S(1)}, s32[8,128]{1,0:T(8,128)S(1)}, u32[]{:S(2)}, u32[]{:S(2)}) collective-permute-start(s32[8,128]{1,0:T(8,128)S(1)} %get-tuple-element.59.meta_s.meta_ref), channel_id=1, source_target_pairs={{0,1},{1,0},{2,3},{3,2},{4,5},{5,4},{6,7},{7,6},{8,9},{9,8},{10,11... | collective-permute-start | bytes 12296 | tf_op jit(solution)/shard_map/ppermute | solution.py:451
  40.0 4.5 %collective-permute-start.4 = (bf16[1024,384]{1,0:T(8,128)(2,1)S(1)}, bf16[1024,384]{1,0:T(8,128)(2,1)S(1)}, u32[]{:S(2)}, u32[]{:S(2)}) collective-permute-start(bf16[1024,384]{1,0:T(8,128)(2,1)S(1)} %normalise.4.refs_0_), channel_id=1, source_target_pairs={{0,1},{1,0},{2,3},{3,2},{4,5},{5,4},{6,7},{7,6},{8,9},{9,8},{10,11... | collective-permute-start | bytes 2359304 | tf_op jit(solution)/shard_map/ppermute | solution.py:451
  43.1 2.2 %collective-permute-start.3 = (bf16[1024,256]{1,0:T(8,128)(2,1)S(1)}, bf16[1024,256]{1,0:T(8,128)(2,1)S(1)}, u32[]{:S(2)}, u32[]{:S(2)}) collective-permute-start(bf16[1024,256]{1,0:T(8,128)(2,1)S(1)} %normalise.5.refs_1_), channel_id=1, source_target_pairs={{0,1},{1,0},{2,3},{3,2},{4,5},{5,4},{6,7},{7,6},{8,9},{9,8},{10,11... | collective-permute-start | bytes 1572872 | tf_op jit(solution)/shard_map/ppermute | solution.py:451

commit v8 on v7

--- a/solution.py
+++ b/solution.py
@@ -392,28 +392,41 @@
 
 
 def result_kernel(meta_ref, their_meta_ref, normed_ref, gram_in, frame_in, out_hbm, *scratch):
-    out_ref, frame_ref, sems = scratch
+    out_ref, gram_ref, frame_ref, left_ref, sems = scratch
     rows, total = gram_in.shape
+    tiles, own_tiles = total // TILE, rows // TILE
     pixels = meta_ref[PIXELS : PIXELS + 1, 0:BLOCK] + their_meta_ref[PIXELS : PIXELS + 1, 0:BLOCK]
     own = lax.broadcasted_iota(jnp.int32, (1, BLOCK), 1) == lax.axis_index("frame")
     number = jnp.sum(jnp.where(own, pixels, 0).astype(jnp.float32), axis=1, keepdims=True)
-    ones = jnp.ones((8, normed_ref.shape[1]), jnp.bfloat16)
-    frame_ref[...] = frame_in[...] + dot_nt(ones, normed_ref[...])
-    first_row = pl.multiple_of(lax.axis_index("pix") * rows, rows)
-    row_sum = jnp.broadcast_to(frame_ref[0:1, pl.ds(first_row, rows)], (BLOCK, rows)).T
+    set_left(normed_ref, left_ref)
+    first_row = lax.axis_index("pix") * rows
+
+    def columns(i):
+        return pl.ds(pl.multiple_of(lax.rem(first_row + i * TILE, total), TILE), TILE)
+
+    def sum_up(i):
+        column = columns(i)
+        before = [gram_in[:, column], frame_in[:, column]]
+        return add_sums([(left_ref, normed_ref)], before, column)
+
+    def finish(i, gram, frame):
+        result = ((gram * row_inv) * (1.0 / frame[0:1])) * number - 1.0
+        out_ref[i] = result.astype(jnp.bfloat16)
+        copy = pltpu.make_async_copy(out_ref.at[i], out_hbm.at[0, :, columns(i)], sems.at[i])
+        copy.start()
+        return copy
+
+    for i in range(own_tiles):
+        gram_ref[i], frame_ref[:, i * TILE : (i + 1) * TILE] = sum_up(i)
+    row_sum = jnp.broadcast_to(frame_ref[0:1, :], (BLOCK, rows)).T
     row_inv = 1.0 / row_sum[:, 0:1]
-    left = normed_ref[pl.ds(first_row, rows), :]
     copies = []
-    for i, start in enumerate(range(0, total, TILE)):
-        column = slice(start, start + TILE)
-        gram = gram_in[:, column] + dot_nt(left, normed_ref[column, :])
-        col_inv = 1.0 / frame_ref[0:1, column]
-        result = ((gram * row_inv) * col_inv) * number - 1.0
-        out_ref[i] = result.astype(jnp.bfloat16)
-        copies.append(
-            pltpu.make_async_copy(out_ref.at[i], out_hbm.at[0, :, column], sems.at[i])
-        )
-        copies[-1].start()
+    for i in range(tiles):
+        if i < own_tiles:
+            gram, frame = gram_ref[i], frame_ref[:, i * TILE : (i + 1) * TILE]
+        else:
+            gram, frame = sum_up(i)
+        copies.append(finish(i, gram, frame))
     for copy in copies:
         copy.wait()
 
@@ -431,7 +444,9 @@
         out_specs=ANYWHERE,
         scratch_shapes=[
             pltpu.VMEM((tiles, rows, TILE), jnp.bfloat16),
-            pltpu.VMEM((8, total), jnp.float32),
+            pltpu.VMEM((rows // TILE, rows, TILE), jnp.float32),
+            pltpu.VMEM((8, rows), jnp.float32),
+            pltpu.VMEM((rows + ONES, normed.shape[1]), normed.dtype),
             pltpu.SemaphoreType.DMA((tiles,)),
         ],
     )(*metas, normed, *before)

time: 48 us -> 48.2 us (level)
  no operation moved by 1% of the time
where the time goes in v8:
time: 48.2 us; the launch traced here: 47.3 us
  waiting for transfers between devices  24.8 us (51%)
  starting transfers between devices  11 us (23%)
  Pallas kernels  10.2 us (21%)
  between operations  0.71 us (1%)
  other arithmetic  0.64 us (1%)
    all_to_all x1, waiting for transfers between devices, send(): lax.all_to_all(blocks, 'frame', split_axis=0, concat_axis=0, tiled=True)  23.4 us
    all_to_all x1, starting transfers between devices, send(): lax.all_to_all(blocks, 'frame', split_axis=0, concat_axis=0, tiled=True)  6.64 us
    ppermute x4, starting transfers between devices, swap(): return lax.ppermute(x, 'pix', SWAP)  4.32 us
    pallas_call x1, Pallas kernels, pack_move(): call(functools.partial(move_kernel, cap_blocks), 'pack_move', [jax.ShapeD...  2.16 us
    pallas_call x1, Pallas kernels, correlate(): call(result_kernel, 'correlate', pltpu.HBM((1, rows, total), jnp.bfloat16...  1.98 us
    pallas_call x2, Pallas kernels, partial_sums(): call(functools.partial(partial_kernel, len(normed)), 'partial_sums', sums...  1.81 us
    pallas_call x1, Pallas kernels, pack_own(): call(functools.partial(own_kernel, cap_blocks), 'pack_own', jax.ShapeDtyp...  1.8 us
    ppermute x4, waiting for transfers between devices, swap(): return lax.ppermute(x, 'pix', SWAP)  1.42 us
  transfers between devices with their start and end apart: 5, of which 4 were waited for; matrix products, arithmetic and copies ran while one was open for 1% of the time, Pallas kernels for 9%

profile of v8, /device:TPU:11, one launch (start us, length us, event | category | flops | bytes accessed | tf_op | source)
XLA Modules:
  0.0 47.3 jit_solution(12026577784074403524)
XLA Ops:
  0.0 2.2 %pack_move.1 = (bf16[16,224,128]{2,1,0:T(8,128)(2,1)S(1)}, s32[8,128]{1,0:T(8,128)S(1)}, bf16[64,16384]{1,0:T(8,128)(2,1)S(1)}, s32[128,128]{1,0:T(8,128)S(1)}) custom-call(s32[128,128]{1,0:T(8,128)} %bitcast.4, bf16[64,16384]{1,0:T(8,128)(2,1)} %frames_hbm.1), custom_call_target="tpu_custom_call" | custom-call | tf_op jit(solution)/shard_map/pack_move/pallas_call | solution.py:152
  2.2 0.7 %collective-permute-start.1 = (bf16[16,224,128]{2,1,0:T(8,128)(2,1)S(1)}, bf16[16,224,128]{2,1,0:T(8,128)(2,1)S(1)}, u32[]{:S(2)}, u32[]{:S(2)}) collective-permute-start(bf16[16,224,128]{2,1,0:T(8,128)(2,1)S(1)} %get-tuple-element.58), channel_id=1, source_target_pairs={{0,1},{1,0},{2,3},{3,2},{4,5},{5,4},{6,7},{7,6},{8,9},{9,8},{10,11... | collective-permute-start | bytes 2752520 | tf_op jit(solution)/shard_map/ppermute | solution.py:466
  2.9 1.8 %pack_own.1.own_ref = bf16[16,288,128]{2,1,0:T(8,128)(2,1)S(1)} custom-call(s32[8,128]{1,0:T(8,128)S(1)} %get-tuple-element.59.meta_s.meta_ref, s32[128,128]{1,0:T(8,128)S(1)} %get-tuple-element.56.cm_ref, bf16[64,16384]{1,0:T(8,128)(2,1)S(1)} %get-tuple-element.57.frames_ref), custom_call_target="tpu_custom_call" | custom-call | bytes 4194304 | tf_op jit(solution)/shard_map/pack_own/pallas_call | solution.py:204
  4.7 0.3 collective-permute-done.1.theirs_ref
  5.0 1.3 %share.1 = bf16[16,288,128]{2,1,0:T(8,128)(2,1)} custom-call(s32[8,128]{1,0:T(8,128)S(1)} %get-tuple-element.59.meta_s.meta_ref, bf16[16,288,128]{2,1,0:T(8,128)(2,1)S(1)} %pack_own.1.own_ref, bf16[16,224,128]{2,1,0:T(8,128)(2,1)S(1)} %collective-permute-done.1.theirs_ref), custom_call_target="tpu_custom_call" | custom-call | bytes 4194304 | tf_op jit(solution)/shard_map/share/pallas_call | solution.py:226
  6.3 6.6 %all-to-all-start.1 = ((bf16[16,288,128]{2,1,0:T(8,128)(2,1)}), bf16[16,288,128]{2,1,0:T(8,128)(2,1)S(1)}, u32[]{:S(2)}, u32[]{:S(2)}) async-start(bf16[16,288,128]{2,1,0:T(8,128)(2,1)} %share.1), calls=%async_computation.1 | async-start | bytes 2359296 | tf_op jit(solution)/shard_map/all_to_all | solution.py:469
  13.0 0.9 %collective-permute-start.2 = (s32[8,128]{1,0:T(8,128)S(1)}, s32[8,128]{1,0:T(8,128)S(1)}, u32[]{:S(2)}, u32[]{:S(2)}) collective-permute-start(s32[8,128]{1,0:T(8,128)S(1)} %get-tuple-element.59.meta_s.meta_ref), channel_id=1, source_target_pairs={{0,1},{1,0},{2,3},{3,2},{4,5},{5,4},{6,7},{7,6},{8,9},{9,8},{10,11... | collective-permute-start | bytes 12296 | tf_op jit(solution)/shard_map/ppermute | solution.py:466
  13.9 0.8 %collective-permute-done.2 = s32[8,128]{1,0:T(8,128)S(1)} collective-permute-done((s32[8,128]{1,0:T(8,128)S(1)}, s32[8,128]{1,0:T(8,128)S(1)}, u32[]{:S(2)}, u32[]{:S(2)}) %collective-permute-start.2) | collective-permute-done | bytes 4128 | tf_op jit(solution)/shard_map/ppermute | solution.py:466
  14.7 0.6 %or_reduce_fusion = pred[]{:T(512)} fusion(s32[8,128]{1,0:T(8,128)S(1)} %collective-permute-done.2, s32[8,128]{1,0:T(8,128)S(1)} %get-tuple-element.59.meta_s.meta_ref), kind=kLoop, calls=%fused_computation | loop fusion | flops 255 | bytes 257 | tf_op jit(solution)/shard_map/reduce_or | solution.py:481
  16.0 23.4 %all-to-all-done.1.raw_ref = bf16[16,288,128]{2,1,0:T(8,128)(2,1)S(1)} async-done(((bf16[16,288,128]{2,1,0:T(8,128)(2,1)}), bf16[16,288,128]{2,1,0:T(8,128)(2,1)S(1)}, u32[]{:S(2)}, u32[]{:S(2)}) %all-to-all-start.1) | async-done | bytes 1179680 | tf_op jit(solution)/shard_map/all_to_all | solution.py:469
  39.4 0.6 %normalise.4.refs_0_ = bf16[1024,384]{1,0:T(8,128)(2,1)S(1)} custom-call(bf16[16,288,128]{2,1,0:T(8,128)(2,1)S(1)} %all-to-all-done.1.raw_ref, s32[1]{0:T(128)} %bitcast.2.refs_0_), custom_call_target="tpu_custom_call" | custom-call | flops 4718592 | bytes 1572864 | tf_op jit(solution)/shard_map/normalise/pallas_call | solution.py:330
  40.0 2.6 %collective-permute-start.4 = (bf16[1024,384]{1,0:T(8,128)(2,1)S(1)}, bf16[1024,384]{1,0:T(8,128)(2,1)S(1)}, u32[]{:S(2)}, u32[]{:S(2)}) collective-permute-start(bf16[1024,384]{1,0:T(8,128)(2,1)S(1)} %normalise.4.refs_0_), channel_id=1, source_target_pairs={{0,1},{1,0},{2,3},{3,2},{4,5},{5,4},{6,7},{7,6},{8,9},{9,8},{10,11... | collective-permute-start | bytes 2359304 | tf_op jit(solution)/shard_map/ppermute | solution.py:466
  42.6 0.5 %normalise.5.refs_1_ = bf16[1024,256]{1,0:T(8,128)(2,1)S(1)} custom-call(bf16[16,288,128]{2,1,0:T(8,128)(2,1)S(1)} %all-to-all-done.1.raw_ref, bf16[1024,384]{1,0:T(8,128)(2,1)S(1)} %normalise.4.refs_0_), custom_call_target="tpu_custom_call" | custom-call | flops 3145728 | bytes 1048576 | tf_op jit(solution)/shard_map/normalise/pallas_call | solution.py:330
  43.1 0.1 collective-permute-start.3
  43.1 1.0 %partial_sums.4 = (f32[512,1024]{1,0:T(8,128)S(1)}, f32[8,1024]{1,0:T(8,128)S(1)}) custom-call(bf16[1024,384]{1,0:T(8,128)(2,1)S(1)} %normalise.4.refs_0_, bf16[1024,256]{1,0:T(8,128)(2,1)S(1)} %normalise.5.refs_1_), custom_call_target="tpu_custom_call" | custom-call | flops 805306368 | bytes 2097152 | tf_op jit(solution)/shard_map/partial_sums/pallas_call | solution.py:382
  44.2 0.3 collective-permute-done.4.refs_0_
  44.5 0.8 %partial_sums.5 = (f32[512,1024]{1,0:T(8,128)S(1)}, f32[8,1024]{1,0:T(8,128)S(1)}) custom-call(bf16[1024,384]{1,0:T(8,128)(2,1)S(1)} %collective-permute-done.4.refs_0_, f32[512,1024]{1,0:T(8,128)S(1)} %get-tuple-element.60.refs_1_, f32[8,1024]{1,0:T(8,128)S(1)} %get-tuple-element.61.refs_2_), custom_call_target="tpu_custom_call" | custom-call | flops 402653184 | bytes 2097152 | tf_op jit(solution)/shard_map/partial_sums/pallas_call | solution.py:382
  45.3 0.0 collective-permute-done.3
  45.3 2.0 %conditional.1 = (bf16[1,512,1024]{2,1,0:T(8,128)(2,1)}) conditional(s32[]{:T(128)} %convert_element_type.4, (s32[8,128]{1,0:T(8,128)S(1)}, s32[8,128]{1,0:T(8,128)S(1)}, bf16[1024,256]{1,0:T(8,128)(2,1)S(1)}, f32[512,1024]{1,0:T(8,128)S(1)}, f32[8,1024]{1,0:T(8,128)S(1)}) %tuple.13, (s32[8,128]{1,0:T(8,128)S(1)}, s32[8,128]{1,0:T(8,128)S(1)}, ...), branch_computations={%region_1.0_spmd, %region_2.0_spmd} | conditional | flops 2428502016 | bytes 22020144 | solution.py:501
  45.3 2.0 %correlate.2 = bf16[1,512,1024]{2,1,0:T(8,128)(2,1)} custom-call(s32[8,128]{1,0:T(8,128)S(1)} %get-tuple-element.32.meta_ref, s32[8,128]{1,0:T(8,128)S(1)} %get-tuple-element.33.their_meta_ref, bf16[1024,256]{1,0:T(8,128)(2,1)S(1)} %get-tuple-element.34.normed_ref, f32[512,1024]{1,0:T(8,128)S(1)} %get-tuple-element.35.gram_in, ...), custom_call_target="tpu_custom_call" | custom-call | flops 268435456 | bytes 3145728 | tf_op jit(solution)/shard_map/cond/branch_0_fun/correlate/pallas_call | solution.py:437
Async XLA Ops:
  2.2 2.8 %collective-permute-start.1 = (bf16[16,224,128]{2,1,0:T(8,128)(2,1)S(1)}, bf16[16,224,128]{2,1,0:T(8,128)(2,1)S(1)}, u32[]{:S(2)}, u32[]{:S(2)}) collective-permute-start(bf16[16,224,128]{2,1,0:T(8,128)(2,1)S(1)} %get-tuple-element.58), channel_id=1, source_target_pairs={{0,1},{1,0},{2,3},{3,2},{4,5},{5,4},{6,7},{7,6},{8,9},{9,8},{10,11... | collective-permute-start | bytes 2752520 | tf_op jit(solution)/shard_map/ppermute | solution.py:466
  6.3 33.1 %all-to-all-start.1 = ((bf16[16,288,128]{2,1,0:T(8,128)(2,1)}), bf16[16,288,128]{2,1,0:T(8,128)(2,1)S(1)}, u32[]{:S(2)}, u32[]{:S(2)}) async-start(bf16[16,288,128]{2,1,0:T(8,128)(2,1)} %share.1), calls=%async_computation.1 | async-start | bytes 2359296 | tf_op jit(solution)/shard_map/all_to_all | solution.py:469
  13.0 1.8 %collective-permute-start.2 = (s32[8,128]{1,0:T(8,128)S(1)}, s32[8,128]{1,0:T(8,128)S(1)}, u32[]{:S(2)}, u32[]{:S(2)}) collective-permute-start(s32[8,128]{1,0:T(8,128)S(1)} %get-tuple-element.59.meta_s.meta_ref), channel_id=1, source_target_pairs={{0,1},{1,0},{2,3},{3,2},{4,5},{5,4},{6,7},{7,6},{8,9},{9,8},{10,11... | collective-permute-start | bytes 12296 | tf_op jit(solution)/shard_map/ppermute | solution.py:466
  40.0 4.5 %collective-permute-start.4 = (bf16[1024,384]{1,0:T(8,128)(2,1)S(1)}, bf16[1024,384]{1,0:T(8,128)(2,1)S(1)}, u32[]{:S(2)}, u32[]{:S(2)}) collective-permute-start(bf16[1024,384]{1,0:T(8,128)(2,1)S(1)} %normalise.4.refs_0_), channel_id=1, source_target_pairs={{0,1},{1,0},{2,3},{3,2},{4,5},{5,4},{6,7},{7,6},{8,9},{9,8},{10,11... | collective-permute-start | bytes 2359304 | tf_op jit(solution)/shard_map/ppermute | solution.py:466
  43.1 2.2 %collective-permute-start.3 = (bf16[1024,256]{1,0:T(8,128)(2,1)S(1)}, bf16[1024,256]{1,0:T(8,128)(2,1)S(1)}, u32[]{:S(2)}, u32[]{:S(2)}) collective-permute-start(bf16[1024,256]{1,0:T(8,128)(2,1)S(1)} %normalise.5.refs_1_), channel_id=1, source_target_pairs={{0,1},{1,0},{2,3},{3,2},{4,5},{5,4},{6,7},{7,6},{8,9},{9,8},{10,11... | collective-permute-start | bytes 1572872 | tf_op jit(solution)/shard_map/ppermute | solution.py:466

commit v9 on v7

--- a/solution.py
+++ b/solution.py
@@ -36,6 +36,10 @@
 
 def dot_nt(a, b):
     return lax.dot_general(a, b, (((1,), (1,)), ((), ())), preferred_element_type=jnp.float32)
+
+
+def list_group(n):
+    return sorted(range(n), key=lambda i: (i >= n // 2, i % 2 if i < n // 2 else 0, i))
 
 
 def count_half_rows(rows):
@@ -216,10 +220,10 @@
     n, height, _ = out_ref.shape
     rows = height - theirs_ref.shape[1]
     helped = meta_ref[PIXELS : PIXELS + 1, 0:BLOCK] != cap_blocks * BLOCK
-    out_ref[:, 0:rows] = own_ref[:, 0:rows]
-    for q in range(n):
+    for to, q in enumerate(list_group(n)):
         other = gate(helped[:, q : q + 1])
-        out_ref[q, rows:] = own_ref[q, rows:] + theirs_ref[q] * other
+        out_ref[to, 0:rows] = own_ref[q, 0:rows]
+        out_ref[to, rows:] = own_ref[q, rows:] + theirs_ref[q] * other
 
 
 def share(meta, own, theirs, cap_blocks):
@@ -246,7 +250,7 @@
     pltpu.sync_copy(frames_hbm, frames_ref)
     pltpu.sync_copy(cm_hbm, cm_ref)
     right = lax.broadcasted_iota(jnp.int32, (1, BLOCK), 1) >= BLOCK // 2
-    for q in range(n):
+    for to, q in enumerate(list_group(n)):
         counts = [[ref[row, q] for row in range(PIXELS + 1)] for ref in (meta_s, their_meta_s)]
         large, twice = left_out(*counts, cap_blocks * BLOCK)
         for i in range(cap_blocks):
@@ -255,7 +259,7 @@
             if i >= kept:
                 wanted |= twice & right if i == kept else twice
             valid = (cm_ref[pl.ds(block, 1), :] >= 0) & (i < meta_s[COUNT, q])
-            out_ref[q, i] = take(frames_ref, block) * gate(valid & wanted)
+            out_ref[to, i] = take(frames_ref, block) * gate(valid & wanted)
 
 
 def pack_rest(meta, their_meta, frames, cm, cap_blocks):
@@ -286,13 +290,13 @@
         slot = first + i
         padded[i, 0:PAD] = zero
         padded[i, PAD + total : 2 * PAD + total] = zero
-        for source in range(n):
+        for place, source in enumerate(list_group(n)):
             start = PAD + source * rows
             if slot < whole:
-                block = raw_ref[source, slot * rows : (slot + 1) * rows]
+                block = raw_ref[place, slot * rows : (slot + 1) * rows]
                 padded[i, start : start + rows] = block.astype(jnp.float32)
             else:
-                early, late = unfold(raw_ref[source, slot * rows : height], rows)
+                early, late = unfold(raw_ref[place, slot * rows : height], rows)
                 padded[i, start : start + rows // 2] = early
                 padded[i, start + rows // 2 : start + rows] = late
 
@@ -451,7 +455,14 @@
         return lax.ppermute(x, "pix", SWAP)
 
     def send(blocks):
-        return lax.all_to_all(blocks, "frame", split_axis=0, concat_axis=0, tiled=True)
+        return lax.all_to_all(
+            blocks,
+            "frame",
+            split_axis=0,
+            concat_axis=0,
+            axis_index_groups=[list_group(n)],
+            tiled=True,
+        )
 
     moving, meta, near_frames, near_cm = pack_move(cm, frames, cap_blocks)
     theirs = swap(moving)

time: 48 us -> 47.8 us (level); the launches traced: 47 us -> 47.4 us
  waiting for transfers between devices: 24.8 us -> 25.9 us
  starting transfers between devices: 10.9 us -> 10.2 us
    all_to_all x1, waiting for transfers between devices: 23.4 us -> 24.5 us  [send(): lax.all_to_all(blocks, 'frame', split_axis=0, concat_axis=0, axis_index_g...]
    ppermute x4, starting transfers between devices: 4.31 us -> 3.52 us  [swap(): return lax.ppermute(x, 'pix', SWAP)]
where the time goes in v9:
time: 47.8 us; the launch traced here: 47.4 us
  waiting for transfers between devices  25.9 us (54%)
  starting transfers between devices  10.2 us (21%)
  Pallas kernels  9.94 us (21%)
  between operations  0.71 us (1%)
  other arithmetic  0.64 us (1%)
    all_to_all x1, waiting for transfers between devices, send(): lax.all_to_all(blocks, 'frame', split_axis=0, concat_axis=0, axis_index_g...  24.5 us
    all_to_all x1, starting transfers between devices, send(): lax.all_to_all(blocks, 'frame', split_axis=0, concat_axis=0, axis_index_g...  6.64 us
    ppermute x4, starting transfers between devices, swap(): return lax.ppermute(x, 'pix', SWAP)  3.52 us
    pallas_call x1, Pallas kernels, pack_move(): call(functools.partial(move_kernel, cap_blocks), 'pack_move', [jax.ShapeD...  2.17 us
    pallas_call x2, Pallas kernels, partial_sums(): call(functools.partial(partial_kernel, len(normed)), 'partial_sums', sums...  1.81 us
    pallas_call x1, Pallas kernels, pack_own(): call(functools.partial(own_kernel, cap_blocks), 'pack_own', jax.ShapeDtyp...  1.8 us
    pallas_call x1, Pallas kernels, correlate(): call(result_kernel, 'correlate', pltpu.HBM((1, rows, total), jnp.bfloat16...  1.75 us
    ppermute x4, waiting for transfers between devices, swap(): return lax.ppermute(x, 'pix', SWAP)  1.42 us
  transfers between devices with their start and end apart: 5, of which 4 were waited for; matrix products, arithmetic and copies ran while one was open for 1% of the time, Pallas kernels for 9%

profile of v9, /device:TPU:11, one launch (start us, length us, event | category | flops | bytes accessed | tf_op | source)
XLA Modules:
  0.0 47.4 jit_solution(13089660359447782195)
XLA Ops:
  0.0 2.2 %pack_move.1 = (bf16[16,224,128]{2,1,0:T(8,128)(2,1)S(1)}, s32[8,128]{1,0:T(8,128)S(1)}, bf16[64,16384]{1,0:T(8,128)(2,1)S(1)}, s32[128,128]{1,0:T(8,128)S(1)}) custom-call(s32[128,128]{1,0:T(8,128)} %bitcast.4, bf16[64,16384]{1,0:T(8,128)(2,1)} %frames_hbm.1), custom_call_target="tpu_custom_call" | custom-call | tf_op jit(solution)/shard_map/pack_move/pallas_call | solution.py:156
  2.2 0.7 %collective-permute-start.1 = (bf16[16,224,128]{2,1,0:T(8,128)(2,1)S(1)}, bf16[16,224,128]{2,1,0:T(8,128)(2,1)S(1)}, u32[]{:S(2)}, u32[]{:S(2)}) collective-permute-start(bf16[16,224,128]{2,1,0:T(8,128)(2,1)S(1)} %get-tuple-element.58), channel_id=1, source_target_pairs={{0,1},{1,0},{2,3},{3,2},{4,5},{5,4},{6,7},{7,6},{8,9},{9,8},{10,11... | collective-permute-start | bytes 2752520 | tf_op jit(solution)/shard_map/ppermute | solution.py:455
  2.9 1.8 %pack_own.1.own_ref = bf16[16,288,128]{2,1,0:T(8,128)(2,1)S(1)} custom-call(s32[8,128]{1,0:T(8,128)S(1)} %get-tuple-element.59.meta_s.meta_ref, s32[128,128]{1,0:T(8,128)S(1)} %get-tuple-element.56.cm_ref, bf16[64,16384]{1,0:T(8,128)(2,1)S(1)} %get-tuple-element.57.frames_ref), custom_call_target="tpu_custom_call" | custom-call | bytes 4194304 | tf_op jit(solution)/shard_map/pack_own/pallas_call | solution.py:208
  4.7 0.3 collective-permute-done.1.theirs_ref
  5.0 1.3 %share.1 = bf16[16,288,128]{2,1,0:T(8,128)(2,1)} custom-call(s32[8,128]{1,0:T(8,128)S(1)} %get-tuple-element.59.meta_s.meta_ref, bf16[16,288,128]{2,1,0:T(8,128)(2,1)S(1)} %pack_own.1.own_ref, bf16[16,224,128]{2,1,0:T(8,128)(2,1)S(1)} %collective-permute-done.1.theirs_ref), custom_call_target="tpu_custom_call" | custom-call | bytes 4194304 | tf_op jit(solution)/shard_map/share/pallas_call | solution.py:230
  6.3 6.6 %all-to-all-start.1 = ((bf16[16,288,128]{2,1,0:T(8,128)(2,1)}), bf16[16,288,128]{2,1,0:T(8,128)(2,1)S(1)}, u32[]{:S(2)}, u32[]{:S(2)}) async-start(bf16[16,288,128]{2,1,0:T(8,128)(2,1)} %share.1), calls=%async_computation.1 | async-start | bytes 2359296 | tf_op jit(solution)/shard_map/all_to_all | solution.py:458
  13.0 0.9 %collective-permute-start.2 = (s32[8,128]{1,0:T(8,128)S(1)}, s32[8,128]{1,0:T(8,128)S(1)}, u32[]{:S(2)}, u32[]{:S(2)}) collective-permute-start(s32[8,128]{1,0:T(8,128)S(1)} %get-tuple-element.59.meta_s.meta_ref), channel_id=1, source_target_pairs={{0,1},{1,0},{2,3},{3,2},{4,5},{5,4},{6,7},{7,6},{8,9},{9,8},{10,11... | collective-permute-start | bytes 12296 | tf_op jit(solution)/shard_map/ppermute | solution.py:455
  13.9 0.8 %collective-permute-done.2 = s32[8,128]{1,0:T(8,128)S(1)} collective-permute-done((s32[8,128]{1,0:T(8,128)S(1)}, s32[8,128]{1,0:T(8,128)S(1)}, u32[]{:S(2)}, u32[]{:S(2)}) %collective-permute-start.2) | collective-permute-done | bytes 4128 | tf_op jit(solution)/shard_map/ppermute | solution.py:455
  14.7 0.6 %or_reduce_fusion = pred[]{:T(512)} fusion(s32[8,128]{1,0:T(8,128)S(1)} %collective-permute-done.2, s32[8,128]{1,0:T(8,128)S(1)} %get-tuple-element.59.meta_s.meta_ref), kind=kLoop, calls=%fused_computation | loop fusion | flops 255 | bytes 257 | tf_op jit(solution)/shard_map/reduce_or | solution.py:477
  16.0 24.5 %all-to-all-done.1.raw_ref = bf16[16,288,128]{2,1,0:T(8,128)(2,1)S(1)} async-done(((bf16[16,288,128]{2,1,0:T(8,128)(2,1)}), bf16[16,288,128]{2,1,0:T(8,128)(2,1)S(1)}, u32[]{:S(2)}, u32[]{:S(2)}) %all-to-all-start.1) | async-done | bytes 1179680 | tf_op jit(solution)/shard_map/all_to_all | solution.py:458
  40.5 0.6 %normalise.4.refs_0_ = bf16[1024,384]{1,0:T(8,128)(2,1)S(1)} custom-call(bf16[16,288,128]{2,1,0:T(8,128)(2,1)S(1)} %all-to-all-done.1.raw_ref, s32[1]{0:T(128)} %bitcast.2.refs_0_), custom_call_target="tpu_custom_call" | custom-call | flops 4718592 | bytes 1572864 | tf_op jit(solution)/shard_map/normalise/pallas_call | solution.py:334
  41.1 1.8 %collective-permute-start.4 = (bf16[1024,384]{1,0:T(8,128)(2,1)S(1)}, bf16[1024,384]{1,0:T(8,128)(2,1)S(1)}, u32[]{:S(2)}, u32[]{:S(2)}) collective-permute-start(bf16[1024,384]{1,0:T(8,128)(2,1)S(1)} %normalise.4.refs_0_), channel_id=1, source_target_pairs={{0,1},{1,0},{2,3},{3,2},{4,5},{5,4},{6,7},{7,6},{8,9},{9,8},{10,11... | collective-permute-start | bytes 2359304 | tf_op jit(solution)/shard_map/ppermute | solution.py:455
  42.9 0.5 %normalise.5.refs_1_ = bf16[1024,256]{1,0:T(8,128)(2,1)S(1)} custom-call(bf16[16,288,128]{2,1,0:T(8,128)(2,1)S(1)} %all-to-all-done.1.raw_ref, bf16[1024,384]{1,0:T(8,128)(2,1)S(1)} %normalise.4.refs_0_), custom_call_target="tpu_custom_call" | custom-call | flops 3145728 | bytes 1048576 | tf_op jit(solution)/shard_map/normalise/pallas_call | solution.py:334
  43.4 0.1 collective-permute-start.3
  43.5 1.0 %partial_sums.4 = (f32[512,1024]{1,0:T(8,128)S(1)}, f32[8,1024]{1,0:T(8,128)S(1)}) custom-call(bf16[1024,384]{1,0:T(8,128)(2,1)S(1)} %normalise.4.refs_0_, bf16[1024,256]{1,0:T(8,128)(2,1)S(1)} %normalise.5.refs_1_), custom_call_target="tpu_custom_call" | custom-call | flops 805306368 | bytes 2097152 | tf_op jit(solution)/shard_map/partial_sums/pallas_call | solution.py:386
  44.5 0.3 collective-permute-done.4.refs_0_
  44.8 0.8 %partial_sums.5 = (f32[512,1024]{1,0:T(8,128)S(1)}, f32[8,1024]{1,0:T(8,128)S(1)}) custom-call(bf16[1024,384]{1,0:T(8,128)(2,1)S(1)} %collective-permute-done.4.refs_0_, f32[512,1024]{1,0:T(8,128)S(1)} %get-tuple-element.60.refs_1_, f32[8,1024]{1,0:T(8,128)S(1)} %get-tuple-element.61.refs_2_), custom_call_target="tpu_custom_call" | custom-call | flops 402653184 | bytes 2097152 | tf_op jit(solution)/shard_map/partial_sums/pallas_call | solution.py:386
  45.6 0.0 collective-permute-done.3
  45.6 1.8 %conditional.1 = (bf16[1,512,1024]{2,1,0:T(8,128)(2,1)}) conditional(s32[]{:T(128)} %convert_element_type.4, (s32[8,128]{1,0:T(8,128)S(1)}, s32[8,128]{1,0:T(8,128)S(1)}, bf16[1024,256]{1,0:T(8,128)(2,1)S(1)}, f32[512,1024]{1,0:T(8,128)S(1)}, f32[8,1024]{1,0:T(8,128)S(1)}) %tuple.13, (s32[8,128]{1,0:T(8,128)S(1)}, s32[8,128]{1,0:T(8,128)S(1)}, ...), branch_computations={%region_1.0_spmd, %region_2.0_spmd} | conditional | flops 2428502016 | bytes 22020144 | solution.py:497
  45.6 1.8 %correlate.2 = bf16[1,512,1024]{2,1,0:T(8,128)(2,1)} custom-call(s32[8,128]{1,0:T(8,128)S(1)} %get-tuple-element.32.meta_ref, s32[8,128]{1,0:T(8,128)S(1)} %get-tuple-element.33.their_meta_ref, bf16[1024,256]{1,0:T(8,128)(2,1)S(1)} %get-tuple-element.34.normed_ref, f32[512,1024]{1,0:T(8,128)S(1)} %get-tuple-element.35.gram_in, ...), custom_call_target="tpu_custom_call" | custom-call | flops 268435456 | bytes 3145728 | tf_op jit(solution)/shard_map/cond/branch_0_fun/correlate/pallas_call | solution.py:428
Async XLA Ops:
  2.2 2.8 %collective-permute-start.1 = (bf16[16,224,128]{2,1,0:T(8,128)(2,1)S(1)}, bf16[16,224,128]{2,1,0:T(8,128)(2,1)S(1)}, u32[]{:S(2)}, u32[]{:S(2)}) collective-permute-start(bf16[16,224,128]{2,1,0:T(8,128)(2,1)S(1)} %get-tuple-element.58), channel_id=1, source_target_pairs={{0,1},{1,0},{2,3},{3,2},{4,5},{5,4},{6,7},{7,6},{8,9},{9,8},{10,11... | collective-permute-start | bytes 2752520 | tf_op jit(solution)/shard_map/ppermute | solution.py:455
  6.3 34.2 %all-to-all-start.1 = ((bf16[16,288,128]{2,1,0:T(8,128)(2,1)}), bf16[16,288,128]{2,1,0:T(8,128)(2,1)S(1)}, u32[]{:S(2)}, u32[]{:S(2)}) async-start(bf16[16,288,128]{2,1,0:T(8,128)(2,1)} %share.1), calls=%async_computation.1 | async-start | bytes 2359296 | tf_op jit(solution)/shard_map/all_to_all | solution.py:458
  13.0 1.8 %collective-permute-start.2 = (s32[8,128]{1,0:T(8,128)S(1)}, s32[8,128]{1,0:T(8,128)S(1)}, u32[]{:S(2)}, u32[]{:S(2)}) collective-permute-start(s32[8,128]{1,0:T(8,128)S(1)} %get-tuple-element.59.meta_s.meta_ref), channel_id=1, source_target_pairs={{0,1},{1,0},{2,3},{3,2},{4,5},{5,4},{6,7},{7,6},{8,9},{9,8},{10,11... | collective-permute-start | bytes 12296 | tf_op jit(solution)/shard_map/ppermute | solution.py:455
  41.1 3.7 %collective-permute-start.4 = (bf16[1024,384]{1,0:T(8,128)(2,1)S(1)}, bf16[1024,384]{1,0:T(8,128)(2,1)S(1)}, u32[]{:S(2)}, u32[]{:S(2)}) collective-permute-start(bf16[1024,384]{1,0:T(8,128)(2,1)S(1)} %normalise.4.refs_0_), channel_id=1, source_target_pairs={{0,1},{1,0},{2,3},{3,2},{4,5},{5,4},{6,7},{7,6},{8,9},{9,8},{10,11... | collective-permute-start | bytes 2359304 | tf_op jit(solution)/shard_map/ppermute | solution.py:455
  43.4 2.2 %collective-permute-start.3 = (bf16[1024,256]{1,0:T(8,128)(2,1)S(1)}, bf16[1024,256]{1,0:T(8,128)(2,1)S(1)}, u32[]{:S(2)}, u32[]{:S(2)}) collective-permute-start(bf16[1024,256]{1,0:T(8,128)(2,1)S(1)} %normalise.5.refs_1_), channel_id=1, source_target_pairs={{0,1},{1,0},{2,3},{3,2},{4,5},{5,4},{6,7},{7,6},{8,9},{9,8},{10,11... | collective-permute-start | bytes 1572872 | tf_op jit(solution)/shard_map/ppermute | solution.py:455

commit v10 on v9

--- a/solution.py
+++ b/solution.py
@@ -39,7 +39,9 @@
 
 
 def list_group(n):
-    return sorted(range(n), key=lambda i: (i >= n // 2, i % 2 if i < n // 2 else 0, i))
+    side = n // 4
+    order = sorted(range(n // 2), key=lambda i: (i % side >= side // 2, i))
+    return order + list(range(n // 2, n))
 
 
 def count_half_rows(rows):

time: 47.8 us -> 47.7 us (level)
  the two profiles are of different devices: /device:TPU:11 before, /device:TPU:5 now
where the time goes in v10:
time: 47.7 us; the launch traced here: 47.5 us
  waiting for transfers between devices  25.2 us (53%)
  starting transfers between devices  11 us (23%)
  Pallas kernels  9.94 us (21%)
  between operations  0.71 us (1%)
  other arithmetic  0.64 us (1%)
    all_to_all x1, waiting for transfers between devices, send(): lax.all_to_all(blocks, 'frame', split_axis=0, concat_axis=0, axis_index_g...  23.8 us
    all_to_all x1, starting transfers between devices, send(): lax.all_to_all(blocks, 'frame', split_axis=0, concat_axis=0, axis_index_g...  6.72 us
    ppermute x4, starting transfers between devices, swap(): return lax.ppermute(x, 'pix', SWAP)  4.32 us
    pallas_call x1, Pallas kernels, pack_move(): call(functools.partial(move_kernel, cap_blocks), 'pack_move', [jax.ShapeD...  2.16 us
    pallas_call x2, Pallas kernels, partial_sums(): call(functools.partial(partial_kernel, len(normed)), 'partial_sums', sums...  1.81 us
    pallas_call x1, Pallas kernels, pack_own(): call(functools.partial(own_kernel, cap_blocks), 'pack_own', jax.ShapeDtyp...  1.8 us
    pallas_call x1, Pallas kernels, correlate(): call(result_kernel, 'correlate', pltpu.HBM((1, rows, total), jnp.bfloat16...  1.75 us
    ppermute x4, waiting for transfers between devices, swap(): return lax.ppermute(x, 'pix', SWAP)  1.42 us
  transfers between devices with their start and end apart: 5, of which 4 were waited for; matrix products, arithmetic and copies ran while one was open for 1% of the time, Pallas kernels for 9%

profile of v10, /device:TPU:5, one launch (start us, length us, event | category | flops | bytes accessed | tf_op | source)
XLA Modules:
  0.0 47.5 jit_solution(342025655117182598)
XLA Ops:
  0.0 2.2 %pack_move.1 = (bf16[16,224,128]{2,1,0:T(8,128)(2,1)S(1)}, s32[8,128]{1,0:T(8,128)S(1)}, bf16[64,16384]{1,0:T(8,128)(2,1)S(1)}, s32[128,128]{1,0:T(8,128)S(1)}) custom-call(s32[128,128]{1,0:T(8,128)} %bitcast.4, bf16[64,16384]{1,0:T(8,128)(2,1)} %frames_hbm.1), custom_call_target="tpu_custom_call" | custom-call | tf_op jit(solution)/shard_map/pack_move/pallas_call | solution.py:158
  2.2 0.7 %collective-permute-start.1 = (bf16[16,224,128]{2,1,0:T(8,128)(2,1)S(1)}, bf16[16,224,128]{2,1,0:T(8,128)(2,1)S(1)}, u32[]{:S(2)}, u32[]{:S(2)}) collective-permute-start(bf16[16,224,128]{2,1,0:T(8,128)(2,1)S(1)} %get-tuple-element.58), channel_id=1, source_target_pairs={{0,1},{1,0},{2,3},{3,2},{4,5},{5,4},{6,7},{7,6},{8,9},{9,8},{10,11... | collective-permute-start | bytes 2752520 | tf_op jit(solution)/shard_map/ppermute | solution.py:457
  2.9 1.8 %pack_own.1.own_ref = bf16[16,288,128]{2,1,0:T(8,128)(2,1)S(1)} custom-call(s32[8,128]{1,0:T(8,128)S(1)} %get-tuple-element.59.meta_s.meta_ref, s32[128,128]{1,0:T(8,128)S(1)} %get-tuple-element.56.cm_ref, bf16[64,16384]{1,0:T(8,128)(2,1)S(1)} %get-tuple-element.57.frames_ref), custom_call_target="tpu_custom_call" | custom-call | bytes 4194304 | tf_op jit(solution)/shard_map/pack_own/pallas_call | solution.py:210
  4.7 0.3 collective-permute-done.1.theirs_ref
  5.0 1.3 %share.1 = bf16[16,288,128]{2,1,0:T(8,128)(2,1)} custom-call(s32[8,128]{1,0:T(8,128)S(1)} %get-tuple-element.59.meta_s.meta_ref, bf16[16,288,128]{2,1,0:T(8,128)(2,1)S(1)} %pack_own.1.own_ref, bf16[16,224,128]{2,1,0:T(8,128)(2,1)S(1)} %collective-permute-done.1.theirs_ref), custom_call_target="tpu_custom_call" | custom-call | bytes 4194304 | tf_op jit(solution)/shard_map/share/pallas_call | solution.py:232
  6.3 6.7 %all-to-all-start.1 = ((bf16[16,288,128]{2,1,0:T(8,128)(2,1)}), bf16[16,288,128]{2,1,0:T(8,128)(2,1)S(1)}, u32[]{:S(2)}, u32[]{:S(2)}) async-start(bf16[16,288,128]{2,1,0:T(8,128)(2,1)} %share.1), calls=%async_computation.1 | async-start | bytes 2359296 | tf_op jit(solution)/shard_map/all_to_all | solution.py:460
  13.0 0.9 %collective-permute-start.2 = (s32[8,128]{1,0:T(8,128)S(1)}, s32[8,128]{1,0:T(8,128)S(1)}, u32[]{:S(2)}, u32[]{:S(2)}) collective-permute-start(s32[8,128]{1,0:T(8,128)S(1)} %get-tuple-element.59.meta_s.meta_ref), channel_id=1, source_target_pairs={{0,1},{1,0},{2,3},{3,2},{4,5},{5,4},{6,7},{7,6},{8,9},{9,8},{10,11... | collective-permute-start | bytes 12296 | tf_op jit(solution)/shard_map/ppermute | solution.py:457
  14.0 0.8 %collective-permute-done.2 = s32[8,128]{1,0:T(8,128)S(1)} collective-permute-done((s32[8,128]{1,0:T(8,128)S(1)}, s32[8,128]{1,0:T(8,128)S(1)}, u32[]{:S(2)}, u32[]{:S(2)}) %collective-permute-start.2) | collective-permute-done | bytes 4128 | tf_op jit(solution)/shard_map/ppermute | solution.py:457
  14.8 0.6 %or_reduce_fusion = pred[]{:T(512)} fusion(s32[8,128]{1,0:T(8,128)S(1)} %collective-permute-done.2, s32[8,128]{1,0:T(8,128)S(1)} %get-tuple-element.59.meta_s.meta_ref), kind=kLoop, calls=%fused_computation | loop fusion | flops 255 | bytes 257 | tf_op jit(solution)/shard_map/reduce_or | solution.py:479
  16.1 23.8 %all-to-all-done.1.raw_ref = bf16[16,288,128]{2,1,0:T(8,128)(2,1)S(1)} async-done(((bf16[16,288,128]{2,1,0:T(8,128)(2,1)}), bf16[16,288,128]{2,1,0:T(8,128)(2,1)S(1)}, u32[]{:S(2)}, u32[]{:S(2)}) %all-to-all-start.1) | async-done | bytes 1179680 | tf_op jit(solution)/shard_map/all_to_all | solution.py:460
  39.9 0.6 %normalise.4.refs_0_ = bf16[1024,384]{1,0:T(8,128)(2,1)S(1)} custom-call(bf16[16,288,128]{2,1,0:T(8,128)(2,1)S(1)} %all-to-all-done.1.raw_ref, s32[1]{0:T(128)} %bitcast.2.refs_0_), custom_call_target="tpu_custom_call" | custom-call | flops 4718592 | bytes 1572864 | tf_op jit(solution)/shard_map/normalise/pallas_call | solution.py:336
  40.5 2.6 %collective-permute-start.4 = (bf16[1024,384]{1,0:T(8,128)(2,1)S(1)}, bf16[1024,384]{1,0:T(8,128)(2,1)S(1)}, u32[]{:S(2)}, u32[]{:S(2)}) collective-permute-start(bf16[1024,384]{1,0:T(8,128)(2,1)S(1)} %normalise.4.refs_0_), channel_id=1, source_target_pairs={{0,1},{1,0},{2,3},{3,2},{4,5},{5,4},{6,7},{7,6},{8,9},{9,8},{10,11... | collective-permute-start | bytes 2359304 | tf_op jit(solution)/shard_map/ppermute | solution.py:457
  43.1 0.5 %normalise.5.refs_1_ = bf16[1024,256]{1,0:T(8,128)(2,1)S(1)} custom-call(bf16[16,288,128]{2,1,0:T(8,128)(2,1)S(1)} %all-to-all-done.1.raw_ref, bf16[1024,384]{1,0:T(8,128)(2,1)S(1)} %normalise.4.refs_0_), custom_call_target="tpu_custom_call" | custom-call | flops 3145728 | bytes 1048576 | tf_op jit(solution)/shard_map/normalise/pallas_call | solution.py:336
  43.6 0.1 collective-permute-start.3
  43.6 1.0 %partial_sums.4 = (f32[512,1024]{1,0:T(8,128)S(1)}, f32[8,1024]{1,0:T(8,128)S(1)}) custom-call(bf16[1024,384]{1,0:T(8,128)(2,1)S(1)} %normalise.4.refs_0_, bf16[1024,256]{1,0:T(8,128)(2,1)S(1)} %normalise.5.refs_1_), custom_call_target="tpu_custom_call" | custom-call | flops 805306368 | bytes 2097152 | tf_op jit(solution)/shard_map/partial_sums/pallas_call | solution.py:388
  44.7 0.3 collective-permute-done.4.refs_0_
  45.0 0.8 %partial_sums.5 = (f32[512,1024]{1,0:T(8,128)S(1)}, f32[8,1024]{1,0:T(8,128)S(1)}) custom-call(bf16[1024,384]{1,0:T(8,128)(2,1)S(1)} %collective-permute-done.4.refs_0_, f32[512,1024]{1,0:T(8,128)S(1)} %get-tuple-element.60.refs_1_, f32[8,1024]{1,0:T(8,128)S(1)} %get-tuple-element.61.refs_2_), custom_call_target="tpu_custom_call" | custom-call | flops 402653184 | bytes 2097152 | tf_op jit(solution)/shard_map/partial_sums/pallas_call | solution.py:388
  45.8 0.0 collective-permute-done.3
  45.8 1.8 %conditional.1 = (bf16[1,512,1024]{2,1,0:T(8,128)(2,1)}) conditional(s32[]{:T(128)} %convert_element_type.4, (s32[8,128]{1,0:T(8,128)S(1)}, s32[8,128]{1,0:T(8,128)S(1)}, bf16[1024,256]{1,0:T(8,128)(2,1)S(1)}, f32[512,1024]{1,0:T(8,128)S(1)}, f32[8,1024]{1,0:T(8,128)S(1)}) %tuple.13, (s32[8,128]{1,0:T(8,128)S(1)}, s32[8,128]{1,0:T(8,128)S(1)}, ...), branch_computations={%region_1.0_spmd, %region_2.0_spmd} | conditional | flops 2428502016 | bytes 22020144 | solution.py:499
  45.8 1.8 %correlate.2 = bf16[1,512,1024]{2,1,0:T(8,128)(2,1)} custom-call(s32[8,128]{1,0:T(8,128)S(1)} %get-tuple-element.32.meta_ref, s32[8,128]{1,0:T(8,128)S(1)} %get-tuple-element.33.their_meta_ref, bf16[1024,256]{1,0:T(8,128)(2,1)S(1)} %get-tuple-element.34.normed_ref, f32[512,1024]{1,0:T(8,128)S(1)} %get-tuple-element.35.gram_in, ...), custom_call_target="tpu_custom_call" | custom-call | flops 268435456 | bytes 3145728 | tf_op jit(solution)/shard_map/cond/branch_0_fun/correlate/pallas_call | solution.py:430
Async XLA Ops:
  2.2 2.8 %collective-permute-start.1 = (bf16[16,224,128]{2,1,0:T(8,128)(2,1)S(1)}, bf16[16,224,128]{2,1,0:T(8,128)(2,1)S(1)}, u32[]{:S(2)}, u32[]{:S(2)}) collective-permute-start(bf16[16,224,128]{2,1,0:T(8,128)(2,1)S(1)} %get-tuple-element.58), channel_id=1, source_target_pairs={{0,1},{1,0},{2,3},{3,2},{4,5},{5,4},{6,7},{7,6},{8,9},{9,8},{10,11... | collective-permute-start | bytes 2752520 | tf_op jit(solution)/shard_map/ppermute | solution.py:457
  6.3 33.5 %all-to-all-start.1 = ((bf16[16,288,128]{2,1,0:T(8,128)(2,1)}), bf16[16,288,128]{2,1,0:T(8,128)(2,1)S(1)}, u32[]{:S(2)}, u32[]{:S(2)}) async-start(bf16[16,288,128]{2,1,0:T(8,128)(2,1)} %share.1), calls=%async_computation.1 | async-start | bytes 2359296 | tf_op jit(solution)/shard_map/all_to_all | solution.py:460
  13.0 1.8 %collective-permute-start.2 = (s32[8,128]{1,0:T(8,128)S(1)}, s32[8,128]{1,0:T(8,128)S(1)}, u32[]{:S(2)}, u32[]{:S(2)}) collective-permute-start(s32[8,128]{1,0:T(8,128)S(1)} %get-tuple-element.59.meta_s.meta_ref), channel_id=1, source_target_pairs={{0,1},{1,0},{2,3},{3,2},{4,5},{5,4},{6,7},{7,6},{8,9},{9,8},{10,11... | collective-permute-start | bytes 12296 | tf_op jit(solution)/shard_map/ppermute | solution.py:457
  40.5 4.5 %collective-permute-start.4 = (bf16[1024,384]{1,0:T(8,128)(2,1)S(1)}, bf16[1024,384]{1,0:T(8,128)(2,1)S(1)}, u32[]{:S(2)}, u32[]{:S(2)}) collective-permute-start(bf16[1024,384]{1,0:T(8,128)(2,1)S(1)} %normalise.4.refs_0_), channel_id=1, source_target_pairs={{0,1},{1,0},{2,3},{3,2},{4,5},{5,4},{6,7},{7,6},{8,9},{9,8},{10,11... | collective-permute-start | bytes 2359304 | tf_op jit(solution)/shard_map/ppermute | solution.py:457
  43.6 2.2 %collective-permute-start.3 = (bf16[1024,256]{1,0:T(8,128)(2,1)S(1)}, bf16[1024,256]{1,0:T(8,128)(2,1)S(1)}, u32[]{:S(2)}, u32[]{:S(2)}) collective-permute-start(bf16[1024,256]{1,0:T(8,128)(2,1)S(1)} %normalise.5.refs_1_), channel_id=1, source_target_pairs={{0,1},{1,0},{2,3},{3,2},{4,5},{5,4},{6,7},{7,6},{8,9},{9,8},{10,11... | collective-permute-start | bytes 1572872 | tf_op jit(solution)/shard_map/ppermute | solution.py:457

commit v11 on v9

--- a/solution.py
+++ b/solution.py
@@ -39,7 +39,9 @@
 
 
 def list_group(n):
-    return sorted(range(n), key=lambda i: (i >= n // 2, i % 2 if i < n // 2 else 0, i))
+    half, side = n // 2, n // 4
+    first = sorted(range(half), key=lambda i: (i % 2, i))
+    return first + sorted(range(half, n), key=lambda i: (i % side >= side // 2, i))
 
 
 def count_half_rows(rows):

time: 47.8 us -> 47.8 us (level)
  no operation moved by 1% of the time
where the time goes in v11:
time: 47.8 us; the launch traced here: 47.4 us
  waiting for transfers between devices  25.9 us (54%)
  starting transfers between devices  10.2 us (21%)
  Pallas kernels  9.93 us (21%)
  between operations  0.71 us (1%)
  other arithmetic  0.64 us (1%)
    all_to_all x1, waiting for transfers between devices, send(): lax.all_to_all(blocks, 'frame', split_axis=0, concat_axis=0, axis_index_g...  24.5 us
    all_to_all x1, starting transfers between devices, send(): lax.all_to_all(blocks, 'frame', split_axis=0, concat_axis=0, axis_index_g...  6.64 us
    ppermute x4, starting transfers between devices, swap(): return lax.ppermute(x, 'pix', SWAP)  3.52 us
    pallas_call x1, Pallas kernels, pack_move(): call(functools.partial(move_kernel, cap_blocks), 'pack_move', [jax.ShapeD...  2.16 us
    pallas_call x2, Pallas kernels, partial_sums(): call(functools.partial(partial_kernel, len(normed)), 'partial_sums', sums...  1.81 us
    pallas_call x1, Pallas kernels, pack_own(): call(functools.partial(own_kernel, cap_blocks), 'pack_own', jax.ShapeDtyp...  1.8 us
    pallas_call x1, Pallas kernels, correlate(): call(result_kernel, 'correlate', pltpu.HBM((1, rows, total), jnp.bfloat16...  1.75 us
    ppermute x4, waiting for transfers between devices, swap(): return lax.ppermute(x, 'pix', SWAP)  1.42 us
  transfers between devices with their start and end apart: 5, of which 4 were waited for; matrix products, arithmetic and copies ran while one was open for 1% of the time, Pallas kernels for 9%

profile of v11, /device:TPU:11, one launch (start us, length us, event | category | flops | bytes accessed | tf_op | source)
XLA Modules:
  0.0 47.4 jit_solution(15310664874012305928)
XLA Ops:
  0.0 2.2 %pack_move.1 = (bf16[16,224,128]{2,1,0:T(8,128)(2,1)S(1)}, s32[8,128]{1,0:T(8,128)S(1)}, bf16[64,16384]{1,0:T(8,128)(2,1)S(1)}, s32[128,128]{1,0:T(8,128)S(1)}) custom-call(s32[128,128]{1,0:T(8,128)} %bitcast.4, bf16[64,16384]{1,0:T(8,128)(2,1)} %frames_hbm.1), custom_call_target="tpu_custom_call" | custom-call | tf_op jit(solution)/shard_map/pack_move/pallas_call | solution.py:158
  2.2 0.7 %collective-permute-start.1 = (bf16[16,224,128]{2,1,0:T(8,128)(2,1)S(1)}, bf16[16,224,128]{2,1,0:T(8,128)(2,1)S(1)}, u32[]{:S(2)}, u32[]{:S(2)}) collective-permute-start(bf16[16,224,128]{2,1,0:T(8,128)(2,1)S(1)} %get-tuple-element.58), channel_id=1, source_target_pairs={{0,1},{1,0},{2,3},{3,2},{4,5},{5,4},{6,7},{7,6},{8,9},{9,8},{10,11... | collective-permute-start | bytes 2752520 | tf_op jit(solution)/shard_map/ppermute | solution.py:457
  2.9 1.8 %pack_own.1.own_ref = bf16[16,288,128]{2,1,0:T(8,128)(2,1)S(1)} custom-call(s32[8,128]{1,0:T(8,128)S(1)} %get-tuple-element.59.meta_s.meta_ref, s32[128,128]{1,0:T(8,128)S(1)} %get-tuple-element.56.cm_ref, bf16[64,16384]{1,0:T(8,128)(2,1)S(1)} %get-tuple-element.57.frames_ref), custom_call_target="tpu_custom_call" | custom-call | bytes 4194304 | tf_op jit(solution)/shard_map/pack_own/pallas_call | solution.py:210
  4.7 0.3 collective-permute-done.1.theirs_ref
  5.0 1.3 %share.1 = bf16[16,288,128]{2,1,0:T(8,128)(2,1)} custom-call(s32[8,128]{1,0:T(8,128)S(1)} %get-tuple-element.59.meta_s.meta_ref, bf16[16,288,128]{2,1,0:T(8,128)(2,1)S(1)} %pack_own.1.own_ref, bf16[16,224,128]{2,1,0:T(8,128)(2,1)S(1)} %collective-permute-done.1.theirs_ref), custom_call_target="tpu_custom_call" | custom-call | bytes 4194304 | tf_op jit(solution)/shard_map/share/pallas_call | solution.py:232
  6.3 6.6 %all-to-all-start.1 = ((bf16[16,288,128]{2,1,0:T(8,128)(2,1)}), bf16[16,288,128]{2,1,0:T(8,128)(2,1)S(1)}, u32[]{:S(2)}, u32[]{:S(2)}) async-start(bf16[16,288,128]{2,1,0:T(8,128)(2,1)} %share.1), calls=%async_computation.1 | async-start | bytes 2359296 | tf_op jit(solution)/shard_map/all_to_all | solution.py:460
  13.0 0.9 %collective-permute-start.2 = (s32[8,128]{1,0:T(8,128)S(1)}, s32[8,128]{1,0:T(8,128)S(1)}, u32[]{:S(2)}, u32[]{:S(2)}) collective-permute-start(s32[8,128]{1,0:T(8,128)S(1)} %get-tuple-element.59.meta_s.meta_ref), channel_id=1, source_target_pairs={{0,1},{1,0},{2,3},{3,2},{4,5},{5,4},{6,7},{7,6},{8,9},{9,8},{10,11... | collective-permute-start | bytes 12296 | tf_op jit(solution)/shard_map/ppermute | solution.py:457
  13.9 0.8 %collective-permute-done.2 = s32[8,128]{1,0:T(8,128)S(1)} collective-permute-done((s32[8,128]{1,0:T(8,128)S(1)}, s32[8,128]{1,0:T(8,128)S(1)}, u32[]{:S(2)}, u32[]{:S(2)}) %collective-permute-start.2) | collective-permute-done | bytes 4128 | tf_op jit(solution)/shard_map/ppermute | solution.py:457
  14.7 0.6 %or_reduce_fusion = pred[]{:T(512)} fusion(s32[8,128]{1,0:T(8,128)S(1)} %collective-permute-done.2, s32[8,128]{1,0:T(8,128)S(1)} %get-tuple-element.59.meta_s.meta_ref), kind=kLoop, calls=%fused_computation | loop fusion | flops 255 | bytes 257 | tf_op jit(solution)/shard_map/reduce_or | solution.py:479
  16.0 24.5 %all-to-all-done.1.raw_ref = bf16[16,288,128]{2,1,0:T(8,128)(2,1)S(1)} async-done(((bf16[16,288,128]{2,1,0:T(8,128)(2,1)}), bf16[16,288,128]{2,1,0:T(8,128)(2,1)S(1)}, u32[]{:S(2)}, u32[]{:S(2)}) %all-to-all-start.1) | async-done | bytes 1179680 | tf_op jit(solution)/shard_map/all_to_all | solution.py:460
  40.5 0.6 %normalise.4.refs_0_ = bf16[1024,384]{1,0:T(8,128)(2,1)S(1)} custom-call(bf16[16,288,128]{2,1,0:T(8,128)(2,1)S(1)} %all-to-all-done.1.raw_ref, s32[1]{0:T(128)} %bitcast.2.refs_0_), custom_call_target="tpu_custom_call" | custom-call | flops 4718592 | bytes 1572864 | tf_op jit(solution)/shard_map/normalise/pallas_call | solution.py:336
  41.1 1.8 %collective-permute-start.4 = (bf16[1024,384]{1,0:T(8,128)(2,1)S(1)}, bf16[1024,384]{1,0:T(8,128)(2,1)S(1)}, u32[]{:S(2)}, u32[]{:S(2)}) collective-permute-start(bf16[1024,384]{1,0:T(8,128)(2,1)S(1)} %normalise.4.refs_0_), channel_id=1, source_target_pairs={{0,1},{1,0},{2,3},{3,2},{4,5},{5,4},{6,7},{7,6},{8,9},{9,8},{10,11... | collective-permute-start | bytes 2359304 | tf_op jit(solution)/shard_map/ppermute | solution.py:457
  42.9 0.5 %normalise.5.refs_1_ = bf16[1024,256]{1,0:T(8,128)(2,1)S(1)} custom-call(bf16[16,288,128]{2,1,0:T(8,128)(2,1)S(1)} %all-to-all-done.1.raw_ref, bf16[1024,384]{1,0:T(8,128)(2,1)S(1)} %normalise.4.refs_0_), custom_call_target="tpu_custom_call" | custom-call | flops 3145728 | bytes 1048576 | tf_op jit(solution)/shard_map/normalise/pallas_call | solution.py:336
  43.4 0.1 collective-permute-start.3
  43.5 1.0 %partial_sums.4 = (f32[512,1024]{1,0:T(8,128)S(1)}, f32[8,1024]{1,0:T(8,128)S(1)}) custom-call(bf16[1024,384]{1,0:T(8,128)(2,1)S(1)} %normalise.4.refs_0_, bf16[1024,256]{1,0:T(8,128)(2,1)S(1)} %normalise.5.refs_1_), custom_call_target="tpu_custom_call" | custom-call | flops 805306368 | bytes 2097152 | tf_op jit(solution)/shard_map/partial_sums/pallas_call | solution.py:388
  44.5 0.3 collective-permute-done.4.refs_0_
  44.8 0.8 %partial_sums.5 = (f32[512,1024]{1,0:T(8,128)S(1)}, f32[8,1024]{1,0:T(8,128)S(1)}) custom-call(bf16[1024,384]{1,0:T(8,128)(2,1)S(1)} %collective-permute-done.4.refs_0_, f32[512,1024]{1,0:T(8,128)S(1)} %get-tuple-element.60.refs_1_, f32[8,1024]{1,0:T(8,128)S(1)} %get-tuple-element.61.refs_2_), custom_call_target="tpu_custom_call" | custom-call | flops 402653184 | bytes 2097152 | tf_op jit(solution)/shard_map/partial_sums/pallas_call | solution.py:388
  45.6 0.0 collective-permute-done.3
  45.6 1.8 %conditional.1 = (bf16[1,512,1024]{2,1,0:T(8,128)(2,1)}) conditional(s32[]{:T(128)} %convert_element_type.4, (s32[8,128]{1,0:T(8,128)S(1)}, s32[8,128]{1,0:T(8,128)S(1)}, bf16[1024,256]{1,0:T(8,128)(2,1)S(1)}, f32[512,1024]{1,0:T(8,128)S(1)}, f32[8,1024]{1,0:T(8,128)S(1)}) %tuple.13, (s32[8,128]{1,0:T(8,128)S(1)}, s32[8,128]{1,0:T(8,128)S(1)}, ...), branch_computations={%region_1.0_spmd, %region_2.0_spmd} | conditional | flops 2428502016 | bytes 22020144 | solution.py:499
  45.6 1.7 %correlate.2 = bf16[1,512,1024]{2,1,0:T(8,128)(2,1)} custom-call(s32[8,128]{1,0:T(8,128)S(1)} %get-tuple-element.32.meta_ref, s32[8,128]{1,0:T(8,128)S(1)} %get-tuple-element.33.their_meta_ref, bf16[1024,256]{1,0:T(8,128)(2,1)S(1)} %get-tuple-element.34.normed_ref, f32[512,1024]{1,0:T(8,128)S(1)} %get-tuple-element.35.gram_in, ...), custom_call_target="tpu_custom_call" | custom-call | flops 268435456 | bytes 3145728 | tf_op jit(solution)/shard_map/cond/branch_0_fun/correlate/pallas_call | solution.py:430
Async XLA Ops:
  2.2 2.8 %collective-permute-start.1 = (bf16[16,224,128]{2,1,0:T(8,128)(2,1)S(1)}, bf16[16,224,128]{2,1,0:T(8,128)(2,1)S(1)}, u32[]{:S(2)}, u32[]{:S(2)}) collective-permute-start(bf16[16,224,128]{2,1,0:T(8,128)(2,1)S(1)} %get-tuple-element.58), channel_id=1, source_target_pairs={{0,1},{1,0},{2,3},{3,2},{4,5},{5,4},{6,7},{7,6},{8,9},{9,8},{10,11... | collective-permute-start | bytes 2752520 | tf_op jit(solution)/shard_map/ppermute | solution.py:457
  6.3 34.2 %all-to-all-start.1 = ((bf16[16,288,128]{2,1,0:T(8,128)(2,1)}), bf16[16,288,128]{2,1,0:T(8,128)(2,1)S(1)}, u32[]{:S(2)}, u32[]{:S(2)}) async-start(bf16[16,288,128]{2,1,0:T(8,128)(2,1)} %share.1), calls=%async_computation.1 | async-start | bytes 2359296 | tf_op jit(solution)/shard_map/all_to_all | solution.py:460
  13.0 1.8 %collective-permute-start.2 = (s32[8,128]{1,0:T(8,128)S(1)}, s32[8,128]{1,0:T(8,128)S(1)}, u32[]{:S(2)}, u32[]{:S(2)}) collective-permute-start(s32[8,128]{1,0:T(8,128)S(1)} %get-tuple-element.59.meta_s.meta_ref), channel_id=1, source_target_pairs={{0,1},{1,0},{2,3},{3,2},{4,5},{5,4},{6,7},{7,6},{8,9},{9,8},{10,11... | collective-permute-start | bytes 12296 | tf_op jit(solution)/shard_map/ppermute | solution.py:457
  41.1 3.7 %collective-permute-start.4 = (bf16[1024,384]{1,0:T(8,128)(2,1)S(1)}, bf16[1024,384]{1,0:T(8,128)(2,1)S(1)}, u32[]{:S(2)}, u32[]{:S(2)}) collective-permute-start(bf16[1024,384]{1,0:T(8,128)(2,1)S(1)} %normalise.4.refs_0_), channel_id=1, source_target_pairs={{0,1},{1,0},{2,3},{3,2},{4,5},{5,4},{6,7},{7,6},{8,9},{9,8},{10,11... | collective-permute-start | bytes 2359304 | tf_op jit(solution)/shard_map/ppermute | solution.py:457
  43.4 2.2 %collective-permute-start.3 = (bf16[1024,256]{1,0:T(8,128)(2,1)S(1)}, bf16[1024,256]{1,0:T(8,128)(2,1)S(1)}, u32[]{:S(2)}, u32[]{:S(2)}) collective-permute-start(bf16[1024,256]{1,0:T(8,128)(2,1)S(1)} %normalise.5.refs_1_), channel_id=1, source_target_pairs={{0,1},{1,0},{2,3},{3,2},{4,5},{5,4},{6,7},{7,6},{8,9},{9,8},{10,11... | collective-permute-start | bytes 1572872 | tf_op jit(solution)/shard_map/ppermute | solution.py:457

commit v12 on v11

--- a/solution.py
+++ b/solution.py
@@ -40,7 +40,7 @@
 
 def list_group(n):
     half, side = n // 2, n // 4
-    first = sorted(range(half), key=lambda i: (i % 2, i))
+    first = sorted(range(half), key=lambda i: (i % side >= side - side // 4, i))
     return first + sorted(range(half, n), key=lambda i: (i % side >= side // 2, i))
 
 

time: 47.8 us -> 48.2 us (level)
  the two profiles are of different devices: /device:TPU:11 before, /device:TPU:19 now
where the time goes in v12:
time: 48.2 us; the launch traced here: 48 us
  waiting for transfers between devices  27.9 us (58%)
  Pallas kernels  9.94 us (21%)
  starting transfers between devices  8.84 us (18%)
  between operations  0.71 us (1%)
  other arithmetic  0.64 us (1%)
    all_to_all x1, waiting for transfers between devices, send(): lax.all_to_all(blocks, 'frame', split_axis=0, concat_axis=0, axis_index_g...  26.4 us
    all_to_all x1, starting transfers between devices, send(): lax.all_to_all(blocks, 'frame', split_axis=0, concat_axis=0, axis_index_g...  6.52 us
    ppermute x4, starting transfers between devices, swap(): return lax.ppermute(x, 'pix', SWAP)  2.32 us
    pallas_call x1, Pallas kernels, pack_move(): call(functools.partial(move_kernel, cap_blocks), 'pack_move', [jax.ShapeD...  2.16 us
    pallas_call x2, Pallas kernels, partial_sums(): call(functools.partial(partial_kernel, len(normed)), 'partial_sums', sums...  1.81 us
    pallas_call x1, Pallas kernels, pack_own(): call(functools.partial(own_kernel, cap_blocks), 'pack_own', jax.ShapeDtyp...  1.8 us
    pallas_call x1, Pallas kernels, correlate(): call(result_kernel, 'correlate', pltpu.HBM((1, rows, total), jnp.bfloat16...  1.75 us
    ppermute x4, waiting for transfers between devices, swap(): return lax.ppermute(x, 'pix', SWAP)  1.42 us
  transfers between devices with their start and end apart: 5, of which 4 were waited for; matrix products, arithmetic and copies ran while one was open for 1% of the time, Pallas kernels for 9%

profile of v12, /device:TPU:19, one launch (start us, length us, event | category | flops | bytes accessed | tf_op | source)
XLA Modules:
  0.0 48.0 jit_solution(8669796763802716786)
XLA Ops:
  0.0 2.2 %pack_move.1 = (bf16[16,224,128]{2,1,0:T(8,128)(2,1)S(1)}, s32[8,128]{1,0:T(8,128)S(1)}, bf16[64,16384]{1,0:T(8,128)(2,1)S(1)}, s32[128,128]{1,0:T(8,128)S(1)}) custom-call(s32[128,128]{1,0:T(8,128)} %bitcast.4, bf16[64,16384]{1,0:T(8,128)(2,1)} %frames_hbm.1), custom_call_target="tpu_custom_call" | custom-call | tf_op jit(solution)/shard_map/pack_move/pallas_call | solution.py:158
  2.2 0.7 %collective-permute-start.1 = (bf16[16,224,128]{2,1,0:T(8,128)(2,1)S(1)}, bf16[16,224,128]{2,1,0:T(8,128)(2,1)S(1)}, u32[]{:S(2)}, u32[]{:S(2)}) collective-permute-start(bf16[16,224,128]{2,1,0:T(8,128)(2,1)S(1)} %get-tuple-element.58), channel_id=1, source_target_pairs={{0,1},{1,0},{2,3},{3,2},{4,5},{5,4},{6,7},{7,6},{8,9},{9,8},{10,11... | collective-permute-start | bytes 2752520 | tf_op jit(solution)/shard_map/ppermute | solution.py:457
  2.9 1.8 %pack_own.1.own_ref = bf16[16,288,128]{2,1,0:T(8,128)(2,1)S(1)} custom-call(s32[8,128]{1,0:T(8,128)S(1)} %get-tuple-element.59.meta_s.meta_ref, s32[128,128]{1,0:T(8,128)S(1)} %get-tuple-element.56.cm_ref, bf16[64,16384]{1,0:T(8,128)(2,1)S(1)} %get-tuple-element.57.frames_ref), custom_call_target="tpu_custom_call" | custom-call | bytes 4194304 | tf_op jit(solution)/shard_map/pack_own/pallas_call | solution.py:210
  4.7 0.3 collective-permute-done.1.theirs_ref
  5.0 1.3 %share.1 = bf16[16,288,128]{2,1,0:T(8,128)(2,1)} custom-call(s32[8,128]{1,0:T(8,128)S(1)} %get-tuple-element.59.meta_s.meta_ref, bf16[16,288,128]{2,1,0:T(8,128)(2,1)S(1)} %pack_own.1.own_ref, bf16[16,224,128]{2,1,0:T(8,128)(2,1)S(1)} %collective-permute-done.1.theirs_ref), custom_call_target="tpu_custom_call" | custom-call | bytes 4194304 | tf_op jit(solution)/shard_map/share/pallas_call | solution.py:232
  6.3 6.5 %all-to-all-start.1 = ((bf16[16,288,128]{2,1,0:T(8,128)(2,1)}), bf16[16,288,128]{2,1,0:T(8,128)(2,1)S(1)}, u32[]{:S(2)}, u32[]{:S(2)}) async-start(bf16[16,288,128]{2,1,0:T(8,128)(2,1)} %share.1), calls=%async_computation.1 | async-start | bytes 2359296 | tf_op jit(solution)/shard_map/all_to_all | solution.py:460
  12.8 0.9 %collective-permute-start.2 = (s32[8,128]{1,0:T(8,128)S(1)}, s32[8,128]{1,0:T(8,128)S(1)}, u32[]{:S(2)}, u32[]{:S(2)}) collective-permute-start(s32[8,128]{1,0:T(8,128)S(1)} %get-tuple-element.59.meta_s.meta_ref), channel_id=1, source_target_pairs={{0,1},{1,0},{2,3},{3,2},{4,5},{5,4},{6,7},{7,6},{8,9},{9,8},{10,11... | collective-permute-start | bytes 12296 | tf_op jit(solution)/shard_map/ppermute | solution.py:457
  13.8 0.8 %collective-permute-done.2 = s32[8,128]{1,0:T(8,128)S(1)} collective-permute-done((s32[8,128]{1,0:T(8,128)S(1)}, s32[8,128]{1,0:T(8,128)S(1)}, u32[]{:S(2)}, u32[]{:S(2)}) %collective-permute-start.2) | collective-permute-done | bytes 4128 | tf_op jit(solution)/shard_map/ppermute | solution.py:457
  14.6 0.6 %or_reduce_fusion = pred[]{:T(512)} fusion(s32[8,128]{1,0:T(8,128)S(1)} %collective-permute-done.2, s32[8,128]{1,0:T(8,128)S(1)} %get-tuple-element.59.meta_s.meta_ref), kind=kLoop, calls=%fused_computation | loop fusion | flops 255 | bytes 257 | tf_op jit(solution)/shard_map/reduce_or | solution.py:479
  15.9 26.4 %all-to-all-done.1.raw_ref = bf16[16,288,128]{2,1,0:T(8,128)(2,1)S(1)} async-done(((bf16[16,288,128]{2,1,0:T(8,128)(2,1)}), bf16[16,288,128]{2,1,0:T(8,128)(2,1)S(1)}, u32[]{:S(2)}, u32[]{:S(2)}) %all-to-all-start.1) | async-done | bytes 1179680 | tf_op jit(solution)/shard_map/all_to_all | solution.py:460
  42.3 0.6 %normalise.4.refs_0_ = bf16[1024,384]{1,0:T(8,128)(2,1)S(1)} custom-call(bf16[16,288,128]{2,1,0:T(8,128)(2,1)S(1)} %all-to-all-done.1.raw_ref, s32[1]{0:T(128)} %bitcast.2.refs_0_), custom_call_target="tpu_custom_call" | custom-call | flops 4718592 | bytes 1572864 | tf_op jit(solution)/shard_map/normalise/pallas_call | solution.py:336
  43.0 0.6 %collective-permute-start.4 = (bf16[1024,384]{1,0:T(8,128)(2,1)S(1)}, bf16[1024,384]{1,0:T(8,128)(2,1)S(1)}, u32[]{:S(2)}, u32[]{:S(2)}) collective-permute-start(bf16[1024,384]{1,0:T(8,128)(2,1)S(1)} %normalise.4.refs_0_), channel_id=1, source_target_pairs={{0,1},{1,0},{2,3},{3,2},{4,5},{5,4},{6,7},{7,6},{8,9},{9,8},{10,11... | collective-permute-start | bytes 2359304 | tf_op jit(solution)/shard_map/ppermute | solution.py:457
  43.5 0.5 normalise.5.refs_1_
  44.0 0.1 collective-permute-start.3
  44.1 1.0 %partial_sums.4 = (f32[512,1024]{1,0:T(8,128)S(1)}, f32[8,1024]{1,0:T(8,128)S(1)}) custom-call(bf16[1024,384]{1,0:T(8,128)(2,1)S(1)} %normalise.4.refs_0_, bf16[1024,256]{1,0:T(8,128)(2,1)S(1)} %normalise.5.refs_1_), custom_call_target="tpu_custom_call" | custom-call | flops 805306368 | bytes 2097152 | tf_op jit(solution)/shard_map/partial_sums/pallas_call | solution.py:388
  45.1 0.3 collective-permute-done.4.refs_0_
  45.4 0.8 %partial_sums.5 = (f32[512,1024]{1,0:T(8,128)S(1)}, f32[8,1024]{1,0:T(8,128)S(1)}) custom-call(bf16[1024,384]{1,0:T(8,128)(2,1)S(1)} %collective-permute-done.4.refs_0_, f32[512,1024]{1,0:T(8,128)S(1)} %get-tuple-element.60.refs_1_, f32[8,1024]{1,0:T(8,128)S(1)} %get-tuple-element.61.refs_2_), custom_call_target="tpu_custom_call" | custom-call | flops 402653184 | bytes 2097152 | tf_op jit(solution)/shard_map/partial_sums/pallas_call | solution.py:388
  46.2 0.0 collective-permute-done.3
  46.2 1.8 %conditional.1 = (bf16[1,512,1024]{2,1,0:T(8,128)(2,1)}) conditional(s32[]{:T(128)} %convert_element_type.4, (s32[8,128]{1,0:T(8,128)S(1)}, s32[8,128]{1,0:T(8,128)S(1)}, bf16[1024,256]{1,0:T(8,128)(2,1)S(1)}, f32[512,1024]{1,0:T(8,128)S(1)}, f32[8,1024]{1,0:T(8,128)S(1)}) %tuple.13, (s32[8,128]{1,0:T(8,128)S(1)}, s32[8,128]{1,0:T(8,128)S(1)}, ...), branch_computations={%region_1.0_spmd, %region_2.0_spmd} | conditional | flops 2428502016 | bytes 22020144 | solution.py:499
  46.2 1.8 %correlate.2 = bf16[1,512,1024]{2,1,0:T(8,128)(2,1)} custom-call(s32[8,128]{1,0:T(8,128)S(1)} %get-tuple-element.32.meta_ref, s32[8,128]{1,0:T(8,128)S(1)} %get-tuple-element.33.their_meta_ref, bf16[1024,256]{1,0:T(8,128)(2,1)S(1)} %get-tuple-element.34.normed_ref, f32[512,1024]{1,0:T(8,128)S(1)} %get-tuple-element.35.gram_in, ...), custom_call_target="tpu_custom_call" | custom-call | flops 268435456 | bytes 3145728 | tf_op jit(solution)/shard_map/cond/branch_0_fun/correlate/pallas_call | solution.py:430
Async XLA Ops:
  2.2 2.8 %collective-permute-start.1 = (bf16[16,224,128]{2,1,0:T(8,128)(2,1)S(1)}, bf16[16,224,128]{2,1,0:T(8,128)(2,1)S(1)}, u32[]{:S(2)}, u32[]{:S(2)}) collective-permute-start(bf16[16,224,128]{2,1,0:T(8,128)(2,1)S(1)} %get-tuple-element.58), channel_id=1, source_target_pairs={{0,1},{1,0},{2,3},{3,2},{4,5},{5,4},{6,7},{7,6},{8,9},{9,8},{10,11... | collective-permute-start | bytes 2752520 | tf_op jit(solution)/shard_map/ppermute | solution.py:457
  6.3 36.0 %all-to-all-start.1 = ((bf16[16,288,128]{2,1,0:T(8,128)(2,1)}), bf16[16,288,128]{2,1,0:T(8,128)(2,1)S(1)}, u32[]{:S(2)}, u32[]{:S(2)}) async-start(bf16[16,288,128]{2,1,0:T(8,128)(2,1)} %share.1), calls=%async_computation.1 | async-start | bytes 2359296 | tf_op jit(solution)/shard_map/all_to_all | solution.py:460
  12.8 1.8 %collective-permute-start.2 = (s32[8,128]{1,0:T(8,128)S(1)}, s32[8,128]{1,0:T(8,128)S(1)}, u32[]{:S(2)}, u32[]{:S(2)}) collective-permute-start(s32[8,128]{1,0:T(8,128)S(1)} %get-tuple-element.59.meta_s.meta_ref), channel_id=1, source_target_pairs={{0,1},{1,0},{2,3},{3,2},{4,5},{5,4},{6,7},{7,6},{8,9},{9,8},{10,11... | collective-permute-start | bytes 12296 | tf_op jit(solution)/shard_map/ppermute | solution.py:457
  43.0 2.5 %collective-permute-start.4 = (bf16[1024,384]{1,0:T(8,128)(2,1)S(1)}, bf16[1024,384]{1,0:T(8,128)(2,1)S(1)}, u32[]{:S(2)}, u32[]{:S(2)}) collective-permute-start(bf16[1024,384]{1,0:T(8,128)(2,1)S(1)} %normalise.4.refs_0_), channel_id=1, source_target_pairs={{0,1},{1,0},{2,3},{3,2},{4,5},{5,4},{6,7},{7,6},{8,9},{9,8},{10,11... | collective-permute-start | bytes 2359304 | tf_op jit(solution)/shard_map/ppermute | solution.py:457
  44.0 2.2 %collective-permute-start.3 = (bf16[1024,256]{1,0:T(8,128)(2,1)S(1)}, bf16[1024,256]{1,0:T(8,128)(2,1)S(1)}, u32[]{:S(2)}, u32[]{:S(2)}) collective-permute-start(bf16[1024,256]{1,0:T(8,128)(2,1)S(1)} %normalise.5.refs_1_), channel_id=1, source_target_pairs={{0,1},{1,0},{2,3},{3,2},{4,5},{5,4},{6,7},{7,6},{8,9},{9,8},{10,11... | collective-permute-start | bytes 1572872 | tf_op jit(solution)/shard_map/ppermute | solution.py:457

commit v13 on v12

--- a/solution.py
+++ b/solution.py
@@ -40,7 +40,7 @@
 
 def list_group(n):
     half, side = n // 2, n // 4
-    first = sorted(range(half), key=lambda i: (i % side >= side - side // 4, i))
+    first = sorted(range(half), key=lambda i: (i > 1 and i % 2, i))
     return first + sorted(range(half, n), key=lambda i: (i % side >= side // 2, i))
 
 

time: 48.2 us -> 47.6 us (0.988)
  the two profiles are of different devices: /device:TPU:19 before, /device:TPU:11 now
where the time goes in v13:
time: 47.6 us; the launch traced here: 47.4 us
  waiting for transfers between devices  25.9 us (54%)
  starting transfers between devices  10.2 us (21%)
  Pallas kernels  9.93 us (21%)
  between operations  0.71 us (1%)
  other arithmetic  0.64 us (1%)
    all_to_all x1, waiting for transfers between devices, send(): lax.all_to_all(blocks, 'frame', split_axis=0, concat_axis=0, axis_index_g...  24.5 us
    all_to_all x1, starting transfers between devices, send(): lax.all_to_all(blocks, 'frame', split_axis=0, concat_axis=0, axis_index_g...  6.64 us
    ppermute x4, starting transfers between devices, swap(): return lax.ppermute(x, 'pix', SWAP)  3.52 us
    pallas_call x1, Pallas kernels, pack_move(): call(functools.partial(move_kernel, cap_blocks), 'pack_move', [jax.ShapeD...  2.16 us
    pallas_call x2, Pallas kernels, partial_sums(): call(functools.partial(partial_kernel, len(normed)), 'partial_sums', sums...  1.81 us
    pallas_call x1, Pallas kernels, pack_own(): call(functools.partial(own_kernel, cap_blocks), 'pack_own', jax.ShapeDtyp...  1.8 us
    pallas_call x1, Pallas kernels, correlate(): call(result_kernel, 'correlate', pltpu.HBM((1, rows, total), jnp.bfloat16...  1.74 us
    ppermute x4, waiting for transfers between devices, swap(): return lax.ppermute(x, 'pix', SWAP)  1.42 us
  transfers between devices with their start and end apart: 5, of which 4 were waited for; matrix products, arithmetic and copies ran while one was open for 1% of the time, Pallas kernels for 9%

profile of v13, /device:TPU:11, one launch (start us, length us, event | category | flops | bytes accessed | tf_op | source)
XLA Modules:
  0.0 47.4 jit_solution(14799379217082005800)
XLA Ops:
  0.0 2.2 %pack_move.1 = (bf16[16,224,128]{2,1,0:T(8,128)(2,1)S(1)}, s32[8,128]{1,0:T(8,128)S(1)}, bf16[64,16384]{1,0:T(8,128)(2,1)S(1)}, s32[128,128]{1,0:T(8,128)S(1)}) custom-call(s32[128,128]{1,0:T(8,128)} %bitcast.4, bf16[64,16384]{1,0:T(8,128)(2,1)} %frames_hbm.1), custom_call_target="tpu_custom_call" | custom-call | tf_op jit(solution)/shard_map/pack_move/pallas_call | solution.py:158
  2.2 0.7 %collective-permute-start.1 = (bf16[16,224,128]{2,1,0:T(8,128)(2,1)S(1)}, bf16[16,224,128]{2,1,0:T(8,128)(2,1)S(1)}, u32[]{:S(2)}, u32[]{:S(2)}) collective-permute-start(bf16[16,224,128]{2,1,0:T(8,128)(2,1)S(1)} %get-tuple-element.58), channel_id=1, source_target_pairs={{0,1},{1,0},{2,3},{3,2},{4,5},{5,4},{6,7},{7,6},{8,9},{9,8},{10,11... | collective-permute-start | bytes 2752520 | tf_op jit(solution)/shard_map/ppermute | solution.py:457
  2.9 1.8 %pack_own.1.own_ref = bf16[16,288,128]{2,1,0:T(8,128)(2,1)S(1)} custom-call(s32[8,128]{1,0:T(8,128)S(1)} %get-tuple-element.59.meta_s.meta_ref, s32[128,128]{1,0:T(8,128)S(1)} %get-tuple-element.56.cm_ref, bf16[64,16384]{1,0:T(8,128)(2,1)S(1)} %get-tuple-element.57.frames_ref), custom_call_target="tpu_custom_call" | custom-call | bytes 4194304 | tf_op jit(solution)/shard_map/pack_own/pallas_call | solution.py:210
  4.7 0.3 collective-permute-done.1.theirs_ref
  5.0 1.3 %share.1 = bf16[16,288,128]{2,1,0:T(8,128)(2,1)} custom-call(s32[8,128]{1,0:T(8,128)S(1)} %get-tuple-element.59.meta_s.meta_ref, bf16[16,288,128]{2,1,0:T(8,128)(2,1)S(1)} %pack_own.1.own_ref, bf16[16,224,128]{2,1,0:T(8,128)(2,1)S(1)} %collective-permute-done.1.theirs_ref), custom_call_target="tpu_custom_call" | custom-call | bytes 4194304 | tf_op jit(solution)/shard_map/share/pallas_call | solution.py:232
  6.3 6.6 %all-to-all-start.1 = ((bf16[16,288,128]{2,1,0:T(8,128)(2,1)}), bf16[16,288,128]{2,1,0:T(8,128)(2,1)S(1)}, u32[]{:S(2)}, u32[]{:S(2)}) async-start(bf16[16,288,128]{2,1,0:T(8,128)(2,1)} %share.1), calls=%async_computation.1 | async-start | bytes 2359296 | tf_op jit(solution)/shard_map/all_to_all | solution.py:460
  13.0 0.9 %collective-permute-start.2 = (s32[8,128]{1,0:T(8,128)S(1)}, s32[8,128]{1,0:T(8,128)S(1)}, u32[]{:S(2)}, u32[]{:S(2)}) collective-permute-start(s32[8,128]{1,0:T(8,128)S(1)} %get-tuple-element.59.meta_s.meta_ref), channel_id=1, source_target_pairs={{0,1},{1,0},{2,3},{3,2},{4,5},{5,4},{6,7},{7,6},{8,9},{9,8},{10,11... | collective-permute-start | bytes 12296 | tf_op jit(solution)/shard_map/ppermute | solution.py:457
  13.9 0.8 %collective-permute-done.2 = s32[8,128]{1,0:T(8,128)S(1)} collective-permute-done((s32[8,128]{1,0:T(8,128)S(1)}, s32[8,128]{1,0:T(8,128)S(1)}, u32[]{:S(2)}, u32[]{:S(2)}) %collective-permute-start.2) | collective-permute-done | bytes 4128 | tf_op jit(solution)/shard_map/ppermute | solution.py:457
  14.7 0.6 %or_reduce_fusion = pred[]{:T(512)} fusion(s32[8,128]{1,0:T(8,128)S(1)} %collective-permute-done.2, s32[8,128]{1,0:T(8,128)S(1)} %get-tuple-element.59.meta_s.meta_ref), kind=kLoop, calls=%fused_computation | loop fusion | flops 255 | bytes 257 | tf_op jit(solution)/shard_map/reduce_or | solution.py:479
  16.0 24.5 %all-to-all-done.1.raw_ref = bf16[16,288,128]{2,1,0:T(8,128)(2,1)S(1)} async-done(((bf16[16,288,128]{2,1,0:T(8,128)(2,1)}), bf16[16,288,128]{2,1,0:T(8,128)(2,1)S(1)}, u32[]{:S(2)}, u32[]{:S(2)}) %all-to-all-start.1) | async-done | bytes 1179680 | tf_op jit(solution)/shard_map/all_to_all | solution.py:460
  40.5 0.6 %normalise.4.refs_0_ = bf16[1024,384]{1,0:T(8,128)(2,1)S(1)} custom-call(bf16[16,288,128]{2,1,0:T(8,128)(2,1)S(1)} %all-to-all-done.1.raw_ref, s32[1]{0:T(128)} %bitcast.2.refs_0_), custom_call_target="tpu_custom_call" | custom-call | flops 4718592 | bytes 1572864 | tf_op jit(solution)/shard_map/normalise/pallas_call | solution.py:336
  41.1 1.8 %collective-permute-start.4 = (bf16[1024,384]{1,0:T(8,128)(2,1)S(1)}, bf16[1024,384]{1,0:T(8,128)(2,1)S(1)}, u32[]{:S(2)}, u32[]{:S(2)}) collective-permute-start(bf16[1024,384]{1,0:T(8,128)(2,1)S(1)} %normalise.4.refs_0_), channel_id=1, source_target_pairs={{0,1},{1,0},{2,3},{3,2},{4,5},{5,4},{6,7},{7,6},{8,9},{9,8},{10,11... | collective-permute-start | bytes 2359304 | tf_op jit(solution)/shard_map/ppermute | solution.py:457
  42.9 0.5 %normalise.5.refs_1_ = bf16[1024,256]{1,0:T(8,128)(2,1)S(1)} custom-call(bf16[16,288,128]{2,1,0:T(8,128)(2,1)S(1)} %all-to-all-done.1.raw_ref, bf16[1024,384]{1,0:T(8,128)(2,1)S(1)} %normalise.4.refs_0_), custom_call_target="tpu_custom_call" | custom-call | flops 3145728 | bytes 1048576 | tf_op jit(solution)/shard_map/normalise/pallas_call | solution.py:336
  43.4 0.1 collective-permute-start.3
  43.5 1.0 %partial_sums.4 = (f32[512,1024]{1,0:T(8,128)S(1)}, f32[8,1024]{1,0:T(8,128)S(1)}) custom-call(bf16[1024,384]{1,0:T(8,128)(2,1)S(1)} %normalise.4.refs_0_, bf16[1024,256]{1,0:T(8,128)(2,1)S(1)} %normalise.5.refs_1_), custom_call_target="tpu_custom_call" | custom-call | flops 805306368 | bytes 2097152 | tf_op jit(solution)/shard_map/partial_sums/pallas_call | solution.py:388
  44.5 0.3 collective-permute-done.4.refs_0_
  44.8 0.8 %partial_sums.5 = (f32[512,1024]{1,0:T(8,128)S(1)}, f32[8,1024]{1,0:T(8,128)S(1)}) custom-call(bf16[1024,384]{1,0:T(8,128)(2,1)S(1)} %collective-permute-done.4.refs_0_, f32[512,1024]{1,0:T(8,128)S(1)} %get-tuple-element.60.refs_1_, f32[8,1024]{1,0:T(8,128)S(1)} %get-tuple-element.61.refs_2_), custom_call_target="tpu_custom_call" | custom-call | flops 402653184 | bytes 2097152 | tf_op jit(solution)/shard_map/partial_sums/pallas_call | solution.py:388
  45.6 0.0 collective-permute-done.3
  45.6 1.8 %conditional.1 = (bf16[1,512,1024]{2,1,0:T(8,128)(2,1)}) conditional(s32[]{:T(128)} %convert_element_type.4, (s32[8,128]{1,0:T(8,128)S(1)}, s32[8,128]{1,0:T(8,128)S(1)}, bf16[1024,256]{1,0:T(8,128)(2,1)S(1)}, f32[512,1024]{1,0:T(8,128)S(1)}, f32[8,1024]{1,0:T(8,128)S(1)}) %tuple.13, (s32[8,128]{1,0:T(8,128)S(1)}, s32[8,128]{1,0:T(8,128)S(1)}, ...), branch_computations={%region_1.0_spmd, %region_2.0_spmd} | conditional | flops 2428502016 | bytes 22020144 | solution.py:499
  45.6 1.7 %correlate.2 = bf16[1,512,1024]{2,1,0:T(8,128)(2,1)} custom-call(s32[8,128]{1,0:T(8,128)S(1)} %get-tuple-element.32.meta_ref, s32[8,128]{1,0:T(8,128)S(1)} %get-tuple-element.33.their_meta_ref, bf16[1024,256]{1,0:T(8,128)(2,1)S(1)} %get-tuple-element.34.normed_ref, f32[512,1024]{1,0:T(8,128)S(1)} %get-tuple-element.35.gram_in, ...), custom_call_target="tpu_custom_call" | custom-call | flops 268435456 | bytes 3145728 | tf_op jit(solution)/shard_map/cond/branch_0_fun/correlate/pallas_call | solution.py:430
Async XLA Ops:
  2.2 2.8 %collective-permute-start.1 = (bf16[16,224,128]{2,1,0:T(8,128)(2,1)S(1)}, bf16[16,224,128]{2,1,0:T(8,128)(2,1)S(1)}, u32[]{:S(2)}, u32[]{:S(2)}) collective-permute-start(bf16[16,224,128]{2,1,0:T(8,128)(2,1)S(1)} %get-tuple-element.58), channel_id=1, source_target_pairs={{0,1},{1,0},{2,3},{3,2},{4,5},{5,4},{6,7},{7,6},{8,9},{9,8},{10,11... | collective-permute-start | bytes 2752520 | tf_op jit(solution)/shard_map/ppermute | solution.py:457
  6.3 34.2 %all-to-all-start.1 = ((bf16[16,288,128]{2,1,0:T(8,128)(2,1)}), bf16[16,288,128]{2,1,0:T(8,128)(2,1)S(1)}, u32[]{:S(2)}, u32[]{:S(2)}) async-start(bf16[16,288,128]{2,1,0:T(8,128)(2,1)} %share.1), calls=%async_computation.1 | async-start | bytes 2359296 | tf_op jit(solution)/shard_map/all_to_all | solution.py:460
  13.0 1.8 %collective-permute-start.2 = (s32[8,128]{1,0:T(8,128)S(1)}, s32[8,128]{1,0:T(8,128)S(1)}, u32[]{:S(2)}, u32[]{:S(2)}) collective-permute-start(s32[8,128]{1,0:T(8,128)S(1)} %get-tuple-element.59.meta_s.meta_ref), channel_id=1, source_target_pairs={{0,1},{1,0},{2,3},{3,2},{4,5},{5,4},{6,7},{7,6},{8,9},{9,8},{10,11... | collective-permute-start | bytes 12296 | tf_op jit(solution)/shard_map/ppermute | solution.py:457
  41.1 3.7 %collective-permute-start.4 = (bf16[1024,384]{1,0:T(8,128)(2,1)S(1)}, bf16[1024,384]{1,0:T(8,128)(2,1)S(1)}, u32[]{:S(2)}, u32[]{:S(2)}) collective-permute-start(bf16[1024,384]{1,0:T(8,128)(2,1)S(1)} %normalise.4.refs_0_), channel_id=1, source_target_pairs={{0,1},{1,0},{2,3},{3,2},{4,5},{5,4},{6,7},{7,6},{8,9},{9,8},{10,11... | collective-permute-start | bytes 2359304 | tf_op jit(solution)/shard_map/ppermute | solution.py:457
  43.4 2.2 %collective-permute-start.3 = (bf16[1024,256]{1,0:T(8,128)(2,1)S(1)}, bf16[1024,256]{1,0:T(8,128)(2,1)S(1)}, u32[]{:S(2)}, u32[]{:S(2)}) collective-permute-start(bf16[1024,256]{1,0:T(8,128)(2,1)S(1)} %normalise.5.refs_1_), channel_id=1, source_target_pairs={{0,1},{1,0},{2,3},{3,2},{4,5},{5,4},{6,7},{7,6},{8,9},{9,8},{10,11... | collective-permute-start | bytes 1572872 | tf_op jit(solution)/shard_map/ppermute | solution.py:457
